TPU v7x, 32 devices: a whole 2x2x4 slice. The times are simulated.
32 devices in a mesh: groups: 2 (over x), dp: 16 (over z, y, core).
Axes of the slice: x: 2, y: 2, z: 4, core: 2. Of those that a mesh axis runs over, the one named last changes fastest.
Arguments:
- image_embeds: bfloat16 [8192, 1280], P(('groups', 'dp')), parts along dimension 0, may hold values from -0.25 to 0.25
- text_embeds: bfloat16 [8192, 1280], P(('groups', 'dp')), parts along dimension 0, may hold values from -0.25 to 0.25
- labels: int32 [8192], P(('groups', 'dp')), parts along dimension 0, may hold values from 0 to 4095, as said below
Outputs:
- grad_images: float32 [8192, 1280], P(('groups', 'dp')), parts along dimension 0
- grad_texts: float32 [8192, 1280], P(('groups', 'dp')), parts along dimension 0
There are 2 independent parts, one for each index of `groups`. A program takes and returns all parts, laid end to end along the dimension named above; each array names one. Nothing has to cross between parts.
Inputs may be any that keep to these rules, and one draw needn't show every extreme that they name: `labels`: each image row's matching text row lies in the same block of 256 rows, and each text row is the match of exactly one image row.
All inputs are finite; a program needn't handle non-finite values.
Results may differ from a plain program's by a relative error of at most 0.0025.
Values may be sent and summed in bfloat16 or wider, within the bound.
No kernel may reach another device: no remote copies, remote signals or barrier semaphores. Data moves between devices by JAX's collectives and lax.ppermute only.
A program may use at most 64 MiB of HBM per device.

v0:
```python
import jax
import jax.numpy as jnp
from jax import lax
from jax.sharding import PartitionSpec as P

WINDOW = 8


logit_scale = 100.0
half_scale = 50.0


def passed_along(block, axis, distance):
    devices = range(lax.axis_size(axis))
    route = [((i - distance) % len(devices), i) for i in devices]
    return lax.ppermute(block, axis, route)


def similarity(row_side, col_side):
    products = lax.dot_general(
        row_side, col_side, (((1,), (1,)), ((), ())), preferred_element_type=jnp.float32
    )
    return logit_scale * products


def running(old_peak, old_total, scores, reduce_dim):
    new_peak = jnp.maximum(old_peak, jnp.max(scores, axis=reduce_dim))
    shifted = jnp.exp(scores - jnp.expand_dims(new_peak, reduce_dim))
    new_total = old_total * jnp.exp(old_peak - new_peak) + jnp.sum(shifted, axis=reduce_dim)
    return (new_peak, new_total)


def weights(scores, row_norm, col_norm, positive):
    combined = (
        jnp.exp(scores - row_norm[:, None])
        + jnp.exp(scores - col_norm[None, :])
        - 2.0 * positive.astype(jnp.float32)
    )
    return combined.astype(jnp.bfloat16)


def forward(block):
    return passed_along(block, "dp", -1)


def backward(block):
    return passed_along(block, "dp", 1)


def shards(image_embeds, text_embeds, labels):
    row_count = image_embeds.shape[0]
    count = lax.axis_size("dp")
    here = lax.axis_index("dp")
    offset = here * row_count
    positions = offset + jnp.arange(row_count, dtype=jnp.int32)
    lowest = jnp.full((row_count,), -jnp.inf, jnp.float32)
    nothing = jnp.zeros((row_count,), jnp.float32)
    diagonal = similarity(image_embeds, text_embeds)
    row_peak, row_total = running(lowest, nothing, diagonal, 1)
    col_peak, col_total = running(lowest, nothing, diagonal, 0)
    kept_text = []
    kept_image = []
    moving_text, moving_image = (text_embeds, image_embeds)
    for step in range(1, WINDOW):
        moving_text = forward(moving_text)
        moving_image = backward(moving_image)
        kept_text.append(moving_text)
        kept_image.append(moving_image)
        row_peak, row_total = running(row_peak, row_total, similarity(image_embeds, moving_text), 1)
        col_peak, col_total = running(col_peak, col_total, similarity(moving_image, text_embeds), 0)
    col_norm = col_peak + jnp.log(col_total)
    row_norm = row_peak + jnp.log(row_total)
    every_row, every_col = (
        lax.all_gather(row_norm, "dp", axis=0, tiled=True),
        lax.all_gather(col_norm, "dp", axis=0, tiled=True),
    )
    mixing = weights(diagonal, row_norm, col_norm, labels[:, None] == positions[None, :])
    image_sum = jnp.dot(mixing, text_embeds, preferred_element_type=jnp.float32)
    text_sum = lax.dot_general(
        mixing, image_embeds, (((0,), (0,)), ((), ())), preferred_element_type=jnp.float32
    )
    no_match = jnp.zeros((row_count, row_count), jnp.bool_)
    moving_text, moving_image = (text_embeds, image_embeds)
    for step in range(1, WINDOW):
        moving_text = forward(moving_text)
        moving_image = backward(moving_image)
        text_block = (here + step) % count
        image_block = (here - step + count) % count
        far_cols = lax.dynamic_slice_in_dim(every_col, text_block * row_count, row_count, 0)
        image_mixing = weights(similarity(image_embeds, moving_text), row_norm, far_cols, no_match)
        image_sum = image_sum + jnp.dot(
            image_mixing, moving_text, preferred_element_type=jnp.float32
        )
        far_rows = lax.dynamic_slice_in_dim(every_row, image_block * row_count, row_count, 0)
        text_mixing = weights(similarity(moving_image, text_embeds), far_rows, col_norm, no_match)
        text_sum = text_sum + lax.dot_general(
            text_mixing, moving_image, (((0,), (0,)), ((), ())), preferred_element_type=jnp.float32
        )
    return (half_scale * image_sum, half_scale * text_sum)


def solution(mesh):
    return jax.shard_map(
        shards,
        mesh=mesh,
        in_specs=(P(("groups", "dp"), None), P(("groups", "dp"), None), P(("groups", "dp"))),
        out_specs=(P(("groups", "dp"), None), P(("groups", "dp"), None)),
        check_vma=False,
    )
```

profile of v0, /device:TPU:0, one launch (start us, length us, event | category | flops | bytes accessed | tf_op | source)
XLA Modules:
  0.0 168.3 jit_solution(12531281767052669187)
XLA Ops:
  0.6 0.5 collective-permute-start.7
  1.1 5.1 %collective-permute-start = (bf16[256,1280]{1,0:T(8,128)(2,1)}, bf16[256,1280]{1,0:T(8,128)(2,1)S(1)}, u32[]{:S(2)}, u32[]{:S(2)}) collective-permute-start(bf16[256,1280]{1,0:T(8,128)(2,1)} %param.4), channel_id=1, source_target_pairs={{1,0},{2,1},{3,2},{4,3},{5,4},{6,5},{7,6},{8,7},{9,8},{10,9},{11,1... | collective-permute-start | bytes 1966088 | tf_op jit(solution)/shard_map/ppermute | solution.py:16
  6.2 8.5 %collective-permute-done.7 = bf16[256,1280]{1,0:T(8,128)(2,1)S(1)} collective-permute-done((bf16[256,1280]{1,0:T(8,128)(2,1)}, bf16[256,1280]{1,0:T(8,128)(2,1)S(1)}, u32[]{:S(2)}, u32[]{:S(2)}) %collective-permute-start.7) | collective-permute-done | bytes 655392 | tf_op jit(solution)/shard_map/ppermute | solution.py:16
  14.7 3.9 %collective-permute-start.8 = (bf16[256,1280]{1,0:T(8,128)(2,1)S(1)}, bf16[256,1280]{1,0:T(8,128)(2,1)S(1)}, u32[]{:S(2)}, u32[]{:S(2)}) collective-permute-start(bf16[256,1280]{1,0:T(8,128)(2,1)S(1)} %collective-permute-done.7), channel_id=1, source_target_pairs={{15,0},{0,1},{1,2},{2,3},{3,4},{4,5},{5,6},{6,7},{7,8},{8,9},{9,10... | collective-permute-start | bytes 1966088 | tf_op jit(solution)/shard_map/ppermute | solution.py:16
  18.6 0.6 collective-permute-start.1
  19.2 8.3 %collective-permute-done.8 = bf16[256,1280]{1,0:T(8,128)(2,1)S(1)} collective-permute-done((bf16[256,1280]{1,0:T(8,128)(2,1)S(1)}, bf16[256,1280]{1,0:T(8,128)(2,1)S(1)}, u32[]{:S(2)}, u32[]{:S(2)}) %collective-permute-start.8) | collective-permute-done | bytes 655392 | tf_op jit(solution)/shard_map/ppermute | solution.py:16
  27.5 7.4 %collective-permute-start.9 = (bf16[256,1280]{1,0:T(8,128)(2,1)S(1)}, bf16[256,1280]{1,0:T(8,128)(2,1)}, u32[]{:S(2)}, u32[]{:S(2)}) collective-permute-start(bf16[256,1280]{1,0:T(8,128)(2,1)S(1)} %collective-permute-done.8), channel_id=1, source_target_pairs={{15,0},{0,1},{1,2},{2,3},{3,4},{4,5},{5,6},{6,7},{7,8},{8,9},{9,10... | collective-permute-start | bytes 1966088 | tf_op jit(solution)/shard_map/ppermute | solution.py:16
  34.9 1.7 %fusion.32 = (f32[256]{0:T(256)S(1)}, f32[256]{0:T(256)S(1)}, f32[256,256]{1,0:T(8,128)S(1)}) fusion(bf16[256,1280]{1,0:T(8,128)(2,1)} %param.3, bf16[256,1280]{1,0:T(8,128)(2,1)} %param.4), kind=kOutput, calls=%fused_computation.95 | convolution fusion | flops 167968256 | bytes 1574912 | tf_op jit(solution)/shard_map/dot_general | solution.py:20
  36.9 3.6 %collective-permute-done.9 = bf16[256,1280]{1,0:T(8,128)(2,1)} collective-permute-done((bf16[256,1280]{1,0:T(8,128)(2,1)S(1)}, bf16[256,1280]{1,0:T(8,128)(2,1)}, u32[]{:S(2)}, u32[]{:S(2)}) %collective-permute-start.9) | collective-permute-done | bytes 655392 | tf_op jit(solution)/shard_map/ppermute | solution.py:16
  40.5 10.7 %collective-permute-start.10 = (bf16[256,1280]{1,0:T(8,128)(2,1)}, bf16[256,1280]{1,0:T(8,128)(2,1)S(1)}, u32[]{:S(2)}, u32[]{:S(2)}) collective-permute-start(bf16[256,1280]{1,0:T(8,128)(2,1)} %collective-permute-done.9), channel_id=1, source_target_pairs={{15,0},{0,1},{1,2},{2,3},{3,4},{4,5},{5,6},{6,7},{7,8},{8,9},{9,10... | collective-permute-start | bytes 1966088 | tf_op jit(solution)/shard_map/ppermute | solution.py:16
  51.6 0.4 fusion.50
  52.5 3.1 %collective-permute-done.10 = bf16[256,1280]{1,0:T(8,128)(2,1)S(1)} collective-permute-done((bf16[256,1280]{1,0:T(8,128)(2,1)}, bf16[256,1280]{1,0:T(8,128)(2,1)S(1)}, u32[]{:S(2)}, u32[]{:S(2)}) %collective-permute-start.10) | collective-permute-done | bytes 655392 | tf_op jit(solution)/shard_map/ppermute | solution.py:16
  55.6 12.4 %collective-permute-start.11 = (bf16[256,1280]{1,0:T(8,128)(2,1)S(1)}, bf16[256,1280]{1,0:T(8,128)(2,1)S(1)}, u32[]{:S(2)}, u32[]{:S(2)}) collective-permute-start(bf16[256,1280]{1,0:T(8,128)(2,1)S(1)} %collective-permute-done.10), channel_id=1, source_target_pairs={{15,0},{0,1},{1,2},{2,3},{3,4},{4,5},{5,6},{6,7},{7,8},{8,9},{9,10... | collective-permute-start | bytes 1966088 | tf_op jit(solution)/shard_map/ppermute | solution.py:16
  68.5 1.5 fusion.41
  70.4 0.9 collective-permute-done.11
  71.3 12.7 %collective-permute-start.12 = (bf16[256,1280]{1,0:T(8,128)(2,1)S(1)}, bf16[256,1280]{1,0:T(8,128)(2,1)S(1)}, u32[]{:S(2)}, u32[]{:S(2)}) collective-permute-start(bf16[256,1280]{1,0:T(8,128)(2,1)S(1)} %collective-permute-done.11), channel_id=1, source_target_pairs={{15,0},{0,1},{1,2},{2,3},{3,4},{4,5},{5,6},{6,7},{7,8},{8,9},{9,10... | collective-permute-start | bytes 1966088 | tf_op jit(solution)/shard_map/ppermute | solution.py:16
  85.3 2.9 %collective-permute-done.12 = bf16[256,1280]{1,0:T(8,128)(2,1)S(1)} collective-permute-done((bf16[256,1280]{1,0:T(8,128)(2,1)S(1)}, bf16[256,1280]{1,0:T(8,128)(2,1)S(1)}, u32[]{:S(2)}, u32[]{:S(2)}) %collective-permute-start.12) | collective-permute-done | bytes 655392 | tf_op jit(solution)/shard_map/ppermute | solution.py:16
  88.1 12.0 %collective-permute-start.13 = (bf16[256,1280]{1,0:T(8,128)(2,1)S(1)}, bf16[256,1280]{1,0:T(8,128)(2,1)S(1)}, u32[]{:S(2)}, u32[]{:S(2)}) collective-permute-start(bf16[256,1280]{1,0:T(8,128)(2,1)S(1)} %collective-permute-done.12), channel_id=1, source_target_pairs={{15,0},{0,1},{1,2},{2,3},{3,4},{4,5},{5,6},{6,7},{7,8},{8,9},{9,10... | collective-permute-start | bytes 1966088 | tf_op jit(solution)/shard_map/ppermute | solution.py:16
  100.1 0.4 fusion.46
  101.5 2.6 %collective-permute-done.13 = bf16[256,1280]{1,0:T(8,128)(2,1)S(1)} collective-permute-done((bf16[256,1280]{1,0:T(8,128)(2,1)S(1)}, bf16[256,1280]{1,0:T(8,128)(2,1)S(1)}, u32[]{:S(2)}, u32[]{:S(2)}) %collective-permute-start.13) | collective-permute-done | bytes 655392 | tf_op jit(solution)/shard_map/ppermute | solution.py:16
  104.6 7.9 %collective-permute-done.6 = bf16[256,1280]{1,0:T(8,128)(2,1)S(1)} collective-permute-done((bf16[256,1280]{1,0:T(8,128)(2,1)S(1)}, bf16[256,1280]{1,0:T(8,128)(2,1)S(1)}, u32[]{:S(2)}, u32[]{:S(2)}) %collective-permute-start.6) | collective-permute-done | bytes 655392 | tf_op jit(solution)/shard_map/ppermute | solution.py:16
  114.2 0.5 fusion.30
  115.2 26.1 %all-gather = f32[16,1,256]{2,1,0:T(1,128)S(1)} all-gather(f32[1,1,256]{2,1,0:T(1,128)S(1)} %bitcast.51), channel_id=1, replica_groups=mesh['groups'=2,'dp'=16] {'dp'}, dimensions={0}, use_global_device_ids=true | all-gather | bytes 17408 | tf_op jit(solution)/shard_map/all_gather | solution.py:75
  141.2 17.6 %all-gather.1 = f32[16,1,256]{2,1,0:T(1,128)S(1)} all-gather(f32[1,1,256]{2,1,0:T(1,128)S(1)} %bitcast.50), channel_id=1, replica_groups=mesh['groups'=2,'dp'=16] {'dp'}, dimensions={0}, use_global_device_ids=true | all-gather | bytes 17408 | tf_op jit(solution)/shard_map/all_gather | solution.py:74
  159.0 0.5 convolution_add_fusion.6
  159.5 0.5 convolution_add_fusion.5
  160.0 1.6 convolution_add_fusion.4
  161.6 0.5 convolution_add_fusion.3
  162.0 0.5 convolution_add_fusion.2
  162.5 0.5 convolution_add_fusion.1
  163.0 1.5 fusion.1
  166.9 1.5 fusion
  (51 shorter events, 9.3 us)
Async XLA Ops:
  0.6 50.5 %copy-start.1 = (bf16[256,1280]{1,0:T(8,128)(2,1)S(1)}, bf16[256,1280]{1,0:T(8,128)(2,1)}, u32[]{:S(2)}) copy-start(bf16[256,1280]{1,0:T(8,128)(2,1)} %param.4) | copy-start | bytes 1966084
  0.6 14.1 %collective-permute-start.7 = (bf16[256,1280]{1,0:T(8,128)(2,1)}, bf16[256,1280]{1,0:T(8,128)(2,1)S(1)}, u32[]{:S(2)}, u32[]{:S(2)}) collective-permute-start(bf16[256,1280]{1,0:T(8,128)(2,1)} %param.3), channel_id=1, source_target_pairs={{15,0},{0,1},{1,2},{2,3},{3,4},{4,5},{5,6},{6,7},{7,8},{8,9},{9,10... | collective-permute-start | bytes 1966088 | tf_op jit(solution)/shard_map/ppermute | solution.py:16
  1.1 17.5 %collective-permute-start = (bf16[256,1280]{1,0:T(8,128)(2,1)}, bf16[256,1280]{1,0:T(8,128)(2,1)S(1)}, u32[]{:S(2)}, u32[]{:S(2)}) collective-permute-start(bf16[256,1280]{1,0:T(8,128)(2,1)} %param.4), channel_id=1, source_target_pairs={{1,0},{2,1},{3,2},{4,3},{5,4},{6,5},{7,6},{8,7},{9,8},{10,9},{11,1... | collective-permute-start | bytes 1966088 | tf_op jit(solution)/shard_map/ppermute | solution.py:16
  14.7 12.8 %collective-permute-start.8 = (bf16[256,1280]{1,0:T(8,128)(2,1)S(1)}, bf16[256,1280]{1,0:T(8,128)(2,1)S(1)}, u32[]{:S(2)}, u32[]{:S(2)}) collective-permute-start(bf16[256,1280]{1,0:T(8,128)(2,1)S(1)} %collective-permute-done.7), channel_id=1, source_target_pairs={{15,0},{0,1},{1,2},{2,3},{3,4},{4,5},{5,6},{6,7},{7,8},{8,9},{9,10... | collective-permute-start | bytes 1966088 | tf_op jit(solution)/shard_map/ppermute | solution.py:16
  18.6 16.3 %collective-permute-start.1 = (bf16[256,1280]{1,0:T(8,128)(2,1)S(1)}, bf16[256,1280]{1,0:T(8,128)(2,1)S(1)}, u32[]{:S(2)}, u32[]{:S(2)}) collective-permute-start(bf16[256,1280]{1,0:T(8,128)(2,1)S(1)} %collective-permute-done), channel_id=1, source_target_pairs={{1,0},{2,1},{3,2},{4,3},{5,4},{6,5},{7,6},{8,7},{9,8},{10,9},{11,1... | collective-permute-start | bytes 1966088 | tf_op jit(solution)/shard_map/ppermute | solution.py:16
  27.5 12.9 %collective-permute-start.9 = (bf16[256,1280]{1,0:T(8,128)(2,1)S(1)}, bf16[256,1280]{1,0:T(8,128)(2,1)}, u32[]{:S(2)}, u32[]{:S(2)}) collective-permute-start(bf16[256,1280]{1,0:T(8,128)(2,1)S(1)} %collective-permute-done.8), channel_id=1, source_target_pairs={{15,0},{0,1},{1,2},{2,3},{3,4},{4,5},{5,6},{6,7},{7,8},{8,9},{9,10... | collective-permute-start | bytes 1966088 | tf_op jit(solution)/shard_map/ppermute | solution.py:16
  34.9 16.6 %collective-permute-start.2 = (bf16[256,1280]{1,0:T(8,128)(2,1)S(1)}, bf16[256,1280]{1,0:T(8,128)(2,1)S(1)}, u32[]{:S(2)}, u32[]{:S(2)}) collective-permute-start(bf16[256,1280]{1,0:T(8,128)(2,1)S(1)} %collective-permute-done.1), channel_id=1, source_target_pairs={{1,0},{2,1},{3,2},{4,3},{5,4},{6,5},{7,6},{8,7},{9,8},{10,9},{11,1... | collective-permute-start | bytes 1966088 | tf_op jit(solution)/shard_map/ppermute | solution.py:16
  36.7 15.0 %copy-start = (bf16[256,1280]{1,0:T(8,128)(2,1)S(1)}, bf16[256,1280]{1,0:T(8,128)(2,1)}, u32[]{:S(2)}) copy-start(bf16[256,1280]{1,0:T(8,128)(2,1)} %param.3) | copy-start | bytes 1966084
  40.5 15.1 %collective-permute-start.10 = (bf16[256,1280]{1,0:T(8,128)(2,1)}, bf16[256,1280]{1,0:T(8,128)(2,1)S(1)}, u32[]{:S(2)}, u32[]{:S(2)}) collective-permute-start(bf16[256,1280]{1,0:T(8,128)(2,1)} %collective-permute-done.9), channel_id=1, source_target_pairs={{15,0},{0,1},{1,2},{2,3},{3,4},{4,5},{5,6},{6,7},{7,8},{8,9},{9,10... | collective-permute-start | bytes 1966088 | tf_op jit(solution)/shard_map/ppermute | solution.py:16
  51.6 16.9 %collective-permute-start.3 = (bf16[256,1280]{1,0:T(8,128)(2,1)S(1)}, bf16[256,1280]{1,0:T(8,128)(2,1)S(1)}, u32[]{:S(2)}, u32[]{:S(2)}) collective-permute-start(bf16[256,1280]{1,0:T(8,128)(2,1)S(1)} %collective-permute-done.2), channel_id=1, source_target_pairs={{1,0},{2,1},{3,2},{4,3},{5,4},{6,5},{7,6},{8,7},{9,8},{10,9},{11,1... | collective-permute-start | bytes 1966088 | tf_op jit(solution)/shard_map/ppermute | solution.py:16
  55.6 15.7 %collective-permute-start.11 = (bf16[256,1280]{1,0:T(8,128)(2,1)S(1)}, bf16[256,1280]{1,0:T(8,128)(2,1)S(1)}, u32[]{:S(2)}, u32[]{:S(2)}) collective-permute-start(bf16[256,1280]{1,0:T(8,128)(2,1)S(1)} %collective-permute-done.10), channel_id=1, source_target_pairs={{15,0},{0,1},{1,2},{2,3},{3,4},{4,5},{5,6},{6,7},{7,8},{8,9},{9,10... | collective-permute-start | bytes 1966088 | tf_op jit(solution)/shard_map/ppermute | solution.py:16
  68.4 15.9 %collective-permute-start.4 = (bf16[256,1280]{1,0:T(8,128)(2,1)S(1)}, bf16[256,1280]{1,0:T(8,128)(2,1)S(1)}, u32[]{:S(2)}, u32[]{:S(2)}) collective-permute-start(bf16[256,1280]{1,0:T(8,128)(2,1)S(1)} %collective-permute-done.3), channel_id=1, source_target_pairs={{1,0},{2,1},{3,2},{4,3},{5,4},{6,5},{7,6},{8,7},{9,8},{10,9},{11,1... | collective-permute-start | bytes 1966088 | tf_op jit(solution)/shard_map/ppermute | solution.py:16
  71.3 16.8 %collective-permute-start.12 = (bf16[256,1280]{1,0:T(8,128)(2,1)S(1)}, bf16[256,1280]{1,0:T(8,128)(2,1)S(1)}, u32[]{:S(2)}, u32[]{:S(2)}) collective-permute-start(bf16[256,1280]{1,0:T(8,128)(2,1)S(1)} %collective-permute-done.11), channel_id=1, source_target_pairs={{15,0},{0,1},{1,2},{2,3},{3,4},{4,5},{5,6},{6,7},{7,8},{8,9},{9,10... | collective-permute-start | bytes 1966088 | tf_op jit(solution)/shard_map/ppermute | solution.py:16
  84.4 16.2 %collective-permute-start.5 = (bf16[256,1280]{1,0:T(8,128)(2,1)S(1)}, bf16[256,1280]{1,0:T(8,128)(2,1)S(1)}, u32[]{:S(2)}, u32[]{:S(2)}) collective-permute-start(bf16[256,1280]{1,0:T(8,128)(2,1)S(1)} %collective-permute-done.4), channel_id=1, source_target_pairs={{1,0},{2,1},{3,2},{4,3},{5,4},{6,5},{7,6},{8,7},{9,8},{10,9},{11,1... | collective-permute-start | bytes 1966088 | tf_op jit(solution)/shard_map/ppermute | solution.py:16
  88.1 16.0 %collective-permute-start.13 = (bf16[256,1280]{1,0:T(8,128)(2,1)S(1)}, bf16[256,1280]{1,0:T(8,128)(2,1)S(1)}, u32[]{:S(2)}, u32[]{:S(2)}) collective-permute-start(bf16[256,1280]{1,0:T(8,128)(2,1)S(1)} %collective-permute-done.12), channel_id=1, source_target_pairs={{15,0},{0,1},{1,2},{2,3},{3,4},{4,5},{5,6},{6,7},{7,8},{8,9},{9,10... | collective-permute-start | bytes 1966088 | tf_op jit(solution)/shard_map/ppermute | solution.py:16
  100.6 11.9 %collective-permute-start.6 = (bf16[256,1280]{1,0:T(8,128)(2,1)S(1)}, bf16[256,1280]{1,0:T(8,128)(2,1)S(1)}, u32[]{:S(2)}, u32[]{:S(2)}) collective-permute-start(bf16[256,1280]{1,0:T(8,128)(2,1)S(1)} %collective-permute-done.5), channel_id=1, source_target_pairs={{1,0},{2,1},{3,2},{4,3},{5,4},{6,5},{7,6},{8,7},{9,8},{10,9},{11,1... | collective-permute-start | bytes 1966088 | tf_op jit(solution)/shard_map/ppermute | solution.py:16
  113.2 1.1 copy-start.2
where the time goes:
time: 169 us; the launch traced here: 168 us
  starting transfers between devices  65.4 us (39%)
  blocking collectives  43.7 us (26%)
  waiting for transfers between devices  37.8 us (22%)
  matrix products  18.8 us (11%)
    ppermute x14, starting transfers between devices, passed_along(): return lax.ppermute(block, axis, route)  65.4 us
    ppermute x14, waiting for transfers between devices, passed_along(): return lax.ppermute(block, axis, route)  37.8 us
    all_gather x1, blocking collectives, shards(): lax.all_gather(col_norm, 'dp', axis=0, tiled=True)  26.1 us
    all_gather x1, blocking collectives, shards(): lax.all_gather(row_norm, 'dp', axis=0, tiled=True)  17.6 us
    dot_general x15, matrix products, similarity(): lax.dot_general(row_side, col_side, (((1,), (1,)), ((), ())), preferred_e...  8.64 us
    dot_general x7, matrix products, shards(): lax.dot_general(text_mixing, moving_image, (((0,), (0,)), ((), ())), pref...  5.45 us
    dot_general x7, matrix products, shards(): jnp.dot(image_mixing, moving_text, preferred_element_type=jnp.float32)  3.78 us
  transfers between devices with their start and end apart: 14, of which 8 were waited for; matrix products, arithmetic and copies ran while one was open for 5% of the time, Pallas kernels for 0%

commit v1 on v0

v1 whole, which is shorter than its diff:
```python
import jax
import jax.numpy as jnp
from jax import lax
from jax.sharding import PartitionSpec as P

WINDOW = 8
LEVEL = 4


logit_scale = 100.0
half_scale = 50.0


def route(count, moves):
    return [
        ((level * LEVEL + a) % count, (level * LEVEL + b) % count)
        for level in range(count // LEVEL)
        for a, b in moves
    ]


def exchange(text, image, rank):
    count = lax.axis_size("dp")

    def send(block, moves):
        return lax.ppermute(block, "dp", route(count, moves))

    low_y = rank < 2
    even = rank % 2 == 0
    cores = [(0, 1), (1, 0), (2, 3), (3, 2)]
    across = [(0, 2), (1, 3), (2, 0), (3, 1)]
    t1 = send(text, [(r + 4, r) for r in range(4)])
    own_y = send(jnp.where(low_y, image, text), across)
    own_c = send(jnp.where(even, image, text), cores)
    i1 = send(image, [(r - 4, r) for r in range(4)])
    t2 = send(t1, [(r + 4, r) for r in (0, 1, 2)])
    i2 = send(i1, [(r - 4, r) for r in (1, 2, 3)])
    own_yc = send(own_y, cores)
    t1_c = send(t1, cores)
    t1_y = send(t1, across)
    i1_c = send(i1, cores)
    i1_y = send(i1, across)
    t1_yc = send(t1_y, cores)
    i1_yc = send(i1_y, cores)
    two_c = send(jnp.where(even, t2, i2), cores)
    two_y = send(jnp.where(low_y, t2, i2), across)
    two_yc = send(two_y, cores)
    texts = [
        text, t1, t1_c, t1_y, t1_yc,
        jnp.where(even, own_c, two_c),
        jnp.where(low_y, own_y, two_y),
        jnp.where(low_y, own_yc, two_yc),
    ]
    images = [
        image, i1, i1_c, i1_y, i1_yc,
        jnp.where(even, two_c, own_c),
        jnp.where(low_y, two_y, own_y),
        jnp.where(low_y, two_yc, own_yc),
    ]
    return texts, images


TEXT_PLACES = (
    (0, 4, 5, 6, 7, 1, 2, 3),
    (1, 5, 4, 7, 6, 8, 3, 2),
    (2, 6, 7, 4, 5, 3, 8, 9),
    (3, 7, 6, 5, 4, 10, 9, 8),
)
IMAGE_PLACES = tuple(tuple(3 - place for place in row) for row in TEXT_PLACES[::-1])


def similarity(row_side, col_side):
    products = lax.dot_general(
        row_side, col_side, (((1,), (1,)), ((), ())), preferred_element_type=jnp.float32
    )
    return logit_scale * products


def log_sums(blocks, reduce_dim):
    peak = jnp.max(jnp.stack([jnp.max(b, axis=reduce_dim) for b in blocks]), axis=0)
    total = sum(
        jnp.sum(jnp.exp(b - jnp.expand_dims(peak, reduce_dim)), axis=reduce_dim) for b in blocks
    )
    return peak + jnp.log(total)


def weights(scores, row_norm, col_norm, positive=None):
    combined = jnp.exp(scores - row_norm[:, None]) + jnp.exp(scores - col_norm[None, :])
    if positive is not None:
        combined = combined - 2.0 * positive.astype(jnp.float32)
    return combined.astype(jnp.bfloat16)


def shards(image_embeds, text_embeds, labels):
    row_count = image_embeds.shape[0]
    count = lax.axis_size("dp")
    here = lax.axis_index("dp")
    rank = here % LEVEL
    positions = here * row_count + jnp.arange(row_count, dtype=jnp.int32)
    texts, images = exchange(text_embeds, image_embeds, rank)
    row_scores = [similarity(image_embeds, t) for t in texts]
    col_scores = [similarity(i, text_embeds) for i in images]
    row_norm = log_sums(row_scores, 1)
    col_norm = log_sums(col_scores, 0)
    norms = jnp.stack([row_norm, col_norm])
    table = lax.all_to_all(
        jnp.broadcast_to(norms[None], (count, *norms.shape)), "dp", 0, 0, tiled=False
    )
    level = here - rank
    text_at = (level + jnp.array(TEXT_PLACES, jnp.int32)[rank] + count) % count
    image_at = (level + jnp.array(IMAGE_PLACES, jnp.int32)[rank] + count) % count
    positive = labels[:, None] == positions[None, :]
    image_sum = 0.0
    text_sum = 0.0
    for slot in range(WINDOW):
        own = positive if slot == 0 else None
        far_cols = lax.dynamic_index_in_dim(table, text_at[slot], 0, False)[1]
        mixing = weights(row_scores[slot], row_norm, far_cols, own)
        image_sum += jnp.dot(mixing, texts[slot], preferred_element_type=jnp.float32)
        far_rows = lax.dynamic_index_in_dim(table, image_at[slot], 0, False)[0]
        mixing = weights(col_scores[slot], far_rows, col_norm, own)
        text_sum += lax.dot_general(
            mixing, images[slot], (((0,), (0,)), ((), ())), preferred_element_type=jnp.float32
        )
    return (half_scale * image_sum, half_scale * text_sum)


def solution(mesh):
    return jax.shard_map(
        shards,
        mesh=mesh,
        in_specs=(P(("groups", "dp"), None), P(("groups", "dp"), None), P(("groups", "dp"))),
        out_specs=(P(("groups", "dp"), None), P(("groups", "dp"), None)),
        check_vma=False,
    )
```

time: 169 us -> 153 us (0.905)
  blocking collectives: 43.7 us -> 0 us
  starting transfers between devices: 65.4 us -> 25.1 us
  between operations: 0.91 us -> 31.5 us
  waiting for transfers between devices: 37.8 us -> 57.5 us
  local copies, waits for them, and re-layouts: 0.21 us -> 9.5 us
  other arithmetic: 1.61 us -> 5.38 us
  matrix products: 18.8 us -> 22.5 us
    ppermute x14 -> x16, starting transfers between devices: 65.4 us -> 20.5 us  [send(): return lax.ppermute(block, 'dp', route(count, moves))]
    all_gather x2 -> x0, blocking collectives: 43.7 us -> none  [the longest x1 26.1 us: shards(): lax.all_gather(col_norm, 'dp', axis=0, tiled=True)]
    ppermute x14 -> x16, waiting for transfers between devices: 37.8 us -> 50.8 us  [send(): return lax.ppermute(block, 'dp', route(count, moves))]
    unnamed x6 -> x98, local copies, waits for them, and re-layouts: 0.02 us -> 6.74 us
    all_to_all x0 -> x1, waiting for transfers between devices: none -> 6.66 us  [shards(): lax.all_to_all(jnp.broadcast_to(norms[None], (count, *norms.shape)), 'dp'...]
    select_n x0 -> x3, other arithmetic: none -> 4.62 us  [the longest x1 2.53 us: exchange(): own_c = send(jnp.where(even, image, text), cores)]
    all_to_all x0 -> x1, starting transfers between devices: none -> 4.6 us  [shards(): lax.all_to_all(jnp.broadcast_to(norms[None], (count, *norms.shape)), 'dp'...]
    dot_general x16, matrix products: 10.1 us -> 12.9 us  [the longest x8 6.83 us: shards(): jnp.dot(mixing, texts[slot], preferred_element_type=jnp.float32)]
  transfers between devices with their start and end apart: 14 -> 17, of which waited for: 8 -> 6; matrix products, arithmetic and copies ran while one was open for 5% -> 10% of each run, Pallas kernels for 0% -> 0%
where the time goes in v1:
time: 153 us; the launch traced here: 151 us
  waiting for transfers between devices  57.5 us (38%)
  between operations  31.5 us (21%)
  starting transfers between devices  25.1 us (16%)
  matrix products  22.5 us (15%)
  local copies, waits for them, and re-layouts  9.5 us (6%)
  other arithmetic  5.38 us (4%)
    ppermute x16, waiting for transfers between devices, send(): return lax.ppermute(block, 'dp', route(count, moves))  50.8 us
    ppermute x16, starting transfers between devices, send(): return lax.ppermute(block, 'dp', route(count, moves))  20.5 us
    dot_general x15, matrix products, similarity(): lax.dot_general(row_side, col_side, (((1,), (1,)), ((), ())), preferred_e...  9.58 us
    dot_general x8, matrix products, shards(): jnp.dot(mixing, texts[slot], preferred_element_type=jnp.float32)  6.83 us
    unnamed x98, local copies, waits for them, and re-layouts  6.74 us
    all_to_all x1, waiting for transfers between devices, shards(): lax.all_to_all(jnp.broadcast_to(norms[None], (count, *norms.shape)), 'dp'...  6.66 us
    dot_general x8, matrix products, shards(): lax.dot_general(mixing, images[slot], (((0,), (0,)), ((), ())), preferred...  6.06 us
    all_to_all x1, starting transfers between devices, shards(): lax.all_to_all(jnp.broadcast_to(norms[None], (count, *norms.shape)), 'dp'...  4.6 us
  transfers between devices with their start and end apart: 17, of which 6 were waited for; matrix products, arithmetic and copies ran while one was open for 10% of the time, Pallas kernels for 0%

profile of v1, /device:TPU:0, one launch (start us, length us, event | category | flops | bytes accessed | tf_op | source)
XLA Modules:
  0.0 151.5 jit_solution(1594580773136270947)
XLA Ops:
  0.6 5.1 %collective-permute-start = (bf16[256,1280]{1,0:T(8,128)(2,1)}, bf16[256,1280]{1,0:T(8,128)(2,1)}, u32[]{:S(2)}, u32[]{:S(2)}) collective-permute-start(bf16[256,1280]{1,0:T(8,128)(2,1)} %param.6), channel_id=1, source_target_pairs={{4,0},{5,1},{6,2},{7,3},{8,4},{9,5},{10,6},{11,7},{12,8},{13,9},{1... | collective-permute-start | bytes 1966088 | tf_op jit(solution)/shard_map/ppermute | solution.py:26
  5.7 2.5 %broadcast_select_fusion.9 = (bf16[256,1280]{1,0:T(8,128)(2,1)}, bf16[256,1280]{1,0:T(8,128)(2,1)}) fusion(bf16[256,1280]{1,0:T(8,128)(2,1)} %param.5, bf16[256,1280]{1,0:T(8,128)(2,1)} %param.6, pred[]{:T(512)S(6)} %eq.22, pred[]{:T(512)S(6)} %lt.76), kind=kLoop, calls=%fused_computation.40 | loop fusion | flops 655360 | bytes 2621442 | tf_op jit(solution)/shard_map/jit(_where)/select_n | solution.py:34
  8.3 1.5 %collective-permute-start.9 = (bf16[256,1280]{1,0:T(8,128)(2,1)}, bf16[256,1280]{1,0:T(8,128)(2,1)}, u32[]{:S(2)}, u32[]{:S(2)}) collective-permute-start(bf16[256,1280]{1,0:T(8,128)(2,1)} %get-tuple-element.30), channel_id=1, source_target_pairs={{0,2},{1,3},{2,0},{3,1},{4,6},{5,7},{6,4},{7,5},{8,10},{9,11},{10,... | collective-permute-start | bytes 1966088 | tf_op jit(solution)/shard_map/ppermute | solution.py:26
  9.8 0.7 and_select_fusion
  11.0 10.2 %collective-permute-done = bf16[256,1280]{1,0:T(8,128)(2,1)} collective-permute-done((bf16[256,1280]{1,0:T(8,128)(2,1)}, bf16[256,1280]{1,0:T(8,128)(2,1)}, u32[]{:S(2)}, u32[]{:S(2)}) %collective-permute-start) | collective-permute-done | bytes 655392 | tf_op jit(solution)/shard_map/ppermute | solution.py:26
  21.2 6.2 %collective-permute-start.5 = (bf16[256,1280]{1,0:T(8,128)(2,1)}, bf16[256,1280]{1,0:T(8,128)(2,1)S(1)}, u32[]{:S(2)}, u32[]{:S(2)}) collective-permute-start(bf16[256,1280]{1,0:T(8,128)(2,1)} %collective-permute-done), channel_id=1, source_target_pairs={{4,0},{5,1},{6,2},{8,4},{9,5},{10,6},{12,8},{13,9},{14,10},{0,12},... | collective-permute-start | bytes 1966088 | tf_op jit(solution)/shard_map/ppermute | solution.py:26
  27.4 8.8 %collective-permute-done.6 = bf16[256,1280]{1,0:T(8,128)(2,1)} collective-permute-done((bf16[256,1280]{1,0:T(8,128)(2,1)}, bf16[256,1280]{1,0:T(8,128)(2,1)}, u32[]{:S(2)}, u32[]{:S(2)}) %collective-permute-start.6) | collective-permute-done | bytes 655392 | tf_op jit(solution)/shard_map/ppermute | solution.py:26
  36.2 1.5 collective-permute-start.7
  37.7 0.7 fusion.74
  48.1 0.7 fusion.73
  69.2 2.4 %collective-permute-start.14 = (bf16[256,1280]{1,0:T(8,128)(2,1)}, bf16[256,1280]{1,0:T(8,128)(2,1)S(1)}, u32[]{:S(2)}, u32[]{:S(2)}) collective-permute-start(bf16[256,1280]{1,0:T(8,128)(2,1)} %collective-permute-done.6), channel_id=1, source_target_pairs={{0,2},{1,3},{2,0},{3,1},{4,6},{5,7},{6,4},{7,5},{8,10},{9,11},{10,... | collective-permute-start | bytes 1966088 | tf_op jit(solution)/shard_map/ppermute | solution.py:26
  71.7 1.5 fusion.81
  73.2 1.6 %fusion.88 = (f32[256]{0:T(256)S(1)}, f32[256,256]{1,0:T(8,128)S(1)}) fusion(bf16[256,1280]{1,0:T(8,128)(2,1)S(1)} %copy-done, bf16[256,1280]{1,0:T(8,128)(2,1)} %collective-permute-done), kind=kOutput, calls=%fused_computation.181 | convolution fusion | flops 167902976 | bytes 1573888 | tf_op jit(solution)/shard_map/dot_general | solution.py:73
  74.9 0.8 copy-done.47
  75.7 1.4 broadcast_select_fusion.8
  77.1 10.4 %collective-permute-done.14 = bf16[256,1280]{1,0:T(8,128)(2,1)S(1)} collective-permute-done((bf16[256,1280]{1,0:T(8,128)(2,1)}, bf16[256,1280]{1,0:T(8,128)(2,1)S(1)}, u32[]{:S(2)}, u32[]{:S(2)}) %collective-permute-start.14) | collective-permute-done | bytes 655392 | tf_op jit(solution)/shard_map/ppermute | solution.py:26
  87.5 2.0 %collective-permute-start.10 = (bf16[256,1280]{1,0:T(8,128)(2,1)S(1)}, bf16[256,1280]{1,0:T(8,128)(2,1)S(1)}, u32[]{:S(2)}, u32[]{:S(2)}) collective-permute-start(bf16[256,1280]{1,0:T(8,128)(2,1)S(1)} %get-tuple-element.32), channel_id=1, source_target_pairs={{0,2},{1,3},{2,0},{3,1},{4,6},{5,7},{6,4},{7,5},{8,10},{9,11},{10,... | collective-permute-start | bytes 1966088 | tf_op jit(solution)/shard_map/ppermute | solution.py:26
  89.9 11.6 %collective-permute-done.2 = bf16[256,1280]{1,0:T(8,128)(2,1)S(1)} collective-permute-done((bf16[256,1280]{1,0:T(8,128)(2,1)}, bf16[256,1280]{1,0:T(8,128)(2,1)S(1)}, u32[]{:S(2)}, u32[]{:S(2)}) %collective-permute-start.2) | collective-permute-done | bytes 655392 | tf_op jit(solution)/shard_map/ppermute | solution.py:26
  104.0 9.7 %collective-permute-done.10 = bf16[256,1280]{1,0:T(8,128)(2,1)S(1)} collective-permute-done((bf16[256,1280]{1,0:T(8,128)(2,1)S(1)}, bf16[256,1280]{1,0:T(8,128)(2,1)S(1)}, u32[]{:S(2)}, u32[]{:S(2)}) %collective-permute-start.10) | collective-permute-done | bytes 655392 | tf_op jit(solution)/shard_map/ppermute | solution.py:26
  116.8 1.6 %fusion.83 = (f32[256]{0:T(256)S(1)}, f32[256,256]{1,0:T(8,128)S(1)}) fusion(bf16[256,1280]{1,0:T(8,128)(2,1)S(1)} %copy-done, bf16[256,1280]{1,0:T(8,128)(2,1)} %collective-permute-done.9, bf16[256,1280]{1,0:T(8,128)(2,1)S(1)} %collective-permute-done.10, pred[]{:T(512)S(6)} %lt.76), kind=kOutput, calls=%fused_computation.176 | convolution fusion | flops 168230656 | bytes 2229249 | tf_op jit(solution)/shard_map/dot_general | solution.py:73
  119.6 0.7 exponential_reduce_fusion.14
  120.4 0.6 broadcast_in_dim.2
  121.0 4.6 %all-to-all-start = ((f32[16,2,256]{2,1,0:T(2,128)}), f32[16,2,256]{2,1,0:T(2,128)}, u32[]{:S(2)}, u32[]{:S(2)}) async-start(f32[16,2,256]{2,1,0:T(2,128)} %broadcast_in_dim.2), calls=%async_computation | async-start | bytes 65536 | tf_op jit(solution)/shard_map/all_to_all | solution.py:106
  125.6 6.7 %all-to-all-done = f32[16,2,256]{2,1,0:T(2,128)} async-done(((f32[16,2,256]{2,1,0:T(2,128)}), f32[16,2,256]{2,1,0:T(2,128)}, u32[]{:S(2)}, u32[]{:S(2)}) %all-to-all-start) | async-done | bytes 32800 | tf_op jit(solution)/shard_map/all_to_all | solution.py:106
  132.3 0.8 constant_dynamic-slice_fusion
  134.1 0.6 copy-done.3
  139.0 1.6 %fusion.12 = f32[256,1280]{1,0:T(8,128)S(1)} fusion(bf16[256,1280]{1,0:T(8,128)(2,1)} %collective-permute-done.9, bf16[256,1280]{1,0:T(8,128)(2,1)S(1)} %copy-done.5, pred[]{:T(512)S(6)} %lt.76, f32[256,256]{1,0:T(8,128)S(1)} %copy-done.41, f32[256]{0:T(256)S(1)} %bitcast.84, f32[256]{0:T(256)S(1)} %log_add_fusion.1), kind=kOutput, calls=%fused_computation.77 | convolution fusion | flops 168361984 | bytes 2885633 | tf_op jit(solution)/shard_map/dot_general | solution.py:119
  140.6 1.6 %convolution_add_fusion.3 = f32[256,1280]{1,0:T(8,128)S(1)} fusion(f32[256,1280]{1,0:T(8,128)S(1)} %fusion.16, bf16[256,1280]{1,0:T(8,128)(2,1)} %collective-permute-done.6, f32[256,256]{1,0:T(8,128)S(1)} %copy-done.21, f32[256]{0:T(256)S(1)} %bitcast.83, f32[256]{0:T(256)S(1)} %log_add_fusion), kind=kOutput, calls=%fused_computation.3 | convolution fusion | flops 168361984 | bytes 3540992 | tf_op jit(solution)/shard_map/dot_general | solution.py:122
  144.8 1.5 %fusion.7 = f32[256,1280]{1,0:T(8,128)} fusion(f32[256,1280]{1,0:T(8,128)S(1)} %fusion.6, bf16[256,1280]{1,0:T(8,128)(2,1)S(1)} %copy-done.17, bf16[256,1280]{1,0:T(8,128)(2,1)S(1)} %copy-done.15, pred[]{:T(512)S(6)} %lt.76, f32[256,256]{1,0:T(8,128)S(1)} %copy-done.37, f32[256]{0:T(256)S(1)} %bitcast.92, f32[256]{0:T(256)S(1)} %log_add_fusion), kind=kOutput, calls=%fused_computation.15 | convolution fusion | flops 169017344 | bytes 4196353 | tf_op jit(solution)/shard_map/dot_general | solution.py:122
  146.3 1.5 %convolution_add_fusion.7 = f32[256,1280]{1,0:T(8,128)S(1)} fusion(f32[256,1280]{1,0:T(8,128)S(1)} %fusion.18, bf16[256,1280]{1,0:T(8,128)(2,1)} %collective-permute-done, f32[256,256]{1,0:T(8,128)S(1)} %copy-done.19, f32[256]{0:T(256)S(1)} %bitcast.81, f32[256]{0:T(256)S(1)} %log_add_fusion.1), kind=kOutput, calls=%fused_computation.7 | convolution fusion | flops 168361984 | bytes 3540992 | tf_op jit(solution)/shard_map/dot_general | solution.py:119
  148.3 0.6 copy-done.13
  149.9 1.5 %fusion.3 = f32[256,1280]{1,0:T(8,128)} fusion(f32[256,1280]{1,0:T(8,128)S(1)} %fusion.2, bf16[256,1280]{1,0:T(8,128)(2,1)S(1)} %copy-done.15, bf16[256,1280]{1,0:T(8,128)(2,1)S(1)} %copy-done.17, pred[]{:T(512)S(6)} %lt.76, f32[256,256]{1,0:T(8,128)S(1)} %copy-done.35, f32[256]{0:T(256)S(1)} %bitcast.90, f32[256]{0:T(256)S(1)} %log_add_fusion.1), kind=kOutput, calls=%fused_computation.11 | convolution fusion | flops 169017344 | bytes 4196353 | tf_op jit(solution)/shard_map/dot_general | solution.py:119
  (144 shorter events, 16.6 us)
Async XLA Ops:
  0.6 20.6 %collective-permute-start = (bf16[256,1280]{1,0:T(8,128)(2,1)}, bf16[256,1280]{1,0:T(8,128)(2,1)}, u32[]{:S(2)}, u32[]{:S(2)}) collective-permute-start(bf16[256,1280]{1,0:T(8,128)(2,1)} %param.6), channel_id=1, source_target_pairs={{4,0},{5,1},{6,2},{7,3},{8,4},{9,5},{10,6},{11,7},{12,8},{13,9},{1... | collective-permute-start | bytes 1966088 | tf_op jit(solution)/shard_map/ppermute | solution.py:26
  5.7 30.4 %collective-permute-start.6 = (bf16[256,1280]{1,0:T(8,128)(2,1)}, bf16[256,1280]{1,0:T(8,128)(2,1)}, u32[]{:S(2)}, u32[]{:S(2)}) collective-permute-start(bf16[256,1280]{1,0:T(8,128)(2,1)} %param.5), channel_id=1, source_target_pairs={{12,0},{13,1},{14,2},{15,3},{0,4},{1,5},{2,6},{3,7},{4,8},{5,9},{6... | collective-permute-start | bytes 1966088 | tf_op jit(solution)/shard_map/ppermute | solution.py:26
  5.7 4.8 %copy-start = (bf16[256,1280]{1,0:T(8,128)(2,1)S(1)}, bf16[256,1280]{1,0:T(8,128)(2,1)}, u32[]{:S(2)}) copy-start(bf16[256,1280]{1,0:T(8,128)(2,1)} %param.5) | copy-start | bytes 1966084
  5.7 4.8 %copy-start.1 = (bf16[256,1280]{1,0:T(8,128)(2,1)S(1)}, bf16[256,1280]{1,0:T(8,128)(2,1)}, u32[]{:S(2)}) copy-start(bf16[256,1280]{1,0:T(8,128)(2,1)} %param.6) | copy-start | bytes 1966084
  8.3 93.7 %collective-permute-start.9 = (bf16[256,1280]{1,0:T(8,128)(2,1)}, bf16[256,1280]{1,0:T(8,128)(2,1)}, u32[]{:S(2)}, u32[]{:S(2)}) collective-permute-start(bf16[256,1280]{1,0:T(8,128)(2,1)} %get-tuple-element.30), channel_id=1, source_target_pairs={{0,2},{1,3},{2,0},{3,1},{4,6},{5,7},{6,4},{7,5},{8,10},{9,11},{10,... | collective-permute-start | bytes 1966088 | tf_op jit(solution)/shard_map/ppermute | solution.py:26
  21.2 53.6 %collective-permute-start.5 = (bf16[256,1280]{1,0:T(8,128)(2,1)}, bf16[256,1280]{1,0:T(8,128)(2,1)S(1)}, u32[]{:S(2)}, u32[]{:S(2)}) collective-permute-start(bf16[256,1280]{1,0:T(8,128)(2,1)} %collective-permute-done), channel_id=1, source_target_pairs={{4,0},{5,1},{6,2},{8,4},{9,5},{10,6},{12,8},{13,9},{14,10},{0,12},... | collective-permute-start | bytes 1966088 | tf_op jit(solution)/shard_map/ppermute | solution.py:26
  36.2 39.5 %collective-permute-start.7 = (bf16[256,1280]{1,0:T(8,128)(2,1)}, bf16[256,1280]{1,0:T(8,128)(2,1)}, u32[]{:S(2)}, u32[]{:S(2)}) collective-permute-start(bf16[256,1280]{1,0:T(8,128)(2,1)} %collective-permute-done.6), channel_id=1, source_target_pairs={{13,1},{14,2},{15,3},{1,5},{2,6},{3,7},{5,9},{6,10},{7,11},{9,13},... | collective-permute-start | bytes 1966088 | tf_op jit(solution)/shard_map/ppermute | solution.py:26
  69.2 18.3 %collective-permute-start.14 = (bf16[256,1280]{1,0:T(8,128)(2,1)}, bf16[256,1280]{1,0:T(8,128)(2,1)S(1)}, u32[]{:S(2)}, u32[]{:S(2)}) collective-permute-start(bf16[256,1280]{1,0:T(8,128)(2,1)} %collective-permute-done.6), channel_id=1, source_target_pairs={{0,2},{1,3},{2,0},{3,1},{4,6},{5,7},{6,4},{7,5},{8,10},{9,11},{10,... | collective-permute-start | bytes 1966088 | tf_op jit(solution)/shard_map/ppermute | solution.py:26
  71.6 29.9 %collective-permute-start.2 = (bf16[256,1280]{1,0:T(8,128)(2,1)}, bf16[256,1280]{1,0:T(8,128)(2,1)S(1)}, u32[]{:S(2)}, u32[]{:S(2)}) collective-permute-start(bf16[256,1280]{1,0:T(8,128)(2,1)} %collective-permute-done), channel_id=1, source_target_pairs={{0,2},{1,3},{2,0},{3,1},{4,6},{5,7},{6,4},{7,5},{8,10},{9,11},{10,... | collective-permute-start | bytes 1966088 | tf_op jit(solution)/shard_map/ppermute | solution.py:26
  73.2 46.3 %copy-start.20 = (f32[256,256]{1,0:T(8,128)}, f32[256,256]{1,0:T(8,128)S(1)}, u32[]{:S(2)}) copy-start(f32[256,256]{1,0:T(8,128)S(1)} %get-tuple-element.79) | copy-start | bytes 786436
  74.8 44.7 %copy-start.18 = (f32[256,256]{1,0:T(8,128)}, f32[256,256]{1,0:T(8,128)S(1)}, u32[]{:S(2)}) copy-start(f32[256,256]{1,0:T(8,128)S(1)} %get-tuple-element.93) | copy-start | bytes 786436
  74.8 27.8 %collective-permute-start.13 = (bf16[256,1280]{1,0:T(8,128)(2,1)}, bf16[256,1280]{1,0:T(8,128)(2,1)S(1)}, u32[]{:S(2)}, u32[]{:S(2)}) collective-permute-start(bf16[256,1280]{1,0:T(8,128)(2,1)} %collective-permute-done.6), channel_id=1, source_target_pairs={{0,1},{1,0},{2,3},{3,2},{4,5},{5,4},{6,7},{7,6},{8,9},{9,8},{10,11... | collective-permute-start | bytes 1966088 | tf_op jit(solution)/shard_map/ppermute | solution.py:26
  75.7 27.4 %collective-permute-start.1 = (bf16[256,1280]{1,0:T(8,128)(2,1)}, bf16[256,1280]{1,0:T(8,128)(2,1)S(1)}, u32[]{:S(2)}, u32[]{:S(2)}) collective-permute-start(bf16[256,1280]{1,0:T(8,128)(2,1)} %collective-permute-done), channel_id=1, source_target_pairs={{0,1},{1,0},{2,3},{3,2},{4,5},{5,4},{6,7},{7,6},{8,9},{9,8},{10,11... | collective-permute-start | bytes 1966088 | tf_op jit(solution)/shard_map/ppermute | solution.py:26
  87.5 14.5 %copy-start.2 = (bf16[256,1280]{1,0:T(8,128)(2,1)}, bf16[256,1280]{1,0:T(8,128)(2,1)S(1)}, u32[]{:S(2)}) copy-start(bf16[256,1280]{1,0:T(8,128)(2,1)S(1)} %collective-permute-done.14) | copy-start | bytes 1966084
  87.5 14.5 %copy-start.46 = (bf16[256,1280]{1,0:T(8,128)(2,1)S(1)}, bf16[256,1280]{1,0:T(8,128)(2,1)}, u32[]{:S(2)}) copy-start(bf16[256,1280]{1,0:T(8,128)(2,1)} %get-tuple-element.29) | copy-start | bytes 1966084
  87.5 26.3 %collective-permute-start.10 = (bf16[256,1280]{1,0:T(8,128)(2,1)S(1)}, bf16[256,1280]{1,0:T(8,128)(2,1)S(1)}, u32[]{:S(2)}, u32[]{:S(2)}) collective-permute-start(bf16[256,1280]{1,0:T(8,128)(2,1)S(1)} %get-tuple-element.32), channel_id=1, source_target_pairs={{0,2},{1,3},{2,0},{3,1},{4,6},{5,7},{6,4},{7,5},{8,10},{9,11},{10,... | collective-permute-start | bytes 1966088 | tf_op jit(solution)/shard_map/ppermute | solution.py:26
  89.9 29.6 %copy-start.24 = (f32[256,256]{1,0:T(8,128)}, f32[256,256]{1,0:T(8,128)S(1)}, u32[]{:S(2)}) copy-start(f32[256,256]{1,0:T(8,128)S(1)} %get-tuple-element.74) | copy-start | bytes 786436
  101.5 12.2 %collective-permute-start.15 = (bf16[256,1280]{1,0:T(8,128)(2,1)S(1)}, bf16[256,1280]{1,0:T(8,128)(2,1)S(1)}, u32[]{:S(2)}, u32[]{:S(2)}) collective-permute-start(bf16[256,1280]{1,0:T(8,128)(2,1)S(1)} %collective-permute-done.14), channel_id=1, source_target_pairs={{0,1},{1,0},{2,3},{3,2},{4,5},{5,4},{6,7},{7,6},{8,9},{9,8},{10,11... | collective-permute-start | bytes 1966088 | tf_op jit(solution)/shard_map/ppermute | solution.py:26
  102.0 17.5 %copy-start.26 = (f32[256,256]{1,0:T(8,128)}, f32[256,256]{1,0:T(8,128)S(1)}, u32[]{:S(2)}) copy-start(f32[256,256]{1,0:T(8,128)S(1)} %get-tuple-element.89) | copy-start | bytes 786436
  102.0 12.7 %collective-permute-start.4 = (bf16[256,1280]{1,0:T(8,128)(2,1)S(1)}, bf16[256,1280]{1,0:T(8,128)(2,1)S(1)}, u32[]{:S(2)}, u32[]{:S(2)}) collective-permute-start(bf16[256,1280]{1,0:T(8,128)(2,1)S(1)} %copy-done.46), channel_id=1, source_target_pairs={{0,1},{1,0},{2,3},{3,2},{4,5},{5,4},{6,7},{7,6},{8,9},{9,8},{10,11... | collective-permute-start | bytes 1966088 | tf_op jit(solution)/shard_map/ppermute | solution.py:26
  102.6 12.1 %collective-permute-start.8 = (bf16[256,1280]{1,0:T(8,128)(2,1)S(1)}, bf16[256,1280]{1,0:T(8,128)(2,1)S(1)}, u32[]{:S(2)}, u32[]{:S(2)}) collective-permute-start(bf16[256,1280]{1,0:T(8,128)(2,1)S(1)} %get-tuple-element.31), channel_id=1, source_target_pairs={{0,1},{1,0},{2,3},{3,2},{4,5},{5,4},{6,7},{7,6},{8,9},{9,8},{10,11... | collective-permute-start | bytes 1966088 | tf_op jit(solution)/shard_map/ppermute | solution.py:26
  103.1 16.5 %copy-start.28 = (f32[256,256]{1,0:T(8,128)}, f32[256,256]{1,0:T(8,128)S(1)}, u32[]{:S(2)}) copy-start(f32[256,256]{1,0:T(8,128)S(1)} %get-tuple-element.76) | copy-start | bytes 786436
  103.1 15.3 %collective-permute-start.11 = (bf16[256,1280]{1,0:T(8,128)(2,1)}, bf16[256,1280]{1,0:T(8,128)(2,1)S(1)}, u32[]{:S(2)}, u32[]{:S(2)}) collective-permute-start(bf16[256,1280]{1,0:T(8,128)(2,1)} %collective-permute-done.9), channel_id=1, source_target_pairs={{0,1},{1,0},{2,3},{3,2},{4,5},{5,4},{6,7},{7,6},{8,9},{9,8},{10,11... | collective-permute-start | bytes 1966088 | tf_op jit(solution)/shard_map/ppermute | solution.py:26
  104.0 15.5 %copy-start.22 = (f32[256,256]{1,0:T(8,128)}, f32[256,256]{1,0:T(8,128)S(1)}, u32[]{:S(2)}) copy-start(f32[256,256]{1,0:T(8,128)S(1)} %get-tuple-element.91) | copy-start | bytes 786436
  113.8 2.1 %collective-permute-start.3 = (bf16[256,1280]{1,0:T(8,128)(2,1)S(1)}, bf16[256,1280]{1,0:T(8,128)(2,1)S(1)}, u32[]{:S(2)}, u32[]{:S(2)}) collective-permute-start(bf16[256,1280]{1,0:T(8,128)(2,1)S(1)} %collective-permute-done.2), channel_id=1, source_target_pairs={{0,1},{1,0},{2,3},{3,2},{4,5},{5,4},{6,7},{7,6},{8,9},{9,8},{10,11... | collective-permute-start | bytes 1966088 | tf_op jit(solution)/shard_map/ppermute | solution.py:26
  113.8 4.6 %collective-permute-start.12 = (bf16[256,1280]{1,0:T(8,128)(2,1)S(1)}, bf16[256,1280]{1,0:T(8,128)(2,1)S(1)}, u32[]{:S(2)}, u32[]{:S(2)}) collective-permute-start(bf16[256,1280]{1,0:T(8,128)(2,1)S(1)} %collective-permute-done.10), channel_id=1, source_target_pairs={{0,1},{1,0},{2,3},{3,2},{4,5},{5,4},{6,7},{7,6},{8,9},{9,8},{10,11... | collective-permute-start | bytes 1966088 | tf_op jit(solution)/shard_map/ppermute | solution.py:26
  114.7 4.9 %copy-start.32 = (f32[256,256]{1,0:T(8,128)}, f32[256,256]{1,0:T(8,128)S(1)}, u32[]{:S(2)}) copy-start(f32[256,256]{1,0:T(8,128)S(1)} %get-tuple-element.72) | copy-start | bytes 786436
  115.1 4.4 %copy-start.42 = (f32[256,256]{1,0:T(8,128)}, f32[256,256]{1,0:T(8,128)S(1)}, u32[]{:S(2)}) copy-start(f32[256,256]{1,0:T(8,128)S(1)} %get-tuple-element.70) | copy-start | bytes 786436
  115.8 3.7 %copy-start.38 = (f32[256,256]{1,0:T(8,128)}, f32[256,256]{1,0:T(8,128)S(1)}, u32[]{:S(2)}) copy-start(f32[256,256]{1,0:T(8,128)S(1)} %get-tuple-element.85) | copy-start | bytes 786436
  116.3 3.3 %copy-start.30 = (f32[256,256]{1,0:T(8,128)}, f32[256,256]{1,0:T(8,128)S(1)}, u32[]{:S(2)}) copy-start(f32[256,256]{1,0:T(8,128)S(1)} %get-tuple-element.87) | copy-start | bytes 786436
  119.6 13.5 %copy-start.48 = (s32[256]{0:T(256)S(1)}, s32[256]{0:T(256)}, u32[]{:S(2)}) copy-start(s32[256]{0:T(256)} %param.7) | copy-start | bytes 3076
  121.0 11.3 %all-to-all-start = ((f32[16,2,256]{2,1,0:T(2,128)}), f32[16,2,256]{2,1,0:T(2,128)}, u32[]{:S(2)}, u32[]{:S(2)}) async-start(f32[16,2,256]{2,1,0:T(2,128)} %broadcast_in_dim.2), calls=%async_computation | async-start | bytes 65536 | tf_op jit(solution)/shard_map/all_to_all | solution.py:106
  (34 other events, 43.2 us)

commit v2 on v0

v2 whole, which is shorter than its diff:
```python
import jax
import jax.numpy as jnp
from jax import lax
from jax.experimental import pallas as pl
from jax.experimental.pallas import tpu as pltpu
from jax.sharding import PartitionSpec as P

WINDOW = 8
LEVEL = 4
ROW_PLACE = 16
TABLE_ROWS = 24

logit_scale = 100.0
half_scale = 50.0
vmem_bytes = 48 * 1024 * 1024


def send(block, moves):
    count = lax.axis_size("dp")
    route = [
        ((level * LEVEL + a) % count, (level * LEVEL + b) % count)
        for level in range(count // LEVEL)
        for a, b in moves
    ]
    return lax.ppermute(block, "dp", route)


def after(block, *earlier):
    return lax.optimization_barrier((block, *earlier))[0]


def scores_of(rows, cols):
    products = lax.dot_general(
        rows, cols, (((1,), (1,)), ((), ())), preferred_element_type=jnp.float32
    )
    return logit_scale * products


def as_column(row):
    return jnp.transpose(jnp.broadcast_to(row, (128, row.shape[1])))[:, :1]


def as_row(column):
    return jnp.transpose(jnp.broadcast_to(column, (column.shape[0], 128)))[:1, :]


def near_offsets(rank):
    return 0, 4, 5 - 2 * (rank % 2), 6 - 4 * (rank // 2), 7 - 2 * rank


def for_far(rank, pairs, body):
    even = rank % 2 == 0
    low = rank < 2
    cases = (
        (even, pairs[0], 1),
        (jnp.logical_not(even), pairs[1], 7),
        (low, pairs[2], 2),
        (jnp.logical_not(low), pairs[3], 6),
        (low, pairs[4], 3 - 2 * rank),
        (jnp.logical_not(low), pairs[5], 11 - 2 * rank),
    )
    for index, (chosen, ref, offset) in enumerate(cases):
        pl.when(chosen)(lambda: body(index // 2, ref, offset))


def near_scores(*refs):
    own, others = refs[0], refs[1:6]
    score_ref, peak_ref, total_ref, stat_ref = refs[6:]
    rank = lax.axis_index("dp") % LEVEL
    offsets = near_offsets(rank)
    stat_ref[...] = jnp.zeros_like(stat_ref)
    for slot, other in enumerate(others):
        scores = scores_of(own[...], other[...])
        score_ref[slot] = scores
        peak = jnp.max(scores, axis=0, keepdims=True)
        total = jnp.sum(jnp.exp(scores - peak), axis=0, keepdims=True)
        stat_ref[pl.ds(offsets[slot], 1), :] = peak
        stat_ref[pl.ds(WINDOW + offsets[slot], 1), :] = total
    peak = jnp.max(jnp.max(score_ref[...], axis=0), axis=1, keepdims=True)
    shifted = jnp.exp(score_ref[...] - peak[None])
    total = jnp.sum(jnp.sum(shifted, axis=0), axis=1, keepdims=True)
    peak_ref[...] = jnp.broadcast_to(peak, peak_ref.shape)
    total_ref[...] = jnp.broadcast_to(total, total_ref.shape)


def far_scores(*refs):
    own, pairs = refs[0], refs[1:7]
    near_peak, near_total, near_stat = refs[7:10]
    score_ref, norm_ref, table_ref, stat_ref = refs[10:]
    rank = lax.axis_index("dp") % LEVEL
    stat_ref[...] = near_stat[...]

    def one(slot, other, offset):
        scores = scores_of(own[...], other[...])
        score_ref[slot] = scores
        peak = jnp.max(scores, axis=0, keepdims=True)
        total = jnp.sum(jnp.exp(scores - peak), axis=0, keepdims=True)
        stat_ref[pl.ds(offset, 1), :] = peak
        stat_ref[pl.ds(WINDOW + offset, 1), :] = total

    for_far(rank, pairs, one)
    old_peak = near_peak[:, :1]
    peak = jnp.max(jnp.max(score_ref[...], axis=0), axis=1, keepdims=True)
    peak = jnp.maximum(peak, old_peak)
    shifted = jnp.exp(score_ref[...] - peak[None])
    total = jnp.sum(jnp.sum(shifted, axis=0), axis=1, keepdims=True)
    total = total + near_total[:, :1] * jnp.exp(old_peak - peak)
    norm = peak + jnp.log(total)
    norm_ref[...] = jnp.broadcast_to(norm, norm_ref.shape)
    stat_ref[pl.ds(ROW_PLACE, 1), :] = as_row(norm)
    for index in range(table_ref.shape[0]):
        table_ref[index] = stat_ref[...]


def merged_column(table, text):
    count = table.shape[0]
    peaks = []
    totals = []
    for offset in range(WINDOW):
        source = (text - offset + count) % count
        peaks.append(table[source, pl.ds(offset, 1), :])
        totals.append(table[source, pl.ds(WINDOW + offset, 1), :])
    peaks = jnp.concatenate(peaks, axis=0)
    totals = jnp.concatenate(totals, axis=0)
    peak = jnp.max(peaks, axis=0, keepdims=True)
    total = jnp.sum(totals * jnp.exp(peaks - peak), axis=0, keepdims=True)
    return peak + jnp.log(total)


def mixed(scores, self_norm, other_norm, positive=None):
    combined = jnp.exp(scores - self_norm) + jnp.exp(scores - other_norm)
    if positive is not None:
        combined = combined - 2.0 * positive.astype(jnp.float32)
    return combined.astype(jnp.bfloat16)


def image_products(*refs):
    label_ref, norm_ref, table, near_ref, far_ref = refs[:5]
    near, pairs = refs[5:10], refs[10:16]
    out_ref = refs[16]
    here = lax.axis_index("dp")
    rank = here % LEVEL
    count = table.shape[0]
    norm = norm_ref[:, :1]
    rows = out_ref.shape[0]
    offsets = near_offsets(rank)
    for slot, other in enumerate(near):
        positive = None
        if slot == 0:
            lane = lax.broadcasted_iota(jnp.int32, (rows, rows), 1)
            positive = label_ref[...] == here * rows + lane
        col = merged_column(table, (here + offsets[slot]) % count)
        mixing = mixed(near_ref[slot], norm, col, positive)
        product = jnp.dot(mixing, other[...], preferred_element_type=jnp.float32)
        if slot == 0:
            out_ref[...] = product
        else:
            out_ref[...] += product

    def one(slot, other, offset):
        col = merged_column(table, (here + offset) % count)
        mixing = mixed(far_ref[slot], norm, col)
        out_ref[...] += jnp.dot(mixing, other[...], preferred_element_type=jnp.float32)

    for_far(rank, pairs, one)
    out_ref[...] = half_scale * out_ref[...]


def near_text_products(*refs):
    label_ref, table, own = refs[:3]
    near = refs[3:8]
    out_ref, norm_ref = refs[8:]
    here = lax.axis_index("dp")
    rank = LEVEL - 1 - here % LEVEL
    count = table.shape[0]
    rows = out_ref.shape[0]
    norm = as_column(merged_column(table, here))
    norm_ref[...] = jnp.broadcast_to(norm, norm_ref.shape)
    offsets = near_offsets(rank)
    for slot, other in enumerate(near):
        positive = None
        if slot == 0:
            sublane = lax.broadcasted_iota(jnp.int32, (rows, rows), 0)
            positive = label_ref[...] == here * rows + sublane
        source = (here - offsets[slot] + count) % count
        row = table[source, pl.ds(ROW_PLACE, 1), :]
        mixing = mixed(scores_of(own[...], other[...]), norm, row, positive)
        product = jnp.dot(mixing, other[...], preferred_element_type=jnp.float32)
        if slot == 0:
            out_ref[...] = product
        else:
            out_ref[...] += product


def far_text_products(*refs):
    norm_ref, table, own, sum_ref = refs[:4]
    pairs = refs[4:10]
    out_ref = refs[10]
    here = lax.axis_index("dp")
    rank = LEVEL - 1 - here % LEVEL
    count = table.shape[0]
    norm = norm_ref[:, :1]
    out_ref[...] = sum_ref[...]

    def one(slot, other, offset):
        source = (here - offset + count) % count
        row = table[source, pl.ds(ROW_PLACE, 1), :]
        mixing = mixed(scores_of(own[...], other[...]), norm, row)
        out_ref[...] += jnp.dot(mixing, other[...], preferred_element_type=jnp.float32)

    for_far(rank, pairs, one)
    out_ref[...] = half_scale * out_ref[...]


def kernel_call(body, outs, blocks, *operands):
    flops = 2 * 256 * 256 * 1280 * blocks
    return pl.pallas_call(
        body,
        out_shape=outs,
        in_specs=[pl.BlockSpec(memory_space=pltpu.VMEM)] * len(operands),
        out_specs=[pl.BlockSpec(memory_space=pltpu.VMEM)] * len(outs),
        compiler_params=pltpu.CompilerParams(vmem_limit_bytes=vmem_bytes),
        cost_estimate=pl.CostEstimate(
            flops=flops, bytes_accessed=blocks * 800000, transcendentals=blocks * 65536 * 2
        ),
        name=body.__name__,
    )(*operands)


cores = [(0, 1), (1, 0), (2, 3), (3, 2)]
across = [(0, 2), (1, 3), (2, 0), (3, 1)]


def shards(image, text, labels):
    rows, width = image.shape
    count = lax.axis_size("dp")
    f32 = jnp.float32

    t1 = send(text, [(r + 4, r) for r in range(4)])
    own_y_t = send(text, [(2, 0), (3, 1)])
    own_y_i = send(image, [(0, 2), (1, 3)])
    own_c_t = send(text, [(1, 0), (3, 2)])
    own_c_i = send(image, [(0, 1), (2, 3)])
    t2 = send(t1, [(r + 4, r) for r in (0, 1, 2)])
    t1_y = send(after(t1, own_y_t, own_y_i), across)
    t1_c = send(t1, cores)
    own_yc_t = send(own_y_t, [(0, 1), (1, 0)])
    own_yc_i = send(own_y_i, [(2, 3), (3, 2)])
    t1_yc = send(t1_y, cores)
    t2_y = send(after(t2, t1_y), [(0, 2), (1, 3)])
    t2_c = send(t2, [(0, 1), (2, 3)])
    t2_yc = send(t2_y, [(2, 3), (3, 2)])

    i1 = send(after(image, t1), [(r - 4, r) for r in range(4)])
    i2 = send(i1, [(r - 4, r) for r in (1, 2, 3)])
    i1_c = send(i1, cores)
    i1_y = send(after(i1, t1_y), across)
    i1_yc = send(i1_y, cores)
    i2_y = send(after(i2, i1_y), [(2, 0), (3, 1)])
    i2_c = send(i2, [(3, 2), (1, 0)])
    i2_yc = send(i2_y, [(0, 1), (1, 0)])

    near_t = [text, t1, t1_c, t1_y, t1_yc]
    far_t = [own_c_t, t2_c, own_y_t, t2_y, own_yc_t, t2_yc]
    near_i = [image, i1, i1_c, i1_y, i1_yc]
    far_i = [own_c_i, i2_c, own_y_i, i2_y, own_yc_i, i2_yc]

    def struct(*shape):
        return jax.ShapeDtypeStruct(shape, f32)

    near_s, peak, total, stat = kernel_call(
        near_scores,
        [struct(5, rows, rows), struct(rows, 128), struct(rows, 128), struct(TABLE_ROWS, rows)],
        5, image, *near_t,
    )
    far_s, norm, message, _ = kernel_call(
        far_scores,
        [struct(3, rows, rows), struct(rows, 128), struct(count, TABLE_ROWS, rows),
         struct(TABLE_ROWS, rows)],
        3, image, *far_t, peak, total, stat,
    )
    table = lax.all_to_all(message, "dp", 0, 0, tiled=True)
    (grad_images,) = kernel_call(
        image_products, [struct(rows, width)], 8,
        labels[:, None], norm, table, near_s, far_s, *near_t, *far_t,
    )
    near_sum, col_norm = kernel_call(
        near_text_products, [struct(rows, width), struct(rows, 128)], 10,
        labels[None, :], table, text, *near_i,
    )
    (grad_texts,) = kernel_call(
        far_text_products, [struct(rows, width)], 6, col_norm, table, text, near_sum, *far_i,
    )
    return grad_images, grad_texts


def solution(mesh):
    return jax.shard_map(
        shards,
        mesh=mesh,
        in_specs=(P(("groups", "dp"), None), P(("groups", "dp"), None), P(("groups", "dp"))),
        out_specs=(P(("groups", "dp"), None), P(("groups", "dp"), None)),
        check_vma=False,
    )
```

time: 169 us -> 131 us (0.78)
  blocking collectives: 43.7 us -> 0 us
  Pallas kernels: 0 us -> 20.4 us
  starting transfers between devices: 65.4 us -> 46.4 us
  matrix products: 18.8 us -> 0 us
  waiting for transfers between devices: 37.8 us -> 51.8 us
  local copies, waits for them, and re-layouts: 0.21 us -> 10.8 us
    all_gather x2 -> x0, blocking collectives: 43.7 us -> none  [the longest x1 26.1 us: shards(): lax.all_gather(col_norm, 'dp', axis=0, tiled=True)]
    ppermute x14 -> x22, starting transfers between devices: 65.4 us -> 37.3 us  [send(): return lax.ppermute(block, 'dp', route)]
    pallas_call x0 -> x5, Pallas kernels: none -> 20.4 us  [kernel_call(): pl.pallas_call(body, out_shape=outs, in_specs=[pl.BlockSpec(memory_space=...]
    dot_general x31 -> x0, matrix products: 18.8 us -> none  [the longest x15 8.64 us: similarity(): lax.dot_general(row_side, col_side, (((1,), (1,)), ((), ())), preferred_e...]
    ppermute x14 -> x22, waiting for transfers between devices: 37.8 us -> 49.8 us  [send(): return lax.ppermute(block, 'dp', route)]
    unnamed x6 -> x46, local copies, waits for them, and re-layouts: 0.02 us -> 10.7 us
    all_to_all x0 -> x1, starting transfers between devices: none -> 9.1 us  [shards(): table = lax.all_to_all(message, 'dp', 0, 0, tiled=True)]
    all_to_all x0 -> x1, waiting for transfers between devices: none -> 2.05 us  [shards(): table = lax.all_to_all(message, 'dp', 0, 0, tiled=True)]
  transfers between devices with their start and end apart: 14 -> 23, of which waited for: 8 -> 7; matrix products, arithmetic and copies ran while one was open for 5% -> 0% of each run, Pallas kernels for 0% -> 11%
where the time goes in v2:
time: 131 us; the launch traced here: 130 us
  waiting for transfers between devices  51.8 us (40%)
  starting transfers between devices  46.4 us (35%)
  Pallas kernels  20.4 us (16%)
  local copies, waits for them, and re-layouts  10.8 us (8%)
    ppermute x22, waiting for transfers between devices, send(): return lax.ppermute(block, 'dp', route)  49.8 us
    ppermute x22, starting transfers between devices, send(): return lax.ppermute(block, 'dp', route)  37.3 us
    pallas_call x5, Pallas kernels, kernel_call(): pl.pallas_call(body, out_shape=outs, in_specs=[pl.BlockSpec(memory_space=...  20.4 us
    unnamed x46, local copies, waits for them, and re-layouts  10.7 us
    all_to_all x1, starting transfers between devices, shards(): table = lax.all_to_all(message, 'dp', 0, 0, tiled=True)  9.1 us
  transfers between devices with their start and end apart: 23, of which 7 were waited for; matrix products, arithmetic and copies ran while one was open for 0% of the time, Pallas kernels for 11%

profile of v2, /device:TPU:0, one launch (start us, length us, event | category | flops | bytes accessed | tf_op | source)
XLA Modules:
  0.0 130.4 jit_solution(12892696508509034527)
XLA Ops:
  0.6 5.1 %collective-permute-start.1 = (bf16[256,1280]{1,0:T(8,128)(2,1)}, bf16[256,1280]{1,0:T(8,128)(2,1)S(1)}, u32[]{:S(2)}, u32[]{:S(2)}) collective-permute-start(bf16[256,1280]{1,0:T(8,128)(2,1)} %refs_2_.3), channel_id=1, source_target_pairs={{4,0},{5,1},{6,2},{7,3},{8,4},{9,5},{10,6},{11,7},{12,8},{13,9},{1... | collective-permute-start | bytes 1966088 | tf_op jit(solution)/shard_map/ppermute | solution.py:25
  5.7 1.3 collective-permute-start.4
  7.0 4.6 %collective-permute-start.5 = (bf16[256,1280]{1,0:T(8,128)(2,1)}, bf16[256,1280]{1,0:T(8,128)(2,1)S(1)}, u32[]{:S(2)}, u32[]{:S(2)}) collective-permute-start(bf16[256,1280]{1,0:T(8,128)(2,1)} %refs_3_.1), channel_id=1, source_target_pairs={{0,2},{1,3},{4,6},{5,7},{8,10},{9,11},{12,14},{13,15},{16,18},{17,... | collective-permute-start | bytes 1966088 | tf_op jit(solution)/shard_map/ppermute | solution.py:25
  11.7 8.4 %collective-permute-done.1.refs_2_.refs_6_ = bf16[256,1280]{1,0:T(8,128)(2,1)S(1)} collective-permute-done((bf16[256,1280]{1,0:T(8,128)(2,1)}, bf16[256,1280]{1,0:T(8,128)(2,1)S(1)}, u32[]{:S(2)}, u32[]{:S(2)}) %collective-permute-start.1) | collective-permute-done | bytes 655392 | tf_op jit(solution)/shard_map/ppermute | solution.py:25
  20.0 4.0 %collective-permute-done.4.refs_3_.refs_12_ = bf16[256,1280]{1,0:T(8,128)(2,1)S(1)} collective-permute-done((bf16[256,1280]{1,0:T(8,128)(2,1)}, bf16[256,1280]{1,0:T(8,128)(2,1)S(1)}, u32[]{:S(2)}, u32[]{:S(2)}) %collective-permute-start.4) | collective-permute-done | bytes 655392 | tf_op jit(solution)/shard_map/ppermute | solution.py:25
  24.0 1.3 %collective-permute-done.5.refs_6_ = bf16[256,1280]{1,0:T(8,128)(2,1)S(1)} collective-permute-done((bf16[256,1280]{1,0:T(8,128)(2,1)}, bf16[256,1280]{1,0:T(8,128)(2,1)S(1)}, u32[]{:S(2)}, u32[]{:S(2)}) %collective-permute-start.5) | collective-permute-done | bytes 655392 | tf_op jit(solution)/shard_map/ppermute | solution.py:25
  25.3 2.3 %collective-permute-start.2 = (bf16[256,1280]{1,0:T(8,128)(2,1)S(1)}, bf16[256,1280]{1,0:T(8,128)(2,1)S(1)}, u32[]{:S(2)}, u32[]{:S(2)}) collective-permute-start(bf16[256,1280]{1,0:T(8,128)(2,1)S(1)} %collective-permute-done.1.refs_2_.refs_6_), channel_id=1, source_target_pairs={{4,0},{5,1},{6,2},{8,4},{9,5},{10,6},{12,8},{13,9},{14,10},{0,12},... | collective-permute-start | bytes 1966088 | tf_op jit(solution)/shard_map/ppermute | solution.py:25
  27.7 2.4 %collective-permute-start.6 = (bf16[256,1280]{1,0:T(8,128)(2,1)S(1)}, bf16[256,1280]{1,0:T(8,128)(2,1)S(1)}, u32[]{:S(2)}, u32[]{:S(2)}) collective-permute-start(bf16[256,1280]{1,0:T(8,128)(2,1)S(1)} %collective-permute-done.1.refs_2_.refs_6_), channel_id=1, source_target_pairs={{0,2},{1,3},{2,0},{3,1},{4,6},{5,7},{6,4},{7,5},{8,10},{9,11},{10,... | collective-permute-start | bytes 1966088 | tf_op jit(solution)/shard_map/ppermute | solution.py:25
  30.1 1.6 %collective-permute-start.12 = (bf16[256,1280]{1,0:T(8,128)(2,1)}, bf16[256,1280]{1,0:T(8,128)(2,1)}, u32[]{:S(2)}, u32[]{:S(2)}) collective-permute-start(bf16[256,1280]{1,0:T(8,128)(2,1)} %refs_3_.1), channel_id=1, source_target_pairs={{12,0},{13,1},{14,2},{15,3},{0,4},{1,5},{2,6},{3,7},{4,8},{5,9},{6... | collective-permute-start | bytes 1966088 | tf_op jit(solution)/shard_map/ppermute | solution.py:25
  31.7 1.3 collective-permute-start
  33.0 23.2 %collective-permute-done.2 = bf16[256,1280]{1,0:T(8,128)(2,1)S(1)} collective-permute-done((bf16[256,1280]{1,0:T(8,128)(2,1)S(1)}, bf16[256,1280]{1,0:T(8,128)(2,1)S(1)}, u32[]{:S(2)}, u32[]{:S(2)}) %collective-permute-start.2) | collective-permute-done | bytes 655392 | tf_op jit(solution)/shard_map/ppermute | solution.py:25
  56.3 1.3 %collective-permute-start.7 = (bf16[256,1280]{1,0:T(8,128)(2,1)S(1)}, bf16[256,1280]{1,0:T(8,128)(2,1)S(1)}, u32[]{:S(2)}, u32[]{:S(2)}) collective-permute-start(bf16[256,1280]{1,0:T(8,128)(2,1)S(1)} %collective-permute-done.2), channel_id=1, source_target_pairs={{0,2},{1,3},{4,6},{5,7},{8,10},{9,11},{12,14},{13,15},{16,18},{17,... | collective-permute-start | bytes 1966088 | tf_op jit(solution)/shard_map/ppermute | solution.py:25
  57.7 1.5 %collective-permute-start.17 = (bf16[256,1280]{1,0:T(8,128)(2,1)}, bf16[256,1280]{1,0:T(8,128)(2,1)}, u32[]{:S(2)}, u32[]{:S(2)}) collective-permute-start(bf16[256,1280]{1,0:T(8,128)(2,1)} %collective-permute-done.12.refs_4_), channel_id=1, source_target_pairs={{13,1},{14,2},{15,3},{1,5},{2,6},{3,7},{5,9},{6,10},{7,11},{9,13},... | collective-permute-start | bytes 1966088 | tf_op jit(solution)/shard_map/ppermute | solution.py:25
  59.7 7.6 %collective-permute-done.7.refs_4_.refs_13_ = bf16[256,1280]{1,0:T(8,128)(2,1)S(1)} collective-permute-done((bf16[256,1280]{1,0:T(8,128)(2,1)S(1)}, bf16[256,1280]{1,0:T(8,128)(2,1)S(1)}, u32[]{:S(2)}, u32[]{:S(2)}) %collective-permute-start.7) | collective-permute-done | bytes 655392 | tf_op jit(solution)/shard_map/ppermute | solution.py:25
  67.3 1.9 %collective-permute-start.8 = (bf16[256,1280]{1,0:T(8,128)(2,1)S(1)}, bf16[256,1280]{1,0:T(8,128)(2,1)S(1)}, u32[]{:S(2)}, u32[]{:S(2)}) collective-permute-start(bf16[256,1280]{1,0:T(8,128)(2,1)S(1)} %collective-permute-done.4.refs_3_.refs_12_), channel_id=1, source_target_pairs={{0,1},{1,0},{4,5},{5,4},{8,9},{9,8},{12,13},{13,12},{16,17},{17,16... | collective-permute-start | bytes 1966088 | tf_op jit(solution)/shard_map/ppermute | solution.py:25
  69.2 5.2 %collective-permute-done.14.refs_6_ = bf16[256,1280]{1,0:T(8,128)(2,1)} collective-permute-done((bf16[256,1280]{1,0:T(8,128)(2,1)}, bf16[256,1280]{1,0:T(8,128)(2,1)}, u32[]{:S(2)}, u32[]{:S(2)}) %collective-permute-start.14) | collective-permute-done | bytes 655392 | tf_op jit(solution)/shard_map/ppermute | solution.py:25
  74.4 1.3 %collective-permute-start.3 = (bf16[256,1280]{1,0:T(8,128)(2,1)S(1)}, bf16[256,1280]{1,0:T(8,128)(2,1)S(1)}, u32[]{:S(2)}, u32[]{:S(2)}) collective-permute-start(bf16[256,1280]{1,0:T(8,128)(2,1)S(1)} %collective-permute-done.2), channel_id=1, source_target_pairs={{0,1},{2,3},{4,5},{6,7},{8,9},{10,11},{12,13},{14,15},{16,17},{18,... | collective-permute-start | bytes 1966088 | tf_op jit(solution)/shard_map/ppermute | solution.py:25
  76.6 1.3 collective-permute-start.19
  79.0 1.1 copy-done.15
  80.1 1.4 %near_scores.1 = (f32[5,256,256]{2,1,0:T(8,128)S(1)}, f32[256,128]{1,0:T(8,128)S(1)}, f32[256,128]{1,0:T(8,128)S(1)}, f32[24,256]{1,0:T(8,128)S(1)}) custom-call(bf16[256,1280]{1,0:T(8,128)(2,1)S(1)} %copy-done.15, bf16[256,1280]{1,0:T(8,128)(2,1)S(1)} %copy-done, bf16[256,1280]{1,0:T(8,128)(2,1)S(1)} %collective-permute-done.1.refs_2_.refs_6_, ...), custom_call_target="tpu_custom_call" | custom-call | flops 838860800 | bytes 4000000 | tf_op jit(solution)/shard_map/near_scores/pallas_call | solution.py:217
  82.7 2.6 %far_scores.1 = (f32[3,256,256]{2,1,0:T(8,128)S(1)}, f32[256,128]{1,0:T(8,128)S(1)}, f32[16,24,256]{2,1,0:T(8,128)}, f32[24,256]{1,0:T(8,128)}) custom-call(bf16[256,1280]{1,0:T(8,128)(2,1)S(1)} %copy-done.15, bf16[256,1280]{1,0:T(8,128)(2,1)S(1)} %collective-permute-done.refs_1_.refs_10_, bf16[256,1280]{1,0:T(8,128)(2,1)S(1)} %collective-permute-done.3.refs_2_.refs_11_, ...), custom_call_target="tpu_custom_call" | custom-call | flops 503316480 | bytes 2400000 | tf_op jit(solution)/shard_map/far_scores/pallas_call | solution.py:217
  86.3 9.1 %all-to-all-start = ((f32[16,24,256]{2,1,0:T(8,128)}), f32[16,24,256]{2,1,0:T(8,128)S(1)}, u32[]{:S(2)}, u32[]{:S(2)}) async-start(f32[16,24,256]{2,1,0:T(8,128)} %get-tuple-element.22), calls=%async_computation | async-start | bytes 786432 | tf_op jit(solution)/shard_map/all_to_all | solution.py:282
  95.8 2.9 %collective-permute-start.16 = (bf16[256,1280]{1,0:T(8,128)(2,1)S(1)}, bf16[256,1280]{1,0:T(8,128)(2,1)}, u32[]{:S(2)}, u32[]{:S(2)}) collective-permute-start(bf16[256,1280]{1,0:T(8,128)(2,1)S(1)} %copy-done.16), channel_id=1, source_target_pairs={{0,1},{2,3},{4,5},{6,7},{8,9},{10,11},{12,13},{14,15},{16,17},{18,... | collective-permute-start | bytes 1966088 | tf_op jit(solution)/shard_map/ppermute | solution.py:25
  98.7 1.5 %collective-permute-start.20 = (bf16[256,1280]{1,0:T(8,128)(2,1)}, bf16[256,1280]{1,0:T(8,128)(2,1)}, u32[]{:S(2)}, u32[]{:S(2)}) collective-permute-start(bf16[256,1280]{1,0:T(8,128)(2,1)} %copy-done.20), channel_id=1, source_target_pairs={{2,3},{3,2},{6,7},{7,6},{10,11},{11,10},{14,15},{15,14},{18,19},{1... | collective-permute-start | bytes 1966088 | tf_op jit(solution)/shard_map/ppermute | solution.py:25
  100.2 1.3 collective-permute-start.18
  101.5 3.9 %collective-permute-start.21 = (bf16[256,1280]{1,0:T(8,128)(2,1)}, bf16[256,1280]{1,0:T(8,128)(2,1)}, u32[]{:S(2)}, u32[]{:S(2)}) collective-permute-start(bf16[256,1280]{1,0:T(8,128)(2,1)} %collective-permute-done.19.refs_7_), channel_id=1, source_target_pairs={{0,1},{1,0},{4,5},{5,4},{8,9},{9,8},{12,13},{13,12},{16,17},{17,16... | collective-permute-start | bytes 1966088 | tf_op jit(solution)/shard_map/ppermute | solution.py:25
  105.5 2.0 %all-to-all-done.refs_2_.refs_1_ = f32[16,24,256]{2,1,0:T(8,128)S(1)} async-done(((f32[16,24,256]{2,1,0:T(8,128)}), f32[16,24,256]{2,1,0:T(8,128)S(1)}, u32[]{:S(2)}, u32[]{:S(2)}) %all-to-all-start) | async-done | bytes 393248 | tf_op jit(solution)/shard_map/all_to_all | solution.py:282
  107.6 1.1 copy-done.5
  108.7 1.1 copy-done.8
  113.0 5.6 %image_products.1 = f32[256,1280]{1,0:T(8,128)} custom-call(s32[256,1]{1,0:T(8,128)S(1)} %copy.5.refs_0_, f32[256,128]{1,0:T(8,128)S(1)} %get-tuple-element.21.refs_1_, f32[16,24,256]{2,1,0:T(8,128)S(1)} %all-to-all-done.refs_2_.refs_1_, f32[5,256,256]{2,1,0:T(8,128)} %copy-done.17, f32[3,256,256]{2,1,0:T(8,128)} %copy-done.19, ...), custom_call_target="tpu_custom_call" | custom-call | flops 1342177280 | bytes 6400000 | tf_op jit(solution)/shard_map/image_products/pallas_call | solution.py:217
  118.6 4.2 %near_text_products.1 = (f32[256,1280]{1,0:T(8,128)S(1)}, f32[256,128]{1,0:T(8,128)S(1)}) custom-call(s32[1,256]{1,0:T(1,128)S(1)} %bitcast.3, f32[16,24,256]{2,1,0:T(8,128)S(1)} %all-to-all-done.refs_2_.refs_1_, bf16[256,1280]{1,0:T(8,128)(2,1)S(1)} %copy-done.1, bf16[256,1280]{1,0:T(8,128)(2,1)S(1)} %copy-done.16, ...), custom_call_target="tpu_custom_call" | custom-call | flops 1677721600 | bytes 8000000 | tf_op jit(solution)/shard_map/near_text_products/pallas_call | solution.py:217
  123.9 6.5 %far_text_products.1 = f32[256,1280]{1,0:T(8,128)} custom-call(f32[256,128]{1,0:T(8,128)S(1)} %get-tuple-element.27.refs_0_, f32[16,24,256]{2,1,0:T(8,128)S(1)} %all-to-all-done.refs_2_.refs_1_, bf16[256,1280]{1,0:T(8,128)(2,1)S(1)} %copy-done.1, f32[256,1280]{1,0:T(8,128)} %copy-done.18, bf16[256,1280]{1,0:T(8,128)(2,1)} %collective-permute-done.16.refs_4_, ...), custom_call_target="tpu_custom_call" | custom-call | flops 1006632960 | bytes 4800000 | tf_op jit(solution)/shard_map/far_text_products/pallas_call | solution.py:217
  (66 shorter events, 9.4 us)
Async XLA Ops:
  0.6 19.4 %collective-permute-start.1 = (bf16[256,1280]{1,0:T(8,128)(2,1)}, bf16[256,1280]{1,0:T(8,128)(2,1)S(1)}, u32[]{:S(2)}, u32[]{:S(2)}) collective-permute-start(bf16[256,1280]{1,0:T(8,128)(2,1)} %refs_2_.3), channel_id=1, source_target_pairs={{4,0},{5,1},{6,2},{7,3},{8,4},{9,5},{10,6},{11,7},{12,8},{13,9},{1... | collective-permute-start | bytes 1966088 | tf_op jit(solution)/shard_map/ppermute | solution.py:25
  5.7 18.3 %collective-permute-start.4 = (bf16[256,1280]{1,0:T(8,128)(2,1)}, bf16[256,1280]{1,0:T(8,128)(2,1)S(1)}, u32[]{:S(2)}, u32[]{:S(2)}) collective-permute-start(bf16[256,1280]{1,0:T(8,128)(2,1)} %refs_2_.3), channel_id=1, source_target_pairs={{2,0},{3,1},{6,4},{7,5},{10,8},{11,9},{14,12},{15,13},{18,16},{19,... | collective-permute-start | bytes 1966088 | tf_op jit(solution)/shard_map/ppermute | solution.py:25
  7.0 18.3 %collective-permute-start.5 = (bf16[256,1280]{1,0:T(8,128)(2,1)}, bf16[256,1280]{1,0:T(8,128)(2,1)S(1)}, u32[]{:S(2)}, u32[]{:S(2)}) collective-permute-start(bf16[256,1280]{1,0:T(8,128)(2,1)} %refs_3_.1), channel_id=1, source_target_pairs={{0,2},{1,3},{4,6},{5,7},{8,10},{9,11},{12,14},{13,15},{16,18},{17,... | collective-permute-start | bytes 1966088 | tf_op jit(solution)/shard_map/ppermute | solution.py:25
  20.0 61.5 %copy-start.7 = (bf16[256,1280]{1,0:T(8,128)(2,1)}, bf16[256,1280]{1,0:T(8,128)(2,1)S(1)}, u32[]{:S(2)}) copy-start(bf16[256,1280]{1,0:T(8,128)(2,1)S(1)} %collective-permute-done.1.refs_2_.refs_6_) | copy-start | bytes 1966084
  25.3 30.9 %collective-permute-start.2 = (bf16[256,1280]{1,0:T(8,128)(2,1)S(1)}, bf16[256,1280]{1,0:T(8,128)(2,1)S(1)}, u32[]{:S(2)}, u32[]{:S(2)}) collective-permute-start(bf16[256,1280]{1,0:T(8,128)(2,1)S(1)} %collective-permute-done.1.refs_2_.refs_6_), channel_id=1, source_target_pairs={{4,0},{5,1},{6,2},{8,4},{9,5},{10,6},{12,8},{13,9},{14,10},{0,12},... | collective-permute-start | bytes 1966088 | tf_op jit(solution)/shard_map/ppermute | solution.py:25
  27.7 28.6 %collective-permute-start.6 = (bf16[256,1280]{1,0:T(8,128)(2,1)S(1)}, bf16[256,1280]{1,0:T(8,128)(2,1)S(1)}, u32[]{:S(2)}, u32[]{:S(2)}) collective-permute-start(bf16[256,1280]{1,0:T(8,128)(2,1)S(1)} %collective-permute-done.1.refs_2_.refs_6_), channel_id=1, source_target_pairs={{0,2},{1,3},{2,0},{3,1},{4,6},{5,7},{6,4},{7,5},{8,10},{9,11},{10,... | collective-permute-start | bytes 1966088 | tf_op jit(solution)/shard_map/ppermute | solution.py:25
  30.1 27.5 %collective-permute-start.12 = (bf16[256,1280]{1,0:T(8,128)(2,1)}, bf16[256,1280]{1,0:T(8,128)(2,1)}, u32[]{:S(2)}, u32[]{:S(2)}) collective-permute-start(bf16[256,1280]{1,0:T(8,128)(2,1)} %refs_3_.1), channel_id=1, source_target_pairs={{12,0},{13,1},{14,2},{15,3},{0,4},{1,5},{2,6},{3,7},{4,8},{5,9},{6... | collective-permute-start | bytes 1966088 | tf_op jit(solution)/shard_map/ppermute | solution.py:25
  31.7 27.5 %collective-permute-start = (bf16[256,1280]{1,0:T(8,128)(2,1)}, bf16[256,1280]{1,0:T(8,128)(2,1)S(1)}, u32[]{:S(2)}, u32[]{:S(2)}) collective-permute-start(bf16[256,1280]{1,0:T(8,128)(2,1)} %refs_2_.3), channel_id=1, source_target_pairs={{1,0},{3,2},{5,4},{7,6},{9,8},{11,10},{13,12},{15,14},{17,16},{19,... | collective-permute-start | bytes 1966088 | tf_op jit(solution)/shard_map/ppermute | solution.py:25
  56.3 25.3 %copy-start.9 = (bf16[256,1280]{1,0:T(8,128)(2,1)}, bf16[256,1280]{1,0:T(8,128)(2,1)S(1)}, u32[]{:S(2)}) copy-start(bf16[256,1280]{1,0:T(8,128)(2,1)S(1)} %collective-permute-done.6.refs_4_.refs_8_) | copy-start | bytes 1966084
  56.3 11.1 %collective-permute-start.7 = (bf16[256,1280]{1,0:T(8,128)(2,1)S(1)}, bf16[256,1280]{1,0:T(8,128)(2,1)S(1)}, u32[]{:S(2)}, u32[]{:S(2)}) collective-permute-start(bf16[256,1280]{1,0:T(8,128)(2,1)S(1)} %collective-permute-done.2), channel_id=1, source_target_pairs={{0,2},{1,3},{4,6},{5,7},{8,10},{9,11},{12,14},{13,15},{16,18},{17,... | collective-permute-start | bytes 1966088 | tf_op jit(solution)/shard_map/ppermute | solution.py:25
  57.6 16.8 %collective-permute-start.14 = (bf16[256,1280]{1,0:T(8,128)(2,1)}, bf16[256,1280]{1,0:T(8,128)(2,1)}, u32[]{:S(2)}, u32[]{:S(2)}) collective-permute-start(bf16[256,1280]{1,0:T(8,128)(2,1)} %collective-permute-done.12.refs_4_), channel_id=1, source_target_pairs={{0,2},{1,3},{2,0},{3,1},{4,6},{5,7},{6,4},{7,5},{8,10},{9,11},{10,... | collective-permute-start | bytes 1966088 | tf_op jit(solution)/shard_map/ppermute | solution.py:25
  57.7 18.1 %collective-permute-start.17 = (bf16[256,1280]{1,0:T(8,128)(2,1)}, bf16[256,1280]{1,0:T(8,128)(2,1)}, u32[]{:S(2)}, u32[]{:S(2)}) collective-permute-start(bf16[256,1280]{1,0:T(8,128)(2,1)} %collective-permute-done.12.refs_4_), channel_id=1, source_target_pairs={{13,1},{14,2},{15,3},{1,5},{2,6},{3,7},{5,9},{6,10},{7,11},{9,13},... | collective-permute-start | bytes 1966088 | tf_op jit(solution)/shard_map/ppermute | solution.py:25
  59.2 17.3 %collective-permute-start.10 = (bf16[256,1280]{1,0:T(8,128)(2,1)S(1)}, bf16[256,1280]{1,0:T(8,128)(2,1)S(1)}, u32[]{:S(2)}, u32[]{:S(2)}) collective-permute-start(bf16[256,1280]{1,0:T(8,128)(2,1)S(1)} %collective-permute-done.1.refs_2_.refs_6_), channel_id=1, source_target_pairs={{0,1},{1,0},{2,3},{3,2},{4,5},{5,4},{6,7},{7,6},{8,9},{9,8},{10,11... | collective-permute-start | bytes 1966088 | tf_op jit(solution)/shard_map/ppermute | solution.py:25
  59.2 17.4 %collective-permute-start.11 = (bf16[256,1280]{1,0:T(8,128)(2,1)S(1)}, bf16[256,1280]{1,0:T(8,128)(2,1)S(1)}, u32[]{:S(2)}, u32[]{:S(2)}) collective-permute-start(bf16[256,1280]{1,0:T(8,128)(2,1)S(1)} %collective-permute-done.6.refs_4_.refs_8_), channel_id=1, source_target_pairs={{0,1},{1,0},{2,3},{3,2},{4,5},{5,4},{6,7},{7,6},{8,9},{9,8},{10,11... | collective-permute-start | bytes 1966088 | tf_op jit(solution)/shard_map/ppermute | solution.py:25
  67.3 15.3 %copy-start.2 = (bf16[256,1280]{1,0:T(8,128)(2,1)}, bf16[256,1280]{1,0:T(8,128)(2,1)S(1)}, u32[]{:S(2)}) copy-start(bf16[256,1280]{1,0:T(8,128)(2,1)S(1)} %collective-permute-done.7.refs_4_.refs_13_) | copy-start | bytes 1966084
  67.3 15.3 %collective-permute-start.8 = (bf16[256,1280]{1,0:T(8,128)(2,1)S(1)}, bf16[256,1280]{1,0:T(8,128)(2,1)S(1)}, u32[]{:S(2)}, u32[]{:S(2)}) collective-permute-start(bf16[256,1280]{1,0:T(8,128)(2,1)S(1)} %collective-permute-done.4.refs_3_.refs_12_), channel_id=1, source_target_pairs={{0,1},{1,0},{4,5},{5,4},{8,9},{9,8},{12,13},{13,12},{16,17},{17,16... | collective-permute-start | bytes 1966088 | tf_op jit(solution)/shard_map/ppermute | solution.py:25
  74.4 8.2 %collective-permute-start.3 = (bf16[256,1280]{1,0:T(8,128)(2,1)S(1)}, bf16[256,1280]{1,0:T(8,128)(2,1)S(1)}, u32[]{:S(2)}, u32[]{:S(2)}) collective-permute-start(bf16[256,1280]{1,0:T(8,128)(2,1)S(1)} %collective-permute-done.2), channel_id=1, source_target_pairs={{0,1},{2,3},{4,5},{6,7},{8,9},{10,11},{12,13},{14,15},{16,17},{18,... | collective-permute-start | bytes 1966088 | tf_op jit(solution)/shard_map/ppermute | solution.py:25
  75.8 6.9 %collective-permute-start.9 = (bf16[256,1280]{1,0:T(8,128)(2,1)S(1)}, bf16[256,1280]{1,0:T(8,128)(2,1)S(1)}, u32[]{:S(2)}, u32[]{:S(2)}) collective-permute-start(bf16[256,1280]{1,0:T(8,128)(2,1)S(1)} %collective-permute-done.7.refs_4_.refs_13_), channel_id=1, source_target_pairs={{2,3},{3,2},{6,7},{7,6},{10,11},{11,10},{14,15},{15,14},{18,19},{1... | collective-permute-start | bytes 1966088 | tf_op jit(solution)/shard_map/ppermute | solution.py:25
  76.5 5.0 %copy-start.11 = (bf16[256,1280]{1,0:T(8,128)(2,1)}, bf16[256,1280]{1,0:T(8,128)(2,1)S(1)}, u32[]{:S(2)}) copy-start(bf16[256,1280]{1,0:T(8,128)(2,1)S(1)} %collective-permute-done.10.refs_3_.refs_7_) | copy-start | bytes 1966084
  76.5 23.7 %collective-permute-start.13 = (bf16[256,1280]{1,0:T(8,128)(2,1)}, bf16[256,1280]{1,0:T(8,128)(2,1)}, u32[]{:S(2)}, u32[]{:S(2)}) collective-permute-start(bf16[256,1280]{1,0:T(8,128)(2,1)} %collective-permute-done.12.refs_4_), channel_id=1, source_target_pairs={{0,1},{1,0},{2,3},{3,2},{4,5},{5,4},{6,7},{7,6},{8,9},{9,8},{10,11... | collective-permute-start | bytes 1966088 | tf_op jit(solution)/shard_map/ppermute | solution.py:25
  76.6 4.9 %copy-start.13 = (bf16[256,1280]{1,0:T(8,128)(2,1)}, bf16[256,1280]{1,0:T(8,128)(2,1)S(1)}, u32[]{:S(2)}) copy-start(bf16[256,1280]{1,0:T(8,128)(2,1)S(1)} %collective-permute-done.11.refs_5_.refs_9_) | copy-start | bytes 1966084
  76.6 24.9 %collective-permute-start.19 = (bf16[256,1280]{1,0:T(8,128)(2,1)}, bf16[256,1280]{1,0:T(8,128)(2,1)}, u32[]{:S(2)}, u32[]{:S(2)}) collective-permute-start(bf16[256,1280]{1,0:T(8,128)(2,1)} %collective-permute-done.17), channel_id=1, source_target_pairs={{2,0},{3,1},{6,4},{7,5},{10,8},{11,9},{14,12},{15,13},{18,16},{19,... | collective-permute-start | bytes 1966088 | tf_op jit(solution)/shard_map/ppermute | solution.py:25
  82.7 13.1 %copy-start.16 = (bf16[256,1280]{1,0:T(8,128)(2,1)S(1)}, bf16[256,1280]{1,0:T(8,128)(2,1)}, u32[]{:S(2)}) copy-start(bf16[256,1280]{1,0:T(8,128)(2,1)} %refs_3_.1) | copy-start | bytes 1966084
  82.7 22.7 %copy-start.22 = (s32[256]{0:T(256)S(1)}, s32[256]{0:T(256)}, u32[]{:S(2)}) copy-start(s32[256]{0:T(256)} %param.5) | copy-start | bytes 3076
  86.3 21.3 %copy-start.1 = (bf16[256,1280]{1,0:T(8,128)(2,1)S(1)}, bf16[256,1280]{1,0:T(8,128)(2,1)}, u32[]{:S(2)}) copy-start(bf16[256,1280]{1,0:T(8,128)(2,1)} %refs_2_.3) | copy-start | bytes 1966084
  86.3 21.3 %all-to-all-start = ((f32[16,24,256]{2,1,0:T(8,128)}), f32[16,24,256]{2,1,0:T(8,128)S(1)}, u32[]{:S(2)}, u32[]{:S(2)}) async-start(f32[16,24,256]{2,1,0:T(8,128)} %get-tuple-element.22), calls=%async_computation | async-start | bytes 786432 | tf_op jit(solution)/shard_map/all_to_all | solution.py:282
  95.4 23.2 %collective-permute-start.15 = (bf16[256,1280]{1,0:T(8,128)(2,1)}, bf16[256,1280]{1,0:T(8,128)(2,1)}, u32[]{:S(2)}, u32[]{:S(2)}) collective-permute-start(bf16[256,1280]{1,0:T(8,128)(2,1)} %collective-permute-done.14.refs_6_), channel_id=1, source_target_pairs={{0,1},{1,0},{2,3},{3,2},{4,5},{5,4},{6,7},{7,6},{8,9},{9,8},{10,11... | collective-permute-start | bytes 1966088 | tf_op jit(solution)/shard_map/ppermute | solution.py:25
  95.8 28.1 %collective-permute-start.16 = (bf16[256,1280]{1,0:T(8,128)(2,1)S(1)}, bf16[256,1280]{1,0:T(8,128)(2,1)}, u32[]{:S(2)}, u32[]{:S(2)}) collective-permute-start(bf16[256,1280]{1,0:T(8,128)(2,1)S(1)} %copy-done.16), channel_id=1, source_target_pairs={{0,1},{2,3},{4,5},{6,7},{8,9},{10,11},{12,13},{14,15},{16,17},{18,... | collective-permute-start | bytes 1966088 | tf_op jit(solution)/shard_map/ppermute | solution.py:25
  98.7 25.2 %collective-permute-start.20 = (bf16[256,1280]{1,0:T(8,128)(2,1)}, bf16[256,1280]{1,0:T(8,128)(2,1)}, u32[]{:S(2)}, u32[]{:S(2)}) collective-permute-start(bf16[256,1280]{1,0:T(8,128)(2,1)} %copy-done.20), channel_id=1, source_target_pairs={{2,3},{3,2},{6,7},{7,6},{10,11},{11,10},{14,15},{15,14},{18,19},{1... | collective-permute-start | bytes 1966088 | tf_op jit(solution)/shard_map/ppermute | solution.py:25
  100.2 23.7 %collective-permute-start.18 = (bf16[256,1280]{1,0:T(8,128)(2,1)}, bf16[256,1280]{1,0:T(8,128)(2,1)}, u32[]{:S(2)}, u32[]{:S(2)}) collective-permute-start(bf16[256,1280]{1,0:T(8,128)(2,1)} %collective-permute-done.17), channel_id=1, source_target_pairs={{3,2},{1,0},{7,6},{5,4},{11,10},{9,8},{15,14},{13,12},{19,18},{17,... | collective-permute-start | bytes 1966088 | tf_op jit(solution)/shard_map/ppermute | solution.py:25
  101.5 22.4 %collective-permute-start.21 = (bf16[256,1280]{1,0:T(8,128)(2,1)}, bf16[256,1280]{1,0:T(8,128)(2,1)}, u32[]{:S(2)}, u32[]{:S(2)}) collective-permute-start(bf16[256,1280]{1,0:T(8,128)(2,1)} %collective-permute-done.19.refs_7_), channel_id=1, source_target_pairs={{0,1},{1,0},{4,5},{5,4},{8,9},{9,8},{12,13},{13,12},{16,17},{17,16... | collective-permute-start | bytes 1966088 | tf_op jit(solution)/shard_map/ppermute | solution.py:25
  118.6 5.3 %copy-start.21 = (bf16[256,1280]{1,0:T(8,128)(2,1)S(1)}, bf16[256,1280]{1,0:T(8,128)(2,1)}, u32[]{:S(2)}) copy-start(bf16[256,1280]{1,0:T(8,128)(2,1)} %copy-done.20) | copy-start | bytes 1966084
  (14 other events, 23.6 us)

commit v3 on v0

v3 whole, which is shorter than its diff:
```python
import jax
import jax.numpy as jnp
from jax import lax
from jax.experimental import pallas as pl
from jax.experimental.pallas import tpu as pltpu
from jax.sharding import PartitionSpec as P

WINDOW = 8
LEVEL = 4
ROW_PLACE = 16
TABLE_ROWS = 24

logit_scale = 100.0
half_scale = 50.0
vmem_bytes = 60 * 1024 * 1024


def send(block, moves):
    count = lax.axis_size("dp")
    route = [
        ((level * LEVEL + a) % count, (level * LEVEL + b) % count)
        for level in range(count // LEVEL)
        for a, b in moves
    ]
    return lax.ppermute(block, "dp", route)


def after(block, *earlier):
    return lax.optimization_barrier((block, *earlier))[0]


def scores_of(rows, cols):
    products = lax.dot_general(
        rows, cols, (((1,), (1,)), ((), ())), preferred_element_type=jnp.float32
    )
    return logit_scale * products


def as_column(row):
    return jnp.transpose(jnp.broadcast_to(row, (128, row.shape[1])))[:, :1]


def as_row(column):
    return jnp.transpose(jnp.broadcast_to(column, (column.shape[0], 128)))[:1, :]


class Loads:
    def __init__(self, sems):
        self.sems = sems
        self.used = 0

    def slot(self, ref):
        self.used += 1
        return ref, self.sems.at[self.used - 1]

    def load(self, dest, *cases):
        slot = self.slot(dest)
        for chosen, ref in cases:
            if chosen is None:
                pltpu.make_async_copy(ref, *slot).start()
            else:
                pl.when(chosen)(pltpu.make_async_copy(ref, *slot).start)
        return slot

    def store(self, source, dest):
        copy = pltpu.make_async_copy(source, *self.slot(dest))
        copy.start()
        return copy


def arrived(*slots):
    for ref, sem in slots:
        pltpu.make_async_copy(ref, ref, sem).wait()


def part(ref, slot, rows):
    return ref.at[pl.ds(slot * rows, rows)]


def place():
    here = lax.axis_index("dp")
    rank = here % LEVEL
    return here, rank // 2, rank % 2


def put_stats(scores, stat_ref, offset):
    peak = jnp.max(scores, axis=0, keepdims=True)
    total = jnp.sum(jnp.exp(scores - peak), axis=0, keepdims=True)
    stat_ref[pl.ds(offset, 1), :] = peak
    stat_ref[pl.ds(WINDOW + offset, 1), :] = total


def row_stats(scores):
    peak = jnp.max(jnp.max(scores, axis=0), axis=1, keepdims=True)
    total = jnp.sum(jnp.sum(jnp.exp(scores - peak[None]), axis=0), axis=1, keepdims=True)
    return peak, total


def merge(peak_a, total_a, peak_b, total_b):
    peak = jnp.maximum(peak_a, peak_b)
    return peak, total_a * jnp.exp(peak_a - peak) + total_b * jnp.exp(peak_b - peak)


def near_scores(image, sibling, text, t1, t1_y, *refs):
    rows_ref, stat_ref, held, own_ref, sib_ref, sems = refs
    rows = image.shape[0]
    _, q, c = place()
    loads = Loads(sems)
    blocks = [part(held, slot, rows) for slot in range(5)]
    arrived(
        *[
            loads.load(block, (None, ref))
            for block, ref in zip(blocks, (image, sibling, text, t1, t1_y))
        ]
    )
    own, sib, *texts = blocks
    offsets = (0, 4, 6 - 4 * q)
    sib_offsets = (3 + 2 * c, 5 - 4 * q + 2 * c)
    stat_ref[...] = jnp.zeros_like(stat_ref)
    for slot, block in enumerate(texts):
        own_ref[slot] = scores_of(own[...], block[...])
        if slot > 0:
            sib_ref[slot - 1] = scores_of(sib[...], block[...])
    for slot in range(3):
        put_stats(own_ref[slot], stat_ref, offsets[slot])
    for slot in range(2):
        put_stats(sib_ref[slot], stat_ref, sib_offsets[slot])
    lane = lax.broadcasted_iota(jnp.int32, rows_ref.shape, 1)
    columns = (*row_stats(own_ref[...]), *row_stats(sib_ref[...]))
    packed = jnp.zeros(rows_ref.shape, jnp.float32)
    for index, column in enumerate(columns):
        packed = jnp.where(lane == index, column, packed)
    rows_ref[...] = packed


def far_scores(near_rows, near_stat, image, sibling, text, t2_lo, t2_hi, own_y, t2_y, *refs):
    message_ref, held, own_ref, sib_ref, stat_ref, sems = refs
    rows = image.shape[0]
    _, q, c = place()
    loads = Loads(sems)
    own, sib, block, last = [part(held, slot, rows) for slot in range(4)]
    arrived(
        loads.load(own, (None, image)),
        loads.load(block, (q == 0, own_y), (q == 1, t2_y)),
        loads.load(sib, (None, sibling)),
        loads.load(last, *last_cases(q, c == 0, t2_lo, t2_hi, text)),
    )
    stat_ref[...] = near_stat[...]
    offset = 2 + 4 * q
    own_ref[0] = scores_of(own[...], block[...])
    sib_ref[0] = scores_of(sib[...], block[...])
    sib_ref[1] = scores_of(sib[...], last[...])
    put_stats(own_ref[0], stat_ref, offset)
    put_stats(sib_ref[0], stat_ref, offset + 2 * c - 1)
    put_stats(sib_ref[1], stat_ref, 7 - 6 * c)
    columns = [near_rows[:, index:index + 1] for index in range(4)]
    own_rows = merge(*columns[:2], *row_stats(own_ref[...]))
    sib_rows = merge(*columns[2:], *row_stats(sib_ref[...]))
    for index, column in enumerate((*own_rows, *sib_rows)):
        stat_ref[pl.ds(ROW_PLACE + index, 1), :] = as_row(column)
    for index in range(message_ref.shape[0]):
        message_ref[index] = stat_ref[...]


def last_cases(q, moved, low_block, high_block, own):
    return (
        (jnp.logical_and(moved, q == 0), low_block),
        (jnp.logical_and(moved, q == 1), high_block),
        (jnp.logical_not(moved), own),
    )


def sibling_of(index):
    return index + 1 - 2 * (index % 2)


def column_norm(table, text):
    count = table.shape[0]
    text = text % count
    peaks = []
    totals = []
    for offset in range(WINDOW):
        source = (text - offset + count) % count
        if offset % 2:
            source = sibling_of(source)
        peaks.append(table[source, pl.ds(offset, 1), :])
        totals.append(table[source, pl.ds(WINDOW + offset, 1), :])
    peaks = jnp.concatenate(peaks, axis=0)
    totals = jnp.concatenate(totals, axis=0)
    peak = jnp.max(peaks, axis=0, keepdims=True)
    total = jnp.sum(totals * jnp.exp(peaks - peak), axis=0, keepdims=True)
    return peak + jnp.log(total)


def row_norms(table, images):
    count = table.shape[0]
    images = [(image + count) % count for image in images]

    def rows_of(sources, place):
        return jnp.concatenate([table[s, pl.ds(place, 1), :] for s in sources], axis=0)

    others = [sibling_of(image) for image in images]
    peak, total = merge(
        rows_of(images, ROW_PLACE),
        rows_of(images, ROW_PLACE + 1),
        rows_of(others, ROW_PLACE + 2),
        rows_of(others, ROW_PLACE + 3),
    )
    return peak + jnp.log(total)


def mixed(scores, self_norm, other_norm, positive=None):
    combined = jnp.exp(scores - self_norm) + jnp.exp(scores - other_norm)
    if positive is not None:
        combined = combined - 2.0 * positive.astype(jnp.float32)
    return combined.astype(jnp.bfloat16)


def wide_products(loads, mixing, blocks, out_ref, out):
    width = blocks.shape[1]
    step = 256 if width % 256 == 0 else width
    stores = []
    for start in range(0, width, step):
        cols = slice(start, start + step)
        product = jnp.dot(mixing[...], blocks[:, cols], preferred_element_type=jnp.float32)
        out_ref[:, cols] = half_scale * product
        stores.append(loads.store(out_ref.at[:, cols], out.at[:, cols]))
    return stores


def tile_products(loads, own, sib, blocks, norms, others, positive, mixes, out_refs, outs):
    rows = own.shape[0]
    for slot in range(4):
        block = part(blocks, slot, rows)
        mixes[0][:, slot * rows:(slot + 1) * rows] = mixed(
            scores_of(own[...], block[...]), norms[0], others[slot],
            positive if slot == 0 else None,
        )
    stores = wide_products(
        loads, mixes[0], blocks.at[pl.ds(0, 4 * rows)], out_refs[0], outs[0]
    )
    for slot in range(1, 5):
        block = part(blocks, slot, rows)
        mixes[1][:, (slot - 1) * rows:slot * rows] = mixed(
            scores_of(sib[...], block[...]), norms[1], others[slot]
        )
    stores += wide_products(
        loads, mixes[1], blocks.at[pl.ds(rows, 4 * rows)], out_refs[1], outs[1]
    )
    for store in stores:
        store.wait()


def image_products(label_ref, table_in, image, sibling, *refs):
    text, t1, t1_y, t2_lo, t2_hi, own_y, t2_y = refs[:7]
    outs, (held, blocks, table, *more) = refs[7:9], refs[9:]
    mixes, out_refs, sems = more[:2], more[2:4], more[4]
    rows = image.shape[0]
    here, q, c = place()
    loads = Loads(sems)
    own, sib = part(held, 0, rows), part(held, 1, rows)
    cases = (
        ((None, text),),
        ((None, t1),),
        ((None, t1_y),),
        ((q == 0, own_y), (q == 1, t2_y)),
        last_cases(q, c == 0, t2_lo, t2_hi, text),
    )
    arrived(
        loads.load(table, (None, table_in)),
        loads.load(own, (None, image)),
        loads.load(sib, (None, sibling)),
        *[loads.load(part(blocks, slot, rows), *case) for slot, case in enumerate(cases)],
    )
    sib_place = sibling_of(here)
    norms = row_norms(table, [here, sib_place])
    norms = [as_column(norms[:1]), as_column(norms[1:])]
    offsets = (0, 4, 6 - 4 * q, 2 + 4 * q, 8 - 8 * c)
    others = [column_norm(table, here + offset) for offset in offsets]
    lane = lax.broadcasted_iota(jnp.int32, (rows, rows), 1)
    match = as_column(label_ref[...].astype(jnp.float32)).astype(jnp.int32)
    positive = match == here * rows + lane
    tile_products(loads, own, sib, blocks, norms, others, positive, mixes, out_refs, outs)


def text_products(label_ref, table_in, text, sibling, *refs):
    image, i1_lo, i1_hi, i1_up, i1_down, i2_lo, i2_hi, own_y, i2_y = refs[:9]
    outs, (held, blocks, table, *more) = refs[9:11], refs[11:]
    mixes, out_refs, sems = more[:2], more[2:4], more[4]
    rows = text.shape[0]
    here, q, c = place()
    loads = Loads(sems)
    own, sib = part(held, 0, rows), part(held, 1, rows)
    cases = (
        ((None, image),),
        ((q == 0, i1_lo), (q == 1, i1_hi)),
        ((q == 0, i1_up), (q == 1, i1_down)),
        ((q == 0, i2_y), (q == 1, own_y)),
        last_cases(q, c == 1, i2_lo, i2_hi, image),
    )
    arrived(
        loads.load(table, (None, table_in)),
        loads.load(own, (None, text)),
        loads.load(sib, (None, sibling)),
        *[loads.load(part(blocks, slot, rows), *case) for slot, case in enumerate(cases)],
    )
    norms = [as_column(column_norm(table, index)) for index in (here, sibling_of(here))]
    offsets = (0, 4, 2 + 4 * q, 6 - 4 * q, 8 * c)
    others = row_norms(table, [here - offset for offset in offsets])
    others = [others[slot:slot + 1] for slot in range(5)]
    sublane = lax.broadcasted_iota(jnp.int32, (rows, rows), 0)
    positive = label_ref[...] == here * rows + sublane
    tile_products(loads, own, sib, blocks, norms, others, positive, mixes, out_refs, outs)


def kernel_call(body, outs, scratch, copies, whole, blocks):
    spaces = [pltpu.VMEM] * len(whole) + [pl.ANY] * len(blocks)
    return pl.pallas_call(
        body,
        out_shape=[out for _, out in outs],
        in_specs=[pl.BlockSpec(memory_space=space) for space in spaces],
        out_specs=[pl.BlockSpec(memory_space=space) for space, _ in outs],
        scratch_shapes=[*scratch, pltpu.SemaphoreType.DMA((copies,))],
        compiler_params=pltpu.CompilerParams(vmem_limit_bytes=vmem_bytes),
        cost_estimate=pl.CostEstimate(
            flops=1000000, bytes_accessed=100000, transcendentals=1000
        ),
        name=body.__name__,
    )(*whole, *blocks)


cores = [(0, 1), (1, 0), (2, 3), (3, 2)]
across = [(0, 2), (1, 3), (2, 0), (3, 1)]


def shards(image, text, labels):
    rows, width = image.shape
    count = lax.axis_size("dp")
    f32 = jnp.float32

    def struct(*shape):
        return jax.ShapeDtypeStruct(shape, f32)

    def square(blocks):
        return pltpu.VMEM((blocks, rows, rows), f32)

    def wide(blocks, dtype=jnp.bfloat16):
        return pltpu.VMEM((blocks * rows, width), dtype)

    t1 = send(text, [(r + 4, r) for r in range(4)])
    own_y_t = send(text, [(2, 0), (3, 1)])
    own_y_i = send(image, [(0, 2), (1, 3)])
    image_c = send(image, cores)
    text_c = send(text, cores)
    t2_lo = send(t1, [(4, 0), (5, 1)])
    t2_hi = send(t1, [(6, 2)])
    t1_y = send(after(t1, own_y_t, own_y_i, image_c), across)
    i1_hi = send(after(image, t1), [(-2, 2), (-1, 3)])
    t2_y = send(after(t2_lo, t1_y), [(0, 2), (1, 3)])
    i1_lo = send(after(image, t2_lo), [(-4, 0), (-3, 1)])
    near_rows, near_stat = kernel_call(
        near_scores,
        [(pltpu.VMEM, struct(rows, 128)), (pltpu.VMEM, struct(TABLE_ROWS, rows))],
        [wide(5), square(3), square(2)], 5, [], [image, image_c, text, t1, t1_y],
    )
    i1_up = send(i1_hi, [(2, 0), (3, 1)])
    i2_hi = send(i1_hi, [(-2, 2), (-1, 3)])
    near_rows = after(near_rows, i1_lo, i1_up)
    (message,) = kernel_call(
        far_scores, [(pltpu.VMEM, struct(count, TABLE_ROWS, rows))],
        [wide(4), square(1), square(2), pltpu.VMEM((TABLE_ROWS, rows), f32)], 4,
        [near_rows, near_stat], [image, image_c, text, t2_lo, t2_hi, own_y_t, t2_y],
    )
    i1_down = send(i1_lo, [(0, 2), (1, 3)])
    i2_lo = send(i1_lo, [(-3, 1)])
    i2_y = send(i2_hi, [(2, 0), (3, 1)])
    table = lax.all_to_all(after(message, i2_lo, i2_hi), "dp", 0, 0, tiled=True)

    def tile_call(body, whole, blocks):
        mix = pltpu.VMEM((rows, 4 * rows), jnp.bfloat16)
        return kernel_call(
            body, [(pl.ANY, struct(rows, width))] * 2,
            [wide(2), wide(5), pltpu.VMEM((count, TABLE_ROWS, rows), f32), mix, mix,
             wide(1, f32), wide(1, f32)], 24, whole, blocks,
        )

    label_row = labels[None, :]
    own_image, sib_image = tile_call(
        image_products, [label_row],
        [table, image, image_c, text, t1, t1_y, t2_lo, t2_hi, own_y_t, t2_y],
    )
    table = after(table, own_image)
    own_text, sib_text = tile_call(
        text_products, [label_row],
        [table, text, text_c, image, i1_lo, i1_hi, i1_up, i1_down, i2_lo, i2_hi, own_y_i, i2_y],
    )
    return own_image + send(sib_image, cores), own_text + send(sib_text, cores)


def solution(mesh):
    return jax.shard_map(
        shards,
        mesh=mesh,
        in_specs=(P(("groups", "dp"), None), P(("groups", "dp"), None), P(("groups", "dp"))),
        out_specs=(P(("groups", "dp"), None), P(("groups", "dp"), None)),
        check_vma=False,
    )
```

time: 169 us -> 113 us (0.67)
  blocking collectives: 43.7 us -> 0 us
  Pallas kernels: 0 us -> 24.1 us
  starting transfers between devices: 65.4 us -> 46.4 us
  matrix products: 18.8 us -> 0 us
    all_gather x2 -> x0, blocking collectives: 43.7 us -> none  [the longest x1 26.1 us: shards(): lax.all_gather(col_norm, 'dp', axis=0, tiled=True)]
    pallas_call x0 -> x4, Pallas kernels: none -> 24.1 us  [kernel_call(): pl.pallas_call(body, out_shape=[out for _, out in outs], in_specs=[pl.Blo...]
    ppermute x14 -> x18, starting transfers between devices: 65.4 us -> 42.5 us  [send(): return lax.ppermute(block, 'dp', route)]
    dot_general x31 -> x0, matrix products: 18.8 us -> none  [the longest x15 8.64 us: similarity(): lax.dot_general(row_side, col_side, (((1,), (1,)), ((), ())), preferred_e...]
    ppermute x14 -> x18, waiting for transfers between devices: 37.8 us -> 30.9 us  [send(): return lax.ppermute(block, 'dp', route)]
    all_to_all x0 -> x1, waiting for transfers between devices: none -> 6.01 us  [shards(): table = lax.all_to_all(after(message, i2_lo, i2_hi), 'dp', 0, 0, tiled=True)]
    all_to_all x0 -> x1, starting transfers between devices: none -> 3.9 us  [shards(): table = lax.all_to_all(after(message, i2_lo, i2_hi), 'dp', 0, 0, tiled=True)]
    add x3 -> x2, other arithmetic: 0.07 us -> 2.39 us  [the longest x1 1.19 us: shards(): own_image + send(sib_image, cores)]
  transfers between devices with their start and end apart: 14 -> 19, of which waited for: 8 -> 9; matrix products, arithmetic and copies ran while one was open for 5% -> 1% of each run, Pallas kernels for 0% -> 21%
where the time goes in v3:
time: 113 us; the launch traced here: 112 us
  starting transfers between devices  46.4 us (41%)
  waiting for transfers between devices  36.9 us (33%)
  Pallas kernels  24.1 us (21%)
  other arithmetic  2.39 us (2%)
  local copies, waits for them, and re-layouts  1.66 us (1%)
    ppermute x18, starting transfers between devices, send(): return lax.ppermute(block, 'dp', route)  42.5 us
    ppermute x18, waiting for transfers between devices, send(): return lax.ppermute(block, 'dp', route)  30.9 us
    pallas_call x4, Pallas kernels, kernel_call(): pl.pallas_call(body, out_shape=[out for _, out in outs], in_specs=[pl.Blo...  24.1 us
    all_to_all x1, waiting for transfers between devices, shards(): table = lax.all_to_all(after(message, i2_lo, i2_hi), 'dp', 0, 0, tiled=True)  6.01 us
    all_to_all x1, starting transfers between devices, shards(): table = lax.all_to_all(after(message, i2_lo, i2_hi), 'dp', 0, 0, tiled=True)  3.9 us
  transfers between devices with their start and end apart: 19, of which 9 were waited for; matrix products, arithmetic and copies ran while one was open for 1% of the time, Pallas kernels for 21%

profile of v3, /device:TPU:0, one launch (start us, length us, event | category | flops | bytes accessed | tf_op | source)
XLA Modules:
  0.0 112.3 jit_solution(3940453958067991596)
XLA Ops:
  0.6 5.1 %collective-permute-start.1 = (bf16[256,1280]{1,0:T(8,128)(2,1)}, bf16[256,1280]{1,0:T(8,128)(2,1)}, u32[]{:S(2)}, u32[]{:S(2)}) collective-permute-start(bf16[256,1280]{1,0:T(8,128)(2,1)} %text.5), channel_id=1, source_target_pairs={{4,0},{5,1},{6,2},{7,3},{8,4},{9,5},{10,6},{11,7},{12,8},{13,9},{1... | collective-permute-start | bytes 1966088 | tf_op jit(solution)/shard_map/ppermute | solution.py:25
  5.7 1.3 %collective-permute-start.2 = (bf16[256,1280]{1,0:T(8,128)(2,1)}, bf16[256,1280]{1,0:T(8,128)(2,1)S(1)}, u32[]{:S(2)}, u32[]{:S(2)}) collective-permute-start(bf16[256,1280]{1,0:T(8,128)(2,1)} %text.5), channel_id=1, source_target_pairs={{2,0},{3,1},{6,4},{7,5},{10,8},{11,9},{14,12},{15,13},{18,16},{19,... | collective-permute-start | bytes 1966088 | tf_op jit(solution)/shard_map/ppermute | solution.py:25
  7.0 4.6 %collective-permute-start.3 = (bf16[256,1280]{1,0:T(8,128)(2,1)}, bf16[256,1280]{1,0:T(8,128)(2,1)S(1)}, u32[]{:S(2)}, u32[]{:S(2)}) collective-permute-start(bf16[256,1280]{1,0:T(8,128)(2,1)} %refs_0_.3), channel_id=1, source_target_pairs={{0,2},{1,3},{4,6},{5,7},{8,10},{9,11},{12,14},{13,15},{16,18},{17,... | collective-permute-start | bytes 1966088 | tf_op jit(solution)/shard_map/ppermute | solution.py:25
  11.7 8.4 %collective-permute-done.1.t1.refs_1_ = bf16[256,1280]{1,0:T(8,128)(2,1)} collective-permute-done((bf16[256,1280]{1,0:T(8,128)(2,1)}, bf16[256,1280]{1,0:T(8,128)(2,1)}, u32[]{:S(2)}, u32[]{:S(2)}) %collective-permute-start.1) | collective-permute-done | bytes 655392 | tf_op jit(solution)/shard_map/ppermute | solution.py:25
  20.0 6.2 %collective-permute-start.5 = (bf16[256,1280]{1,0:T(8,128)(2,1)}, bf16[256,1280]{1,0:T(8,128)(2,1)S(1)}, u32[]{:S(2)}, u32[]{:S(2)}) collective-permute-start(bf16[256,1280]{1,0:T(8,128)(2,1)} %collective-permute-done.1.t1.refs_1_), channel_id=1, source_target_pairs={{4,0},{5,1},{8,4},{9,5},{12,8},{13,9},{0,12},{1,13},{20,16},{21,17... | collective-permute-start | bytes 1966088 | tf_op jit(solution)/shard_map/ppermute | solution.py:25
  26.3 0.7 collective-permute-start.7
  27.0 3.7 %collective-permute-start.4 = (bf16[256,1280]{1,0:T(8,128)(2,1)}, bf16[256,1280]{1,0:T(8,128)(2,1)}, u32[]{:S(2)}, u32[]{:S(2)}) collective-permute-start(bf16[256,1280]{1,0:T(8,128)(2,1)} %collective-permute-done.1.t1.refs_1_), channel_id=1, source_target_pairs={{0,2},{1,3},{2,0},{3,1},{4,6},{5,7},{6,4},{7,5},{8,10},{9,11},{10,... | collective-permute-start | bytes 1966088 | tf_op jit(solution)/shard_map/ppermute | solution.py:25
  30.7 9.0 %collective-permute-done.5.t2_lo.refs_3_ = bf16[256,1280]{1,0:T(8,128)(2,1)S(1)} collective-permute-done((bf16[256,1280]{1,0:T(8,128)(2,1)}, bf16[256,1280]{1,0:T(8,128)(2,1)S(1)}, u32[]{:S(2)}, u32[]{:S(2)}) %collective-permute-start.5) | collective-permute-done | bytes 655392 | tf_op jit(solution)/shard_map/ppermute | solution.py:25
  39.6 1.9 %collective-permute-start.6 = (bf16[256,1280]{1,0:T(8,128)(2,1)}, bf16[256,1280]{1,0:T(8,128)(2,1)}, u32[]{:S(2)}, u32[]{:S(2)}) collective-permute-start(bf16[256,1280]{1,0:T(8,128)(2,1)} %refs_0_.3), channel_id=1, source_target_pairs={{12,0},{13,1},{0,4},{1,5},{4,8},{5,9},{8,12},{9,13},{28,16},{29,17... | collective-permute-start | bytes 1966088 | tf_op jit(solution)/shard_map/ppermute | solution.py:25
  41.6 0.7 collective-permute-start.9
  42.3 1.3 %collective-permute-start.8 = (bf16[256,1280]{1,0:T(8,128)(2,1)S(1)}, bf16[256,1280]{1,0:T(8,128)(2,1)}, u32[]{:S(2)}, u32[]{:S(2)}) collective-permute-start(bf16[256,1280]{1,0:T(8,128)(2,1)S(1)} %collective-permute-done.7.refs_2_), channel_id=1, source_target_pairs={{2,0},{3,1},{6,4},{7,5},{10,8},{11,9},{14,12},{15,13},{18,16},{19,... | collective-permute-start | bytes 1966088 | tf_op jit(solution)/shard_map/ppermute | solution.py:25
  43.6 1.7 %collective-permute-done.4.t1_y.refs_2_ = bf16[256,1280]{1,0:T(8,128)(2,1)} collective-permute-done((bf16[256,1280]{1,0:T(8,128)(2,1)}, bf16[256,1280]{1,0:T(8,128)(2,1)}, u32[]{:S(2)}, u32[]{:S(2)}) %collective-permute-start.4) | collective-permute-done | bytes 655392 | tf_op jit(solution)/shard_map/ppermute | solution.py:25
  45.3 7.6 %collective-permute-start.10 = (bf16[256,1280]{1,0:T(8,128)(2,1)S(1)}, bf16[256,1280]{1,0:T(8,128)(2,1)S(1)}, u32[]{:S(2)}, u32[]{:S(2)}) collective-permute-start(bf16[256,1280]{1,0:T(8,128)(2,1)S(1)} %collective-permute-done.5.t2_lo.refs_3_), channel_id=1, source_target_pairs={{0,2},{1,3},{4,6},{5,7},{8,10},{9,11},{12,14},{13,15},{16,18},{17,... | collective-permute-start | bytes 1966088 | tf_op jit(solution)/shard_map/ppermute | solution.py:25
  52.9 1.5 %collective-permute-start.12 = (bf16[256,1280]{1,0:T(8,128)(2,1)S(1)}, bf16[256,1280]{1,0:T(8,128)(2,1)}, u32[]{:S(2)}, u32[]{:S(2)}) collective-permute-start(bf16[256,1280]{1,0:T(8,128)(2,1)S(1)} %collective-permute-done.7.refs_2_), channel_id=1, source_target_pairs={{14,2},{15,3},{2,6},{3,7},{6,10},{7,11},{10,14},{11,15},{30,18},{3... | collective-permute-start | bytes 1966088 | tf_op jit(solution)/shard_map/ppermute | solution.py:25
  54.4 4.6 %collective-permute-done.6.refs_1_ = bf16[256,1280]{1,0:T(8,128)(2,1)} collective-permute-done((bf16[256,1280]{1,0:T(8,128)(2,1)}, bf16[256,1280]{1,0:T(8,128)(2,1)}, u32[]{:S(2)}, u32[]{:S(2)}) %collective-permute-start.6) | collective-permute-done | bytes 655392 | tf_op jit(solution)/shard_map/ppermute | solution.py:25
  59.0 1.5 %collective-permute-start.11 = (bf16[256,1280]{1,0:T(8,128)(2,1)}, bf16[256,1280]{1,0:T(8,128)(2,1)}, u32[]{:S(2)}, u32[]{:S(2)}) collective-permute-start(bf16[256,1280]{1,0:T(8,128)(2,1)} %collective-permute-done.6.refs_1_), channel_id=1, source_target_pairs={{13,1},{1,5},{5,9},{9,13},{29,17},{17,21},{21,25},{25,29}} | collective-permute-start | bytes 1966088 | tf_op jit(solution)/shard_map/ppermute | solution.py:25
  60.5 4.1 %near_scores.1 = (f32[256,128]{1,0:T(8,128)}, f32[24,256]{1,0:T(8,128)}) custom-call(bf16[256,1280]{1,0:T(8,128)(2,1)} %refs_0_.3, bf16[256,1280]{1,0:T(8,128)(2,1)} %copy-done.1, bf16[256,1280]{1,0:T(8,128)(2,1)} %text.5, bf16[256,1280]{1,0:T(8,128)(2,1)} %collective-permute-done.1.t1.refs_1_, bf16[256,1280]{1,0:T(8,128)(2,1)} %collective-permute-done.4.t1_y.refs_2_), custom_call_target="tpu_custom_call" | custom-call | flops 1000000 | bytes 100000 | tf_op jit(solution)/shard_map/near_scores/pallas_call | solution.py:318
  64.6 0.7 collective-permute-done.10.t2_y.refs_6_
  65.3 0.9 copy-done.6
  66.2 5.5 %far_scores.1 = f32[16,24,256]{2,1,0:T(8,128)} custom-call(f32[256,128]{1,0:T(8,128)} %get-tuple-element.19.near_rows, f32[24,256]{1,0:T(8,128)} %get-tuple-element.20.near_stat, bf16[256,1280]{1,0:T(8,128)(2,1)} %refs_0_.3, bf16[256,1280]{1,0:T(8,128)(2,1)} %copy-done.1, bf16[256,1280]{1,0:T(8,128)(2,1)} %text.5, bf16[256,1280]{1,0:T(8,128)(2,1)} %copy-done.4, ...), custom_call_target="tpu_custom_call" | custom-call | flops 1000000 | bytes 100000 | tf_op jit(solution)/shard_map/far_scores/pallas_call | solution.py:318
  71.8 3.9 %all-to-all-start = ((f32[16,24,256]{2,1,0:T(8,128)}), f32[16,24,256]{2,1,0:T(8,128)S(1)}, u32[]{:S(2)}, u32[]{:S(2)}) async-start(f32[16,24,256]{2,1,0:T(8,128)} %far_scores.1), calls=%async_computation | async-start | bytes 786432 | tf_op jit(solution)/shard_map/all_to_all | solution.py:377
  76.2 4.5 %collective-permute-start.15 = (bf16[256,1280]{1,0:T(8,128)(2,1)}, bf16[256,1280]{1,0:T(8,128)(2,1)}, u32[]{:S(2)}, u32[]{:S(2)}) collective-permute-start(bf16[256,1280]{1,0:T(8,128)(2,1)} %collective-permute-done.6.refs_1_), channel_id=1, source_target_pairs={{0,2},{1,3},{4,6},{5,7},{8,10},{9,11},{12,14},{13,15},{16,18},{17,... | collective-permute-start | bytes 1966088 | tf_op jit(solution)/shard_map/ppermute | solution.py:25
  80.6 1.3 %collective-permute-start.16 = (bf16[256,1280]{1,0:T(8,128)(2,1)}, bf16[256,1280]{1,0:T(8,128)(2,1)}, u32[]{:S(2)}, u32[]{:S(2)}) collective-permute-start(bf16[256,1280]{1,0:T(8,128)(2,1)} %collective-permute-done.12.refs_6_), channel_id=1, source_target_pairs={{2,0},{3,1},{6,4},{7,5},{10,8},{11,9},{14,12},{15,13},{18,16},{19,... | collective-permute-start | bytes 1966088 | tf_op jit(solution)/shard_map/ppermute | solution.py:25
  81.9 6.0 %all-to-all-done.table_in = f32[16,24,256]{2,1,0:T(8,128)S(1)} async-done(((f32[16,24,256]{2,1,0:T(8,128)}), f32[16,24,256]{2,1,0:T(8,128)S(1)}, u32[]{:S(2)}, u32[]{:S(2)}) %all-to-all-start) | async-done | bytes 393248 | tf_op jit(solution)/shard_map/all_to_all | solution.py:377
  87.9 0.8 copy-done.2
  88.7 7.3 %image_products.1 = (f32[256,1280]{1,0:T(8,128)}, f32[256,1280]{1,0:T(8,128)}) custom-call(s32[1,256]{1,0:T(1,128)} %bitcast.1, f32[16,24,256]{2,1,0:T(8,128)} %copy-done.2, bf16[256,1280]{1,0:T(8,128)(2,1)} %refs_0_.3, bf16[256,1280]{1,0:T(8,128)(2,1)} %copy-done.1, bf16[256,1280]{1,0:T(8,128)(2,1)} %text.5, ...), custom_call_target="tpu_custom_call" | custom-call | flops 1000000 | bytes 100000 | tf_op jit(solution)/shard_map/image_products/pallas_call | solution.py:318
  96.1 0.8 collective-permute-done.15.refs_4_
  96.9 3.7 %collective-permute-done.16.refs_8_ = bf16[256,1280]{1,0:T(8,128)(2,1)} collective-permute-done((bf16[256,1280]{1,0:T(8,128)(2,1)}, bf16[256,1280]{1,0:T(8,128)(2,1)}, u32[]{:S(2)}, u32[]{:S(2)}) %collective-permute-start.16) | collective-permute-done | bytes 655392 | tf_op jit(solution)/shard_map/ppermute | solution.py:25
  100.5 7.3 %text_products.1 = (f32[256,1280]{1,0:T(8,128)}, f32[256,1280]{1,0:T(8,128)}) custom-call(s32[1,256]{1,0:T(1,128)} %bitcast.2, f32[16,24,256]{2,1,0:T(8,128)} %copy-done.2, bf16[256,1280]{1,0:T(8,128)(2,1)} %text.5, bf16[256,1280]{1,0:T(8,128)(2,1)} %collective-permute-done.14.sibling, bf16[256,1280]{1,0:T(8,128)(2,1)} %refs_0_.3, ...), custom_call_target="tpu_custom_call" | custom-call | flops 1000000 | bytes 100000 | tf_op jit(solution)/shard_map/text_products/pallas_call | solution.py:318
  107.9 1.2 %add.6 = f32[256,1280]{1,0:T(8,128)} add(f32[256,1280]{1,0:T(8,128)S(1)} %copy-done.7, f32[256,1280]{1,0:T(8,128)S(1)} %collective-permute-done.13) | non-fusion elementwise | flops 327680 | bytes 3932160 | tf_op jit(solution)/shard_map/add | solution.py:397
  109.1 2.0 %collective-permute-done.17 = f32[256,1280]{1,0:T(8,128)S(1)} collective-permute-done((f32[256,1280]{1,0:T(8,128)}, f32[256,1280]{1,0:T(8,128)S(1)}, u32[]{:S(2)}, u32[]{:S(2)}) %collective-permute-start.17) | collective-permute-done | bytes 1310752 | tf_op jit(solution)/shard_map/ppermute | solution.py:25
  111.1 1.2 %add.7 = f32[256,1280]{1,0:T(8,128)} add(f32[256,1280]{1,0:T(8,128)S(1)} %copy-done.8, f32[256,1280]{1,0:T(8,128)S(1)} %collective-permute-done.17) | non-fusion elementwise | flops 327680 | bytes 3932160 | tf_op jit(solution)/shard_map/add | solution.py:397
  (34 shorter events, 0.8 us)
Async XLA Ops:
  0.6 19.4 %collective-permute-start.1 = (bf16[256,1280]{1,0:T(8,128)(2,1)}, bf16[256,1280]{1,0:T(8,128)(2,1)}, u32[]{:S(2)}, u32[]{:S(2)}) collective-permute-start(bf16[256,1280]{1,0:T(8,128)(2,1)} %text.5), channel_id=1, source_target_pairs={{4,0},{5,1},{6,2},{7,3},{8,4},{9,5},{10,6},{11,7},{12,8},{13,9},{1... | collective-permute-start | bytes 1966088 | tf_op jit(solution)/shard_map/ppermute | solution.py:25
  5.7 20.5 %collective-permute-start = (bf16[256,1280]{1,0:T(8,128)(2,1)}, bf16[256,1280]{1,0:T(8,128)(2,1)S(1)}, u32[]{:S(2)}, u32[]{:S(2)}) collective-permute-start(bf16[256,1280]{1,0:T(8,128)(2,1)} %refs_0_.3), channel_id=1, source_target_pairs={{0,1},{1,0},{2,3},{3,2},{4,5},{5,4},{6,7},{7,6},{8,9},{9,8},{10,11... | collective-permute-start | bytes 1966088 | tf_op jit(solution)/shard_map/ppermute | solution.py:25
  5.7 20.5 %collective-permute-start.2 = (bf16[256,1280]{1,0:T(8,128)(2,1)}, bf16[256,1280]{1,0:T(8,128)(2,1)S(1)}, u32[]{:S(2)}, u32[]{:S(2)}) collective-permute-start(bf16[256,1280]{1,0:T(8,128)(2,1)} %text.5), channel_id=1, source_target_pairs={{2,0},{3,1},{6,4},{7,5},{10,8},{11,9},{14,12},{15,13},{18,16},{19,... | collective-permute-start | bytes 1966088 | tf_op jit(solution)/shard_map/ppermute | solution.py:25
  7.0 19.3 %collective-permute-start.3 = (bf16[256,1280]{1,0:T(8,128)(2,1)}, bf16[256,1280]{1,0:T(8,128)(2,1)S(1)}, u32[]{:S(2)}, u32[]{:S(2)}) collective-permute-start(bf16[256,1280]{1,0:T(8,128)(2,1)} %refs_0_.3), channel_id=1, source_target_pairs={{0,2},{1,3},{4,6},{5,7},{8,10},{9,11},{12,14},{13,15},{16,18},{17,... | collective-permute-start | bytes 1966088 | tf_op jit(solution)/shard_map/ppermute | solution.py:25
  20.0 19.6 %collective-permute-start.5 = (bf16[256,1280]{1,0:T(8,128)(2,1)}, bf16[256,1280]{1,0:T(8,128)(2,1)S(1)}, u32[]{:S(2)}, u32[]{:S(2)}) collective-permute-start(bf16[256,1280]{1,0:T(8,128)(2,1)} %collective-permute-done.1.t1.refs_1_), channel_id=1, source_target_pairs={{4,0},{5,1},{8,4},{9,5},{12,8},{13,9},{0,12},{1,13},{20,16},{21,17... | collective-permute-start | bytes 1966088 | tf_op jit(solution)/shard_map/ppermute | solution.py:25
  26.2 34.2 %copy-start.1 = (bf16[256,1280]{1,0:T(8,128)(2,1)}, bf16[256,1280]{1,0:T(8,128)(2,1)S(1)}, u32[]{:S(2)}) copy-start(bf16[256,1280]{1,0:T(8,128)(2,1)S(1)} %collective-permute-done.sibling) | copy-start | bytes 1966084
  26.3 38.3 %copy-start.3 = (bf16[256,1280]{1,0:T(8,128)(2,1)}, bf16[256,1280]{1,0:T(8,128)(2,1)S(1)}, u32[]{:S(2)}) copy-start(bf16[256,1280]{1,0:T(8,128)(2,1)S(1)} %collective-permute-done.2.own_y.refs_5_) | copy-start | bytes 1966084
  26.3 17.3 %copy-start.9 = (bf16[256,1280]{1,0:T(8,128)(2,1)}, bf16[256,1280]{1,0:T(8,128)(2,1)S(1)}, u32[]{:S(2)}) copy-start(bf16[256,1280]{1,0:T(8,128)(2,1)S(1)} %collective-permute-done.3.refs_7_) | copy-start | bytes 1966084
  26.3 16.0 %collective-permute-start.7 = (bf16[256,1280]{1,0:T(8,128)(2,1)}, bf16[256,1280]{1,0:T(8,128)(2,1)S(1)}, u32[]{:S(2)}, u32[]{:S(2)}) collective-permute-start(bf16[256,1280]{1,0:T(8,128)(2,1)} %refs_0_.3), channel_id=1, source_target_pairs={{14,2},{15,3},{2,6},{3,7},{6,10},{7,11},{10,14},{11,15},{30,18},{3... | collective-permute-start | bytes 1966088 | tf_op jit(solution)/shard_map/ppermute | solution.py:25
  27.0 18.3 %collective-permute-start.4 = (bf16[256,1280]{1,0:T(8,128)(2,1)}, bf16[256,1280]{1,0:T(8,128)(2,1)}, u32[]{:S(2)}, u32[]{:S(2)}) collective-permute-start(bf16[256,1280]{1,0:T(8,128)(2,1)} %collective-permute-done.1.t1.refs_1_), channel_id=1, source_target_pairs={{0,2},{1,3},{2,0},{3,1},{4,6},{5,7},{6,4},{7,5},{8,10},{9,11},{10,... | collective-permute-start | bytes 1966088 | tf_op jit(solution)/shard_map/ppermute | solution.py:25
  39.6 24.9 %copy-start.4 = (bf16[256,1280]{1,0:T(8,128)(2,1)}, bf16[256,1280]{1,0:T(8,128)(2,1)S(1)}, u32[]{:S(2)}) copy-start(bf16[256,1280]{1,0:T(8,128)(2,1)S(1)} %collective-permute-done.5.t2_lo.refs_3_) | copy-start | bytes 1966084
  39.6 19.3 %collective-permute-start.6 = (bf16[256,1280]{1,0:T(8,128)(2,1)}, bf16[256,1280]{1,0:T(8,128)(2,1)}, u32[]{:S(2)}, u32[]{:S(2)}) collective-permute-start(bf16[256,1280]{1,0:T(8,128)(2,1)} %refs_0_.3), channel_id=1, source_target_pairs={{12,0},{13,1},{0,4},{1,5},{4,8},{5,9},{8,12},{9,13},{28,16},{29,17... | collective-permute-start | bytes 1966088 | tf_op jit(solution)/shard_map/ppermute | solution.py:25
  41.6 23.0 %collective-permute-start.9 = (bf16[256,1280]{1,0:T(8,128)(2,1)}, bf16[256,1280]{1,0:T(8,128)(2,1)S(1)}, u32[]{:S(2)}, u32[]{:S(2)}) collective-permute-start(bf16[256,1280]{1,0:T(8,128)(2,1)} %collective-permute-done.1.t1.refs_1_), channel_id=1, source_target_pairs={{6,2},{10,6},{14,10},{2,14},{22,18},{26,22},{30,26},{18,30}} | collective-permute-start | bytes 1966088 | tf_op jit(solution)/shard_map/ppermute | solution.py:25
  42.3 22.3 %copy-start.10 = (bf16[256,1280]{1,0:T(8,128)(2,1)}, bf16[256,1280]{1,0:T(8,128)(2,1)S(1)}, u32[]{:S(2)}) copy-start(bf16[256,1280]{1,0:T(8,128)(2,1)S(1)} %collective-permute-done.7.refs_2_) | copy-start | bytes 1966084
  42.3 22.3 %collective-permute-start.8 = (bf16[256,1280]{1,0:T(8,128)(2,1)S(1)}, bf16[256,1280]{1,0:T(8,128)(2,1)}, u32[]{:S(2)}, u32[]{:S(2)}) collective-permute-start(bf16[256,1280]{1,0:T(8,128)(2,1)S(1)} %collective-permute-done.7.refs_2_), channel_id=1, source_target_pairs={{2,0},{3,1},{6,4},{7,5},{10,8},{11,9},{14,12},{15,13},{18,16},{19,... | collective-permute-start | bytes 1966088 | tf_op jit(solution)/shard_map/ppermute | solution.py:25
  45.3 20.0 %collective-permute-start.10 = (bf16[256,1280]{1,0:T(8,128)(2,1)S(1)}, bf16[256,1280]{1,0:T(8,128)(2,1)S(1)}, u32[]{:S(2)}, u32[]{:S(2)}) collective-permute-start(bf16[256,1280]{1,0:T(8,128)(2,1)S(1)} %collective-permute-done.5.t2_lo.refs_3_), channel_id=1, source_target_pairs={{0,2},{1,3},{4,6},{5,7},{8,10},{9,11},{12,14},{13,15},{16,18},{17,... | collective-permute-start | bytes 1966088 | tf_op jit(solution)/shard_map/ppermute | solution.py:25
  52.9 18.9 %collective-permute-start.12 = (bf16[256,1280]{1,0:T(8,128)(2,1)S(1)}, bf16[256,1280]{1,0:T(8,128)(2,1)}, u32[]{:S(2)}, u32[]{:S(2)}) collective-permute-start(bf16[256,1280]{1,0:T(8,128)(2,1)S(1)} %collective-permute-done.7.refs_2_), channel_id=1, source_target_pairs={{14,2},{15,3},{2,6},{3,7},{6,10},{7,11},{10,14},{11,15},{30,18},{3... | collective-permute-start | bytes 1966088 | tf_op jit(solution)/shard_map/ppermute | solution.py:25
  59.0 12.8 %collective-permute-start.11 = (bf16[256,1280]{1,0:T(8,128)(2,1)}, bf16[256,1280]{1,0:T(8,128)(2,1)}, u32[]{:S(2)}, u32[]{:S(2)}) collective-permute-start(bf16[256,1280]{1,0:T(8,128)(2,1)} %collective-permute-done.6.refs_1_), channel_id=1, source_target_pairs={{13,1},{1,5},{5,9},{9,13},{29,17},{17,21},{21,25},{25,29}} | collective-permute-start | bytes 1966088 | tf_op jit(solution)/shard_map/ppermute | solution.py:25
  64.6 1.6 %copy-start.5 = (bf16[256,1280]{1,0:T(8,128)(2,1)}, bf16[256,1280]{1,0:T(8,128)(2,1)S(1)}, u32[]{:S(2)}) copy-start(bf16[256,1280]{1,0:T(8,128)(2,1)S(1)} %collective-permute-done.9.t2_hi.refs_4_) | copy-start | bytes 1966084
  65.3 0.9 copy-start.6
  66.2 9.5 %copy-start = (bf16[256,1280]{1,0:T(8,128)(2,1)S(1)}, bf16[256,1280]{1,0:T(8,128)(2,1)}, u32[]{:S(2)}) copy-start(bf16[256,1280]{1,0:T(8,128)(2,1)} %text.5) | copy-start | bytes 1966084
  71.8 16.1 %all-to-all-start = ((f32[16,24,256]{2,1,0:T(8,128)}), f32[16,24,256]{2,1,0:T(8,128)S(1)}, u32[]{:S(2)}, u32[]{:S(2)}) async-start(f32[16,24,256]{2,1,0:T(8,128)} %far_scores.1), calls=%async_computation | async-start | bytes 786432 | tf_op jit(solution)/shard_map/all_to_all | solution.py:377
  75.7 20.4 %collective-permute-start.14 = (bf16[256,1280]{1,0:T(8,128)(2,1)S(1)}, bf16[256,1280]{1,0:T(8,128)(2,1)}, u32[]{:S(2)}, u32[]{:S(2)}) collective-permute-start(bf16[256,1280]{1,0:T(8,128)(2,1)S(1)} %copy-done), channel_id=1, source_target_pairs={{0,1},{1,0},{2,3},{3,2},{4,5},{5,4},{6,7},{7,6},{8,9},{9,8},{10,11... | collective-permute-start | bytes 1966088 | tf_op jit(solution)/shard_map/ppermute | solution.py:25
  76.2 20.7 %collective-permute-start.15 = (bf16[256,1280]{1,0:T(8,128)(2,1)}, bf16[256,1280]{1,0:T(8,128)(2,1)}, u32[]{:S(2)}, u32[]{:S(2)}) collective-permute-start(bf16[256,1280]{1,0:T(8,128)(2,1)} %collective-permute-done.6.refs_1_), channel_id=1, source_target_pairs={{0,2},{1,3},{4,6},{5,7},{8,10},{9,11},{12,14},{13,15},{16,18},{17,... | collective-permute-start | bytes 1966088 | tf_op jit(solution)/shard_map/ppermute | solution.py:25
  80.6 19.9 %collective-permute-start.16 = (bf16[256,1280]{1,0:T(8,128)(2,1)}, bf16[256,1280]{1,0:T(8,128)(2,1)}, u32[]{:S(2)}, u32[]{:S(2)}) collective-permute-start(bf16[256,1280]{1,0:T(8,128)(2,1)} %collective-permute-done.12.refs_6_), channel_id=1, source_target_pairs={{2,0},{3,1},{6,4},{7,5},{10,8},{11,9},{14,12},{15,13},{18,16},{19,... | collective-permute-start | bytes 1966088 | tf_op jit(solution)/shard_map/ppermute | solution.py:25
  87.9 0.8 copy-start.2
  95.9 12.0 %collective-permute-start.13 = (f32[256,1280]{1,0:T(8,128)}, f32[256,1280]{1,0:T(8,128)S(1)}, u32[]{:S(2)}, u32[]{:S(2)}) collective-permute-start(f32[256,1280]{1,0:T(8,128)} %get-tuple-element.24), channel_id=1, source_target_pairs={{0,1},{1,0},{2,3},{3,2},{4,5},{5,4},{6,7},{7,6},{8,9},{9,8},{10,11... | collective-permute-start | bytes 3932168 | tf_op jit(solution)/shard_map/ppermute | solution.py:25
  96.1 11.8 %copy-start.7 = (f32[256,1280]{1,0:T(8,128)S(1)}, f32[256,1280]{1,0:T(8,128)}, u32[]{:S(2)}) copy-start(f32[256,1280]{1,0:T(8,128)} %get-tuple-element.23) | copy-start | bytes 3932164
  107.8 3.3 %copy-start.8 = (f32[256,1280]{1,0:T(8,128)S(1)}, f32[256,1280]{1,0:T(8,128)}, u32[]{:S(2)}) copy-start(f32[256,1280]{1,0:T(8,128)} %get-tuple-element.26) | copy-start | bytes 3932164
  107.8 3.3 %collective-permute-start.17 = (f32[256,1280]{1,0:T(8,128)}, f32[256,1280]{1,0:T(8,128)S(1)}, u32[]{:S(2)}, u32[]{:S(2)}) collective-permute-start(f32[256,1280]{1,0:T(8,128)} %get-tuple-element.27), channel_id=1, source_target_pairs={{0,1},{1,0},{2,3},{3,2},{4,5},{5,4},{6,7},{7,6},{8,9},{9,8},{10,11... | collective-permute-start | bytes 3932168 | tf_op jit(solution)/shard_map/ppermute | solution.py:25

commit v4 on v3

--- a/solution.py
+++ b/solution.py
@@ -56,10 +56,11 @@
     def load(self, dest, *cases):
         slot = self.slot(dest)
         for chosen, ref in cases:
+            copy = pltpu.make_async_copy(ref, *slot)
             if chosen is None:
-                pltpu.make_async_copy(ref, *slot).start()
+                copy.start()
             else:
-                pl.when(chosen)(pltpu.make_async_copy(ref, *slot).start)
+                pl.when(chosen)(copy.start)
         return slot
 
     def store(self, source, dest):
@@ -223,7 +224,7 @@
     for start in range(0, width, step):
         cols = slice(start, start + step)
         product = jnp.dot(mixing[...], blocks[:, cols], preferred_element_type=jnp.float32)
-        out_ref[:, cols] = half_scale * product
+        out_ref[:, cols] = (half_scale * product).astype(out_ref.dtype)
         stores.append(loads.store(out_ref.at[:, cols], out.at[:, cols]))
     return stores
 
@@ -284,8 +285,8 @@
 
 
 def text_products(label_ref, table_in, text, sibling, *refs):
-    image, i1_lo, i1_hi, i1_up, i1_down, i2_lo, i2_hi, own_y, i2_y = refs[:9]
-    outs, (held, blocks, table, *more) = refs[9:11], refs[11:]
+    image, i1_lo, i1_hi, middle, last, i2_lo, i2_hi, own_y = refs[:8]
+    outs, (held, blocks, table, *more) = refs[8:10], refs[10:]
     mixes, out_refs, sems = more[:2], more[2:4], more[4]
     rows = text.shape[0]
     here, q, c = place()
@@ -294,8 +295,8 @@
     cases = (
         ((None, image),),
         ((q == 0, i1_lo), (q == 1, i1_hi)),
-        ((q == 0, i1_up), (q == 1, i1_down)),
-        ((q == 0, i2_y), (q == 1, own_y)),
+        ((q == 0, middle), (q == 1, last)),
+        ((q == 0, last), (q == 1, own_y)),
         last_cases(q, c == 1, i2_lo, i2_hi, image),
     )
     arrived(
@@ -337,6 +338,7 @@
     rows, width = image.shape
     count = lax.axis_size("dp")
     f32 = jnp.float32
+    low = (lax.axis_index("dp") % LEVEL) < 2
 
     def struct(*shape):
         return jax.ShapeDtypeStruct(shape, f32)
@@ -348,32 +350,30 @@
         return pltpu.VMEM((blocks * rows, width), dtype)
 
     t1 = send(text, [(r + 4, r) for r in range(4)])
-    own_y_t = send(text, [(2, 0), (3, 1)])
-    own_y_i = send(image, [(0, 2), (1, 3)])
+    own_y = send(jnp.where(low, image, text), across)
     image_c = send(image, cores)
     text_c = send(text, cores)
     t2_lo = send(t1, [(4, 0), (5, 1)])
     t2_hi = send(t1, [(6, 2)])
-    t1_y = send(after(t1, own_y_t, own_y_i, image_c), across)
+    t1_y = send(after(t1, own_y), across)
     i1_hi = send(after(image, t1), [(-2, 2), (-1, 3)])
-    t2_y = send(after(t2_lo, t1_y), [(0, 2), (1, 3)])
     i1_lo = send(after(image, t2_lo), [(-4, 0), (-3, 1)])
+    ready = lax.optimization_barrier((t2_lo, i1_hi, t1_y))
+    middle = send(jnp.where(low, ready[0], ready[1]), across)
+
     near_rows, near_stat = kernel_call(
         near_scores,
         [(pltpu.VMEM, struct(rows, 128)), (pltpu.VMEM, struct(TABLE_ROWS, rows))],
         [wide(5), square(3), square(2)], 5, [], [image, image_c, text, t1, t1_y],
     )
-    i1_up = send(i1_hi, [(2, 0), (3, 1)])
-    i2_hi = send(i1_hi, [(-2, 2), (-1, 3)])
-    near_rows = after(near_rows, i1_lo, i1_up)
     (message,) = kernel_call(
         far_scores, [(pltpu.VMEM, struct(count, TABLE_ROWS, rows))],
         [wide(4), square(1), square(2), pltpu.VMEM((TABLE_ROWS, rows), f32)], 4,
-        [near_rows, near_stat], [image, image_c, text, t2_lo, t2_hi, own_y_t, t2_y],
-    )
-    i1_down = send(i1_lo, [(0, 2), (1, 3)])
-    i2_lo = send(i1_lo, [(-3, 1)])
-    i2_y = send(i2_hi, [(2, 0), (3, 1)])
+        [near_rows, near_stat], [image, image_c, text, t2_lo, t2_hi, own_y, middle],
+    )
+    i2_hi = send(i1_hi, [(-2, 2), (-1, 3)])
+    i2_lo = send(after(i1_lo, near_stat), [(-3, 1)])
+    last = send(jnp.where(low, i1_lo, i2_hi), across)
     table = lax.all_to_all(after(message, i2_lo, i2_hi), "dp", 0, 0, tiled=True)
 
     def tile_call(body, whole, blocks):
@@ -387,12 +387,12 @@
     label_row = labels[None, :]
     own_image, sib_image = tile_call(
         image_products, [label_row],
-        [table, image, image_c, text, t1, t1_y, t2_lo, t2_hi, own_y_t, t2_y],
-    )
-    table = after(table, own_image)
+        [table, image, image_c, text, t1, t1_y, t2_lo, t2_hi, own_y, middle],
+    )
     own_text, sib_text = tile_call(
         text_products, [label_row],
-        [table, text, text_c, image, i1_lo, i1_hi, i1_up, i1_down, i2_lo, i2_hi, own_y_i, i2_y],
+        [after(table, own_image), text, text_c, image, i1_lo, i1_hi, middle, last, i2_lo, i2_hi,
+         own_y],
     )
     return own_image + send(sib_image, cores), own_text + send(sib_text, cores)
 

time: 113 us -> 107 us (0.947)
  starting transfers between devices: 46.4 us -> 31.5 us
  other arithmetic: 2.39 us -> 7.87 us
  waiting for transfers between devices: 36.9 us -> 38.8 us
  local copies, waits for them, and re-layouts: 1.66 us -> 3.36 us
    ppermute x18 -> x15, starting transfers between devices: 42.5 us -> 27.8 us  [send(): return lax.ppermute(block, 'dp', route)]
    select_n x0 -> x3, other arithmetic: none -> 4.07 us  [the longest x1 2 us: shards(): last = send(jnp.where(low, i1_lo, i2_hi), across)]
    all_to_all x1, waiting for transfers between devices: 6.01 us -> 8.31 us  [shards(): table = lax.all_to_all(after(message, i2_lo, i2_hi), 'dp', 0, 0, tiled=True)]
    unnamed x22 -> x20, local copies, waits for them, and re-layouts: 1.66 us -> 3.36 us
    add x1, other arithmetic: 1.19 us -> 2.61 us  [shards(): own_image + send(sib_image, cores)]
    ppermute x18 -> x15, waiting for transfers between devices: 30.9 us -> 30.5 us  [send(): return lax.ppermute(block, 'dp', route)]
  transfers between devices with their start and end apart: 19 -> 16, of which waited for: 9 -> 7; matrix products, arithmetic and copies ran while one was open for 1% -> 6% of each run, Pallas kernels for 21% -> 23%
where the time goes in v4:
time: 107 us; the launch traced here: 106 us
  waiting for transfers between devices  38.8 us (36%)
  starting transfers between devices  31.5 us (29%)
  Pallas kernels  24 us (22%)
  other arithmetic  7.87 us (7%)
  local copies, waits for them, and re-layouts  3.36 us (3%)
    ppermute x15, waiting for transfers between devices, send(): return lax.ppermute(block, 'dp', route)  30.5 us
    ppermute x15, starting transfers between devices, send(): return lax.ppermute(block, 'dp', route)  27.8 us
    pallas_call x4, Pallas kernels, kernel_call(): pl.pallas_call(body, out_shape=[out for _, out in outs], in_specs=[pl.Blo...  24 us
    all_to_all x1, waiting for transfers between devices, shards(): table = lax.all_to_all(after(message, i2_lo, i2_hi), 'dp', 0, 0, tiled=True)  8.31 us
    all_to_all x1, starting transfers between devices, shards(): table = lax.all_to_all(after(message, i2_lo, i2_hi), 'dp', 0, 0, tiled=True)  3.72 us
    unnamed x20, local copies, waits for them, and re-layouts  3.36 us
    add x1, other arithmetic, shards(): own_image + send(sib_image, cores)  2.61 us
  transfers between devices with their start and end apart: 16, of which 7 were waited for; matrix products, arithmetic and copies ran while one was open for 6% of the time, Pallas kernels for 23%

profile of v4, /device:TPU:0, one launch (start us, length us, event | category | flops | bytes accessed | tf_op | source)
XLA Modules:
  0.0 106.3 jit_solution(15641011050809869968)
XLA Ops:
  0.6 5.1 %collective-permute-start.1 = (bf16[256,1280]{1,0:T(8,128)(2,1)}, bf16[256,1280]{1,0:T(8,128)(2,1)}, u32[]{:S(2)}, u32[]{:S(2)}) collective-permute-start(bf16[256,1280]{1,0:T(8,128)(2,1)} %text.5), channel_id=1, source_target_pairs={{4,0},{5,1},{6,2},{7,3},{8,4},{9,5},{10,6},{11,7},{12,8},{13,9},{1... | collective-permute-start | bytes 1966088 | tf_op jit(solution)/shard_map/ppermute | solution.py:25
  5.7 1.2 %broadcast_select_fusion.2 = bf16[256,1280]{1,0:T(8,128)(2,1)S(1)} fusion(bf16[256,1280]{1,0:T(8,128)(2,1)} %refs_0_.3, bf16[256,1280]{1,0:T(8,128)(2,1)} %text.5, pred[]{:T(512)S(6)} %lt.10), kind=kLoop, calls=%fused_computation.2 | loop fusion | flops 327680 | bytes 1966081 | tf_op jit(solution)/shard_map/jit(_where)/select_n | solution.py:353
  6.9 1.6 %collective-permute-start.2 = (bf16[256,1280]{1,0:T(8,128)(2,1)S(1)}, bf16[256,1280]{1,0:T(8,128)(2,1)S(1)}, u32[]{:S(2)}, u32[]{:S(2)}) collective-permute-start(bf16[256,1280]{1,0:T(8,128)(2,1)S(1)} %broadcast_select_fusion.2), channel_id=1, source_target_pairs={{0,2},{1,3},{2,0},{3,1},{4,6},{5,7},{6,4},{7,5},{8,10},{9,11},{10,... | collective-permute-start | bytes 1966088 | tf_op jit(solution)/shard_map/ppermute | solution.py:25
  8.5 11.5 %collective-permute-done.1.t1.refs_1_ = bf16[256,1280]{1,0:T(8,128)(2,1)} collective-permute-done((bf16[256,1280]{1,0:T(8,128)(2,1)}, bf16[256,1280]{1,0:T(8,128)(2,1)}, u32[]{:S(2)}, u32[]{:S(2)}) %collective-permute-start.1) | collective-permute-done | bytes 655392 | tf_op jit(solution)/shard_map/ppermute | solution.py:25
  20.1 6.2 %collective-permute-start.4 = (bf16[256,1280]{1,0:T(8,128)(2,1)}, bf16[256,1280]{1,0:T(8,128)(2,1)S(1)}, u32[]{:S(2)}, u32[]{:S(2)}) collective-permute-start(bf16[256,1280]{1,0:T(8,128)(2,1)} %collective-permute-done.1.t1.refs_1_), channel_id=1, source_target_pairs={{4,0},{5,1},{8,4},{9,5},{12,8},{13,9},{0,12},{1,13},{20,16},{21,17... | collective-permute-start | bytes 1966088 | tf_op jit(solution)/shard_map/ppermute | solution.py:25
  26.3 1.5 %collective-permute-start.6 = (bf16[256,1280]{1,0:T(8,128)(2,1)S(1)}, bf16[256,1280]{1,0:T(8,128)(2,1)}, u32[]{:S(2)}, u32[]{:S(2)}) collective-permute-start(bf16[256,1280]{1,0:T(8,128)(2,1)S(1)} %copy-done), channel_id=1, source_target_pairs={{14,2},{15,3},{2,6},{3,7},{6,10},{7,11},{10,14},{11,15},{30,18},{3... | collective-permute-start | bytes 1966088 | tf_op jit(solution)/shard_map/ppermute | solution.py:25
  27.9 11.8 %collective-permute-done.4.t2_lo.refs_3_ = bf16[256,1280]{1,0:T(8,128)(2,1)S(1)} collective-permute-done((bf16[256,1280]{1,0:T(8,128)(2,1)}, bf16[256,1280]{1,0:T(8,128)(2,1)S(1)}, u32[]{:S(2)}, u32[]{:S(2)}) %collective-permute-start.4) | collective-permute-done | bytes 655392 | tf_op jit(solution)/shard_map/ppermute | solution.py:25
  39.6 1.9 %collective-permute-start.8 = (bf16[256,1280]{1,0:T(8,128)(2,1)S(1)}, bf16[256,1280]{1,0:T(8,128)(2,1)}, u32[]{:S(2)}, u32[]{:S(2)}) collective-permute-start(bf16[256,1280]{1,0:T(8,128)(2,1)S(1)} %copy-done), channel_id=1, source_target_pairs={{12,0},{13,1},{0,4},{1,5},{4,8},{5,9},{8,12},{9,13},{28,16},{29,17... | collective-permute-start | bytes 1966088 | tf_op jit(solution)/shard_map/ppermute | solution.py:25
  41.6 1.5 %collective-permute-start.5 = (bf16[256,1280]{1,0:T(8,128)(2,1)}, bf16[256,1280]{1,0:T(8,128)(2,1)}, u32[]{:S(2)}, u32[]{:S(2)}) collective-permute-start(bf16[256,1280]{1,0:T(8,128)(2,1)} %collective-permute-done.1.t1.refs_1_), channel_id=1, source_target_pairs={{6,2},{10,6},{14,10},{2,14},{22,18},{26,22},{30,26},{18,30}} | collective-permute-start | bytes 1966088 | tf_op jit(solution)/shard_map/ppermute | solution.py:25
  43.1 0.8 copy-done.6
  43.9 0.9 broadcast_select_fusion.1
  44.8 4.5 %collective-permute-start.7 = (bf16[256,1280]{1,0:T(8,128)(2,1)}, bf16[256,1280]{1,0:T(8,128)(2,1)S(1)}, u32[]{:S(2)}, u32[]{:S(2)}) collective-permute-start(bf16[256,1280]{1,0:T(8,128)(2,1)} %broadcast_select_fusion.1), channel_id=1, source_target_pairs={{0,2},{1,3},{2,0},{3,1},{4,6},{5,7},{6,4},{7,5},{8,10},{9,11},{10,... | collective-permute-start | bytes 1966088 | tf_op jit(solution)/shard_map/ppermute | solution.py:25
  49.4 1.5 %collective-permute-start.10 = (bf16[256,1280]{1,0:T(8,128)(2,1)}, bf16[256,1280]{1,0:T(8,128)(2,1)}, u32[]{:S(2)}, u32[]{:S(2)}) collective-permute-start(bf16[256,1280]{1,0:T(8,128)(2,1)} %collective-permute-done.6.refs_2_), channel_id=1, source_target_pairs={{14,2},{15,3},{2,6},{3,7},{6,10},{7,11},{10,14},{11,15},{30,18},{3... | collective-permute-start | bytes 1966088 | tf_op jit(solution)/shard_map/ppermute | solution.py:25
  50.9 4.1 %near_scores.1 = (f32[256,128]{1,0:T(8,128)}, f32[24,256]{1,0:T(8,128)}) custom-call(bf16[256,1280]{1,0:T(8,128)(2,1)} %refs_0_.3, bf16[256,1280]{1,0:T(8,128)(2,1)} %collective-permute-done.sibling, bf16[256,1280]{1,0:T(8,128)(2,1)} %text.5, bf16[256,1280]{1,0:T(8,128)(2,1)} %collective-permute-done.1.t1.refs_1_, bf16[256,1280]{1,0:T(8,128)(2,1)} %copy-done.6), custom_call_target="tpu_custom_call" | custom-call | flops 1000000 | bytes 100000 | tf_op jit(solution)/shard_map/near_scores/pallas_call | solution.py:319
  55.0 3.8 %collective-permute-done.8.refs_1_ = bf16[256,1280]{1,0:T(8,128)(2,1)} collective-permute-done((bf16[256,1280]{1,0:T(8,128)(2,1)S(1)}, bf16[256,1280]{1,0:T(8,128)(2,1)}, u32[]{:S(2)}, u32[]{:S(2)}) %collective-permute-start.8) | collective-permute-done | bytes 655392 | tf_op jit(solution)/shard_map/ppermute | solution.py:25
  58.8 1.6 %collective-permute-start.9 = (bf16[256,1280]{1,0:T(8,128)(2,1)}, bf16[256,1280]{1,0:T(8,128)(2,1)}, u32[]{:S(2)}, u32[]{:S(2)}) collective-permute-start(bf16[256,1280]{1,0:T(8,128)(2,1)} %collective-permute-done.8.refs_1_), channel_id=1, source_target_pairs={{13,1},{1,5},{5,9},{9,13},{29,17},{17,21},{21,25},{25,29}} | collective-permute-start | bytes 1966088 | tf_op jit(solution)/shard_map/ppermute | solution.py:25
  60.3 1.5 %collective-permute-done.7.t2_y.refs_6_.refs_3_ = bf16[256,1280]{1,0:T(8,128)(2,1)S(1)} collective-permute-done((bf16[256,1280]{1,0:T(8,128)(2,1)}, bf16[256,1280]{1,0:T(8,128)(2,1)S(1)}, u32[]{:S(2)}, u32[]{:S(2)}) %collective-permute-start.7) | collective-permute-done | bytes 655392 | tf_op jit(solution)/shard_map/ppermute | solution.py:25
  61.9 0.8 copy-done.3
  62.7 5.5 %far_scores.1 = f32[16,24,256]{2,1,0:T(8,128)} custom-call(f32[256,128]{1,0:T(8,128)} %get-tuple-element.17.near_rows, f32[24,256]{1,0:T(8,128)} %get-tuple-element.18.near_stat, bf16[256,1280]{1,0:T(8,128)(2,1)} %refs_0_.3, bf16[256,1280]{1,0:T(8,128)(2,1)} %collective-permute-done.sibling, bf16[256,1280]{1,0:T(8,128)(2,1)} %text.5, ...), custom_call_target="tpu_custom_call" | custom-call | flops 1000000 | bytes 100000 | tf_op jit(solution)/shard_map/far_scores/pallas_call | solution.py:319
  68.2 3.7 %all-to-all-start = ((f32[16,24,256]{2,1,0:T(8,128)}), f32[16,24,256]{2,1,0:T(8,128)S(1)}, u32[]{:S(2)}, u32[]{:S(2)}) async-start(f32[16,24,256]{2,1,0:T(8,128)} %far_scores.1), calls=%async_computation | async-start | bytes 786432 | tf_op jit(solution)/shard_map/all_to_all | solution.py:377
  71.9 2.0 %broadcast_select_fusion = bf16[256,1280]{1,0:T(8,128)(2,1)} fusion(bf16[256,1280]{1,0:T(8,128)(2,1)} %collective-permute-done.8.refs_1_, bf16[256,1280]{1,0:T(8,128)(2,1)} %collective-permute-done.10.refs_6_, pred[]{:T(512)S(6)} %lt.10), kind=kLoop, calls=%fused_computation | loop fusion | flops 327680 | bytes 1966081 | tf_op jit(solution)/shard_map/jit(_where)/select_n | solution.py:376
  73.9 1.9 %collective-permute-start.13 = (bf16[256,1280]{1,0:T(8,128)(2,1)}, bf16[256,1280]{1,0:T(8,128)(2,1)S(1)}, u32[]{:S(2)}, u32[]{:S(2)}) collective-permute-start(bf16[256,1280]{1,0:T(8,128)(2,1)} %broadcast_select_fusion), channel_id=1, source_target_pairs={{0,2},{1,3},{2,0},{3,1},{4,6},{5,7},{6,4},{7,5},{8,10},{9,11},{10,... | collective-permute-start | bytes 1966088 | tf_op jit(solution)/shard_map/ppermute | solution.py:25
  75.8 8.3 %all-to-all-done.table_in = f32[16,24,256]{2,1,0:T(8,128)S(1)} async-done(((f32[16,24,256]{2,1,0:T(8,128)}), f32[16,24,256]{2,1,0:T(8,128)S(1)}, u32[]{:S(2)}, u32[]{:S(2)}) %all-to-all-start) | async-done | bytes 393248 | tf_op jit(solution)/shard_map/all_to_all | solution.py:377
  84.2 0.7 copy-done.5
  84.9 7.3 %image_products.1 = (f32[256,1280]{1,0:T(8,128)}, f32[256,1280]{1,0:T(8,128)}) custom-call(s32[1,256]{1,0:T(1,128)} %bitcast.1, f32[16,24,256]{2,1,0:T(8,128)} %copy-done.5, bf16[256,1280]{1,0:T(8,128)(2,1)} %refs_0_.3, bf16[256,1280]{1,0:T(8,128)(2,1)} %collective-permute-done.sibling, bf16[256,1280]{1,0:T(8,128)(2,1)} %text.5, ...), custom_call_target="tpu_custom_call" | custom-call | flops 1000000 | bytes 100000 | tf_op jit(solution)/shard_map/image_products/pallas_call | solution.py:319
  92.2 0.2 collective-permute-start.11
  92.3 1.3 %collective-permute-done.13.refs_4_ = bf16[256,1280]{1,0:T(8,128)(2,1)S(1)} collective-permute-done((bf16[256,1280]{1,0:T(8,128)(2,1)}, bf16[256,1280]{1,0:T(8,128)(2,1)S(1)}, u32[]{:S(2)}, u32[]{:S(2)}) %collective-permute-start.13) | collective-permute-done | bytes 655392 | tf_op jit(solution)/shard_map/ppermute | solution.py:25
  93.6 0.9 copy-done.9
  94.5 7.2 %text_products.1 = (f32[256,1280]{1,0:T(8,128)}, f32[256,1280]{1,0:T(8,128)}) custom-call(s32[1,256]{1,0:T(1,128)} %bitcast.2, f32[16,24,256]{2,1,0:T(8,128)} %copy-done.5, bf16[256,1280]{1,0:T(8,128)(2,1)} %text.5, bf16[256,1280]{1,0:T(8,128)(2,1)} %collective-permute-done.12.sibling, bf16[256,1280]{1,0:T(8,128)(2,1)} %refs_0_.3, ...), custom_call_target="tpu_custom_call" | custom-call | flops 1000000 | bytes 100000 | tf_op jit(solution)/shard_map/text_products/pallas_call | solution.py:319
  102.0 2.6 %add.11 = f32[256,1280]{1,0:T(8,128)} add(f32[256,1280]{1,0:T(8,128)S(1)} %copy-done.7, f32[256,1280]{1,0:T(8,128)} %collective-permute-done.11) | non-fusion elementwise | flops 327680 | bytes 3932160 | tf_op jit(solution)/shard_map/add | solution.py:397
  104.6 0.5 collective-permute-done.14
  105.1 1.2 %add.12 = f32[256,1280]{1,0:T(8,128)} add(f32[256,1280]{1,0:T(8,128)S(1)} %copy-done.8, f32[256,1280]{1,0:T(8,128)S(1)} %collective-permute-done.14) | non-fusion elementwise | flops 327680 | bytes 3932160 | tf_op jit(solution)/shard_map/add | solution.py:397
  (29 shorter events, 0.3 us)
Async XLA Ops:
  0.6 25.7 %copy-start = (bf16[256,1280]{1,0:T(8,128)(2,1)S(1)}, bf16[256,1280]{1,0:T(8,128)(2,1)}, u32[]{:S(2)}) copy-start(bf16[256,1280]{1,0:T(8,128)(2,1)} %refs_0_.3) | copy-start | bytes 1966084
  0.6 19.4 %collective-permute-start.1 = (bf16[256,1280]{1,0:T(8,128)(2,1)}, bf16[256,1280]{1,0:T(8,128)(2,1)}, u32[]{:S(2)}, u32[]{:S(2)}) collective-permute-start(bf16[256,1280]{1,0:T(8,128)(2,1)} %text.5), channel_id=1, source_target_pairs={{4,0},{5,1},{6,2},{7,3},{8,4},{9,5},{10,6},{11,7},{12,8},{13,9},{1... | collective-permute-start | bytes 1966088 | tf_op jit(solution)/shard_map/ppermute | solution.py:25
  6.9 19.3 %collective-permute-start.2 = (bf16[256,1280]{1,0:T(8,128)(2,1)S(1)}, bf16[256,1280]{1,0:T(8,128)(2,1)S(1)}, u32[]{:S(2)}, u32[]{:S(2)}) collective-permute-start(bf16[256,1280]{1,0:T(8,128)(2,1)S(1)} %broadcast_select_fusion.2), channel_id=1, source_target_pairs={{0,2},{1,3},{2,0},{3,1},{4,6},{5,7},{6,4},{7,5},{8,10},{9,11},{10,... | collective-permute-start | bytes 1966088 | tf_op jit(solution)/shard_map/ppermute | solution.py:25
  20.1 19.6 %collective-permute-start.4 = (bf16[256,1280]{1,0:T(8,128)(2,1)}, bf16[256,1280]{1,0:T(8,128)(2,1)S(1)}, u32[]{:S(2)}, u32[]{:S(2)}) collective-permute-start(bf16[256,1280]{1,0:T(8,128)(2,1)} %collective-permute-done.1.t1.refs_1_), channel_id=1, source_target_pairs={{4,0},{5,1},{8,4},{9,5},{12,8},{13,9},{0,12},{1,13},{20,16},{21,17... | collective-permute-start | bytes 1966088 | tf_op jit(solution)/shard_map/ppermute | solution.py:25
  26.2 28.7 %copy-start.2 = (bf16[256,1280]{1,0:T(8,128)(2,1)}, bf16[256,1280]{1,0:T(8,128)(2,1)S(1)}, u32[]{:S(2)}) copy-start(bf16[256,1280]{1,0:T(8,128)(2,1)S(1)} %collective-permute-done.2.own_y.refs_5_.refs_7_) | copy-start | bytes 1966084
  26.3 16.8 %collective-permute-start.3 = (bf16[256,1280]{1,0:T(8,128)(2,1)}, bf16[256,1280]{1,0:T(8,128)(2,1)S(1)}, u32[]{:S(2)}, u32[]{:S(2)}) collective-permute-start(bf16[256,1280]{1,0:T(8,128)(2,1)} %collective-permute-done.1.t1.refs_1_), channel_id=1, source_target_pairs={{0,2},{1,3},{2,0},{3,1},{4,6},{5,7},{6,4},{7,5},{8,10},{9,11},{10,... | collective-permute-start | bytes 1966088 | tf_op jit(solution)/shard_map/ppermute | solution.py:25
  26.3 16.7 %collective-permute-start.6 = (bf16[256,1280]{1,0:T(8,128)(2,1)S(1)}, bf16[256,1280]{1,0:T(8,128)(2,1)}, u32[]{:S(2)}, u32[]{:S(2)}) collective-permute-start(bf16[256,1280]{1,0:T(8,128)(2,1)S(1)} %copy-done), channel_id=1, source_target_pairs={{14,2},{15,3},{2,6},{3,7},{6,10},{7,11},{10,14},{11,15},{30,18},{3... | collective-permute-start | bytes 1966088 | tf_op jit(solution)/shard_map/ppermute | solution.py:25
  27.9 23.0 %collective-permute-start = (bf16[256,1280]{1,0:T(8,128)(2,1)S(1)}, bf16[256,1280]{1,0:T(8,128)(2,1)}, u32[]{:S(2)}, u32[]{:S(2)}) collective-permute-start(bf16[256,1280]{1,0:T(8,128)(2,1)S(1)} %copy-done), channel_id=1, source_target_pairs={{0,1},{1,0},{2,3},{3,2},{4,5},{5,4},{6,7},{7,6},{8,9},{9,8},{10,11... | collective-permute-start | bytes 1966088 | tf_op jit(solution)/shard_map/ppermute | solution.py:25
  39.6 15.3 %copy-start.4 = (bf16[256,1280]{1,0:T(8,128)(2,1)}, bf16[256,1280]{1,0:T(8,128)(2,1)S(1)}, u32[]{:S(2)}) copy-start(bf16[256,1280]{1,0:T(8,128)(2,1)S(1)} %collective-permute-done.4.t2_lo.refs_3_) | copy-start | bytes 1966084
  39.6 19.1 %collective-permute-start.8 = (bf16[256,1280]{1,0:T(8,128)(2,1)S(1)}, bf16[256,1280]{1,0:T(8,128)(2,1)}, u32[]{:S(2)}, u32[]{:S(2)}) collective-permute-start(bf16[256,1280]{1,0:T(8,128)(2,1)S(1)} %copy-done), channel_id=1, source_target_pairs={{12,0},{13,1},{0,4},{1,5},{4,8},{5,9},{8,12},{9,13},{28,16},{29,17... | collective-permute-start | bytes 1966088 | tf_op jit(solution)/shard_map/ppermute | solution.py:25
  41.6 18.7 %collective-permute-start.5 = (bf16[256,1280]{1,0:T(8,128)(2,1)}, bf16[256,1280]{1,0:T(8,128)(2,1)}, u32[]{:S(2)}, u32[]{:S(2)}) collective-permute-start(bf16[256,1280]{1,0:T(8,128)(2,1)} %collective-permute-done.1.t1.refs_1_), channel_id=1, source_target_pairs={{6,2},{10,6},{14,10},{2,14},{22,18},{26,22},{30,26},{18,30}} | collective-permute-start | bytes 1966088 | tf_op jit(solution)/shard_map/ppermute | solution.py:25
  43.1 0.8 copy-start.6
  44.8 15.5 %copy-start.1 = (bf16[256,1280]{1,0:T(8,128)(2,1)S(1)}, bf16[256,1280]{1,0:T(8,128)(2,1)}, u32[]{:S(2)}) copy-start(bf16[256,1280]{1,0:T(8,128)(2,1)} %text.5) | copy-start | bytes 1966084
  44.8 17.0 %collective-permute-start.7 = (bf16[256,1280]{1,0:T(8,128)(2,1)}, bf16[256,1280]{1,0:T(8,128)(2,1)S(1)}, u32[]{:S(2)}, u32[]{:S(2)}) collective-permute-start(bf16[256,1280]{1,0:T(8,128)(2,1)} %broadcast_select_fusion.1), channel_id=1, source_target_pairs={{0,2},{1,3},{2,0},{3,1},{4,6},{5,7},{6,4},{7,5},{8,10},{9,11},{10,... | collective-permute-start | bytes 1966088 | tf_op jit(solution)/shard_map/ppermute | solution.py:25
  49.4 18.8 %collective-permute-start.10 = (bf16[256,1280]{1,0:T(8,128)(2,1)}, bf16[256,1280]{1,0:T(8,128)(2,1)}, u32[]{:S(2)}, u32[]{:S(2)}) collective-permute-start(bf16[256,1280]{1,0:T(8,128)(2,1)} %collective-permute-done.6.refs_2_), channel_id=1, source_target_pairs={{14,2},{15,3},{2,6},{3,7},{6,10},{7,11},{10,14},{11,15},{30,18},{3... | collective-permute-start | bytes 1966088 | tf_op jit(solution)/shard_map/ppermute | solution.py:25
  58.8 9.4 %collective-permute-start.9 = (bf16[256,1280]{1,0:T(8,128)(2,1)}, bf16[256,1280]{1,0:T(8,128)(2,1)}, u32[]{:S(2)}, u32[]{:S(2)}) collective-permute-start(bf16[256,1280]{1,0:T(8,128)(2,1)} %collective-permute-done.8.refs_1_), channel_id=1, source_target_pairs={{13,1},{1,5},{5,9},{9,13},{29,17},{17,21},{21,25},{25,29}} | collective-permute-start | bytes 1966088 | tf_op jit(solution)/shard_map/ppermute | solution.py:25
  60.3 32.0 %collective-permute-start.12 = (bf16[256,1280]{1,0:T(8,128)(2,1)S(1)}, bf16[256,1280]{1,0:T(8,128)(2,1)}, u32[]{:S(2)}, u32[]{:S(2)}) collective-permute-start(bf16[256,1280]{1,0:T(8,128)(2,1)S(1)} %copy-done.1), channel_id=1, source_target_pairs={{0,1},{1,0},{2,3},{3,2},{4,5},{5,4},{6,7},{7,6},{8,9},{9,8},{10,11... | collective-permute-start | bytes 1966088 | tf_op jit(solution)/shard_map/ppermute | solution.py:25
  61.8 0.8 copy-start.3
  68.2 16.0 %all-to-all-start = ((f32[16,24,256]{2,1,0:T(8,128)}), f32[16,24,256]{2,1,0:T(8,128)S(1)}, u32[]{:S(2)}, u32[]{:S(2)}) async-start(f32[16,24,256]{2,1,0:T(8,128)} %far_scores.1), calls=%async_computation | async-start | bytes 786432 | tf_op jit(solution)/shard_map/all_to_all | solution.py:377
  73.9 19.7 %collective-permute-start.13 = (bf16[256,1280]{1,0:T(8,128)(2,1)}, bf16[256,1280]{1,0:T(8,128)(2,1)S(1)}, u32[]{:S(2)}, u32[]{:S(2)}) collective-permute-start(bf16[256,1280]{1,0:T(8,128)(2,1)} %broadcast_select_fusion), channel_id=1, source_target_pairs={{0,2},{1,3},{2,0},{3,1},{4,6},{5,7},{6,4},{7,5},{8,10},{9,11},{10,... | collective-permute-start | bytes 1966088 | tf_op jit(solution)/shard_map/ppermute | solution.py:25
  84.2 0.7 copy-start.5
  92.2 9.8 %collective-permute-start.11 = (f32[256,1280]{1,0:T(8,128)}, f32[256,1280]{1,0:T(8,128)}, u32[]{:S(2)}, u32[]{:S(2)}) collective-permute-start(f32[256,1280]{1,0:T(8,128)} %get-tuple-element.26), channel_id=1, source_target_pairs={{0,1},{1,0},{2,3},{3,2},{4,5},{5,4},{6,7},{7,6},{8,9},{9,8},{10,11... | collective-permute-start | bytes 3932168 | tf_op jit(solution)/shard_map/ppermute | solution.py:25
  92.3 9.7 %copy-start.7 = (f32[256,1280]{1,0:T(8,128)S(1)}, f32[256,1280]{1,0:T(8,128)}, u32[]{:S(2)}) copy-start(f32[256,1280]{1,0:T(8,128)} %get-tuple-element.25) | copy-start | bytes 3932164
  93.6 0.9 copy-start.9
  101.8 3.3 %copy-start.8 = (f32[256,1280]{1,0:T(8,128)S(1)}, f32[256,1280]{1,0:T(8,128)}, u32[]{:S(2)}) copy-start(f32[256,1280]{1,0:T(8,128)} %get-tuple-element.28) | copy-start | bytes 3932164
  101.8 3.3 %collective-permute-start.14 = (f32[256,1280]{1,0:T(8,128)}, f32[256,1280]{1,0:T(8,128)S(1)}, u32[]{:S(2)}, u32[]{:S(2)}) collective-permute-start(f32[256,1280]{1,0:T(8,128)} %get-tuple-element.29), channel_id=1, source_target_pairs={{0,1},{1,0},{2,3},{3,2},{4,5},{5,4},{6,7},{7,6},{8,9},{9,8},{10,11... | collective-permute-start | bytes 3932168 | tf_op jit(solution)/shard_map/ppermute | solution.py:25

commit v5 on v4

--- a/solution.py
+++ b/solution.py
@@ -12,7 +12,7 @@
 
 logit_scale = 100.0
 half_scale = 50.0
-vmem_bytes = 60 * 1024 * 1024
+vmem_bytes = 52 * 1024 * 1024
 
 
 def send(block, moves):
@@ -229,7 +229,7 @@
     return stores
 
 
-def tile_products(loads, own, sib, blocks, norms, others, positive, mixes, out_refs, outs):
+def tile_products(loads, own, sib, blocks, norms, others, positive, mixes, out_refs, outs, late):
     rows = own.shape[0]
     for slot in range(4):
         block = part(blocks, slot, rows)
@@ -240,6 +240,7 @@
     stores = wide_products(
         loads, mixes[0], blocks.at[pl.ds(0, 4 * rows)], out_refs[0], outs[0]
     )
+    arrived(*late)
     for slot in range(1, 5):
         block = part(blocks, slot, rows)
         mixes[1][:, (slot - 1) * rows:slot * rows] = mixed(
@@ -270,9 +271,9 @@
     arrived(
         loads.load(table, (None, table_in)),
         loads.load(own, (None, image)),
-        loads.load(sib, (None, sibling)),
-        *[loads.load(part(blocks, slot, rows), *case) for slot, case in enumerate(cases)],
-    )
+        *[loads.load(part(blocks, slot, rows), *cases[slot]) for slot in range(4)],
+    )
+    late = [loads.load(sib, (None, sibling)), loads.load(part(blocks, 4, rows), *cases[4])]
     sib_place = sibling_of(here)
     norms = row_norms(table, [here, sib_place])
     norms = [as_column(norms[:1]), as_column(norms[1:])]
@@ -281,7 +282,7 @@
     lane = lax.broadcasted_iota(jnp.int32, (rows, rows), 1)
     match = as_column(label_ref[...].astype(jnp.float32)).astype(jnp.int32)
     positive = match == here * rows + lane
-    tile_products(loads, own, sib, blocks, norms, others, positive, mixes, out_refs, outs)
+    tile_products(loads, own, sib, blocks, norms, others, positive, mixes, out_refs, outs, late)
 
 
 def text_products(label_ref, table_in, text, sibling, *refs):
@@ -302,16 +303,16 @@
     arrived(
         loads.load(table, (None, table_in)),
         loads.load(own, (None, text)),
-        loads.load(sib, (None, sibling)),
-        *[loads.load(part(blocks, slot, rows), *case) for slot, case in enumerate(cases)],
-    )
+        *[loads.load(part(blocks, slot, rows), *cases[slot]) for slot in range(4)],
+    )
+    late = [loads.load(sib, (None, sibling)), loads.load(part(blocks, 4, rows), *cases[4])]
     norms = [as_column(column_norm(table, index)) for index in (here, sibling_of(here))]
     offsets = (0, 4, 2 + 4 * q, 6 - 4 * q, 8 * c)
     others = row_norms(table, [here - offset for offset in offsets])
     others = [others[slot:slot + 1] for slot in range(5)]
     sublane = lax.broadcasted_iota(jnp.int32, (rows, rows), 0)
     positive = label_ref[...] == here * rows + sublane
-    tile_products(loads, own, sib, blocks, norms, others, positive, mixes, out_refs, outs)
+    tile_products(loads, own, sib, blocks, norms, others, positive, mixes, out_refs, outs, late)
 
 
 def kernel_call(body, outs, scratch, copies, whole, blocks):

time: 107 us -> 104 us (0.972)
  waiting for transfers between devices: 38.8 us -> 42.1 us
  Pallas kernels: 24 us -> 21.7 us
  other arithmetic: 7.87 us -> 5.66 us
  local copies, waits for them, and re-layouts: 3.36 us -> 1.95 us
    ppermute x15, waiting for transfers between devices: 30.5 us -> 34 us  [send(): return lax.ppermute(block, 'dp', route)]
    pallas_call x4, Pallas kernels: 24 us -> 21.7 us  [kernel_call(): pl.pallas_call(body, out_shape=[out for _, out in outs], in_specs=[pl.Blo...]
    add x1, other arithmetic: 2.61 us -> 1.2 us  [shards(): own_image + send(sib_image, cores)]
    unnamed x20 -> x30, local copies, waits for them, and re-layouts: 3.36 us -> 1.95 us
  transfers between devices with their start and end apart: 16 -> 16, of which waited for: 7 -> 6; matrix products, arithmetic and copies ran while one was open for 6% -> 4% of each run, Pallas kernels for 23% -> 21%
where the time goes in v5:
time: 104 us; the launch traced here: 103 us
  waiting for transfers between devices  42.1 us (40%)
  starting transfers between devices  30.8 us (30%)
  Pallas kernels  21.7 us (21%)
  other arithmetic  5.66 us (5%)
  local copies, waits for them, and re-layouts  1.95 us (2%)
    ppermute x15, waiting for transfers between devices, send(): return lax.ppermute(block, 'dp', route)  34 us
    ppermute x15, starting transfers between devices, send(): return lax.ppermute(block, 'dp', route)  26.7 us
    pallas_call x4, Pallas kernels, kernel_call(): pl.pallas_call(body, out_shape=[out for _, out in outs], in_specs=[pl.Blo...  21.7 us
    all_to_all x1, waiting for transfers between devices, shards(): table = lax.all_to_all(after(message, i2_lo, i2_hi), 'dp', 0, 0, tiled=True)  8.12 us
    all_to_all x1, starting transfers between devices, shards(): table = lax.all_to_all(after(message, i2_lo, i2_hi), 'dp', 0, 0, tiled=True)  4.08 us
  transfers between devices with their start and end apart: 16, of which 6 were waited for; matrix products, arithmetic and copies ran while one was open for 4% of the time, Pallas kernels for 21%

profile of v5, /device:TPU:0, one launch (start us, length us, event | category | flops | bytes accessed | tf_op | source)
XLA Modules:
  0.0 103.2 jit_solution(13546814293486483013)
XLA Ops:
  0.6 5.1 %collective-permute-start.1 = (bf16[256,1280]{1,0:T(8,128)(2,1)}, bf16[256,1280]{1,0:T(8,128)(2,1)S(1)}, u32[]{:S(2)}, u32[]{:S(2)}) collective-permute-start(bf16[256,1280]{1,0:T(8,128)(2,1)} %text.5), channel_id=1, source_target_pairs={{4,0},{5,1},{6,2},{7,3},{8,4},{9,5},{10,6},{11,7},{12,8},{13,9},{1... | collective-permute-start | bytes 1966088 | tf_op jit(solution)/shard_map/ppermute | solution.py:25
  5.7 1.2 %broadcast_select_fusion.2 = bf16[256,1280]{1,0:T(8,128)(2,1)S(1)} fusion(bf16[256,1280]{1,0:T(8,128)(2,1)} %refs_0_.3, bf16[256,1280]{1,0:T(8,128)(2,1)} %text.5, pred[]{:T(512)S(6)} %lt.10), kind=kLoop, calls=%fused_computation.2 | loop fusion | flops 327680 | bytes 1966081 | tf_op jit(solution)/shard_map/jit(_where)/select_n | solution.py:354
  6.9 1.6 %collective-permute-start.2 = (bf16[256,1280]{1,0:T(8,128)(2,1)S(1)}, bf16[256,1280]{1,0:T(8,128)(2,1)S(1)}, u32[]{:S(2)}, u32[]{:S(2)}) collective-permute-start(bf16[256,1280]{1,0:T(8,128)(2,1)S(1)} %broadcast_select_fusion.2), channel_id=1, source_target_pairs={{0,2},{1,3},{2,0},{3,1},{4,6},{5,7},{6,4},{7,5},{8,10},{9,11},{10,... | collective-permute-start | bytes 1966088 | tf_op jit(solution)/shard_map/ppermute | solution.py:25
  8.5 11.5 %collective-permute-done.1.t1.refs_1_ = bf16[256,1280]{1,0:T(8,128)(2,1)S(1)} collective-permute-done((bf16[256,1280]{1,0:T(8,128)(2,1)}, bf16[256,1280]{1,0:T(8,128)(2,1)S(1)}, u32[]{:S(2)}, u32[]{:S(2)}) %collective-permute-start.1) | collective-permute-done | bytes 655392 | tf_op jit(solution)/shard_map/ppermute | solution.py:25
  20.1 6.1 %collective-permute-start.4 = (bf16[256,1280]{1,0:T(8,128)(2,1)S(1)}, bf16[256,1280]{1,0:T(8,128)(2,1)S(1)}, u32[]{:S(2)}, u32[]{:S(2)}) collective-permute-start(bf16[256,1280]{1,0:T(8,128)(2,1)S(1)} %collective-permute-done.1.t1.refs_1_), channel_id=1, source_target_pairs={{4,0},{5,1},{8,4},{9,5},{12,8},{13,9},{0,12},{1,13},{20,16},{21,17... | collective-permute-start | bytes 1966088 | tf_op jit(solution)/shard_map/ppermute | solution.py:25
  26.2 0.1 collective-permute-start.3
  26.2 0.7 collective-permute-start.6
  27.0 0.1 collective-permute-start
  27.0 12.2 %collective-permute-done.4.t2_lo.refs_3_ = bf16[256,1280]{1,0:T(8,128)(2,1)S(1)} collective-permute-done((bf16[256,1280]{1,0:T(8,128)(2,1)S(1)}, bf16[256,1280]{1,0:T(8,128)(2,1)S(1)}, u32[]{:S(2)}, u32[]{:S(2)}) %collective-permute-start.4) | collective-permute-done | bytes 655392 | tf_op jit(solution)/shard_map/ppermute | solution.py:25
  39.2 1.9 %collective-permute-start.8 = (bf16[256,1280]{1,0:T(8,128)(2,1)S(1)}, bf16[256,1280]{1,0:T(8,128)(2,1)S(1)}, u32[]{:S(2)}, u32[]{:S(2)}) collective-permute-start(bf16[256,1280]{1,0:T(8,128)(2,1)S(1)} %copy-done), channel_id=1, source_target_pairs={{12,0},{13,1},{0,4},{1,5},{4,8},{5,9},{8,12},{9,13},{28,16},{29,17... | collective-permute-start | bytes 1966088 | tf_op jit(solution)/shard_map/ppermute | solution.py:25
  41.1 0.7 collective-permute-start.5
  42.0 5.3 %collective-permute-start.7 = (bf16[256,1280]{1,0:T(8,128)(2,1)S(1)}, bf16[256,1280]{1,0:T(8,128)(2,1)S(1)}, u32[]{:S(2)}, u32[]{:S(2)}) collective-permute-start(bf16[256,1280]{1,0:T(8,128)(2,1)S(1)} %broadcast_select_fusion.1), channel_id=1, source_target_pairs={{0,2},{1,3},{2,0},{3,1},{4,6},{5,7},{6,4},{7,5},{8,10},{9,11},{10,... | collective-permute-start | bytes 1966088 | tf_op jit(solution)/shard_map/ppermute | solution.py:25
  47.3 0.7 collective-permute-start.10
  48.1 3.4 %near_scores.1 = (f32[256,128]{1,0:T(8,128)S(1)}, f32[24,256]{1,0:T(8,128)S(1)}) custom-call(bf16[256,1280]{1,0:T(8,128)(2,1)S(1)} %copy-done, bf16[256,1280]{1,0:T(8,128)(2,1)S(1)} %collective-permute-done.sibling, bf16[256,1280]{1,0:T(8,128)(2,1)} %text.5, bf16[256,1280]{1,0:T(8,128)(2,1)} %copy-done.11, bf16[256,1280]{1,0:T(8,128)(2,1)} %copy-done.12), custom_call_target="tpu_custom_call" | custom-call | flops 1000000 | bytes 100000 | tf_op jit(solution)/shard_map/near_scores/pallas_call | solution.py:320
  51.5 6.8 %collective-permute-done.8.refs_1_ = bf16[256,1280]{1,0:T(8,128)(2,1)S(1)} collective-permute-done((bf16[256,1280]{1,0:T(8,128)(2,1)S(1)}, bf16[256,1280]{1,0:T(8,128)(2,1)S(1)}, u32[]{:S(2)}, u32[]{:S(2)}) %collective-permute-start.8) | collective-permute-done | bytes 655392 | tf_op jit(solution)/shard_map/ppermute | solution.py:25
  58.3 1.5 %collective-permute-start.9 = (bf16[256,1280]{1,0:T(8,128)(2,1)S(1)}, bf16[256,1280]{1,0:T(8,128)(2,1)}, u32[]{:S(2)}, u32[]{:S(2)}) collective-permute-start(bf16[256,1280]{1,0:T(8,128)(2,1)S(1)} %collective-permute-done.8.refs_1_), channel_id=1, source_target_pairs={{13,1},{1,5},{5,9},{9,13},{29,17},{17,21},{21,25},{25,29}} | collective-permute-start | bytes 1966088 | tf_op jit(solution)/shard_map/ppermute | solution.py:25
  59.9 0.8 copy-done.10
  60.7 0.2 copy-done.5
  61.0 4.4 %far_scores.1 = f32[16,24,256]{2,1,0:T(8,128)} custom-call(f32[256,128]{1,0:T(8,128)S(1)} %get-tuple-element.17.near_rows, f32[24,256]{1,0:T(8,128)S(1)} %get-tuple-element.18.near_stat, bf16[256,1280]{1,0:T(8,128)(2,1)S(1)} %copy-done, bf16[256,1280]{1,0:T(8,128)(2,1)S(1)} %collective-permute-done.sibling, bf16[256,1280]{1,0:T(8,128)(2,1)} %text.5, ...), custom_call_target="tpu_custom_call" | custom-call | flops 1000000 | bytes 100000 | tf_op jit(solution)/shard_map/far_scores/pallas_call | solution.py:320
  65.4 0.8 copy-done.9
  66.3 4.1 %all-to-all-start = ((f32[16,24,256]{2,1,0:T(8,128)}), f32[16,24,256]{2,1,0:T(8,128)S(1)}, u32[]{:S(2)}, u32[]{:S(2)}) async-start(f32[16,24,256]{2,1,0:T(8,128)} %far_scores.1), calls=%async_computation | async-start | bytes 786432 | tf_op jit(solution)/shard_map/all_to_all | solution.py:378
  70.4 2.0 %broadcast_select_fusion = bf16[256,1280]{1,0:T(8,128)(2,1)} fusion(bf16[256,1280]{1,0:T(8,128)(2,1)} %copy-done.8, bf16[256,1280]{1,0:T(8,128)(2,1)} %copy-done.9, pred[]{:T(512)S(6)} %lt.10), kind=kLoop, calls=%fused_computation | loop fusion | flops 327680 | bytes 1966081 | tf_op jit(solution)/shard_map/jit(_where)/select_n | solution.py:377
  72.4 2.1 %collective-permute-start.13 = (bf16[256,1280]{1,0:T(8,128)(2,1)}, bf16[256,1280]{1,0:T(8,128)(2,1)}, u32[]{:S(2)}, u32[]{:S(2)}) collective-permute-start(bf16[256,1280]{1,0:T(8,128)(2,1)} %broadcast_select_fusion), channel_id=1, source_target_pairs={{0,2},{1,3},{2,0},{3,1},{4,6},{5,7},{6,4},{7,5},{8,10},{9,11},{10,... | collective-permute-start | bytes 1966088 | tf_op jit(solution)/shard_map/ppermute | solution.py:25
  74.5 8.1 %all-to-all-done.table_in = f32[16,24,256]{2,1,0:T(8,128)S(1)} async-done(((f32[16,24,256]{2,1,0:T(8,128)}), f32[16,24,256]{2,1,0:T(8,128)S(1)}, u32[]{:S(2)}, u32[]{:S(2)}) %all-to-all-start) | async-done | bytes 393248 | tf_op jit(solution)/shard_map/all_to_all | solution.py:378
  82.6 6.9 %image_products.1 = (f32[256,1280]{1,0:T(8,128)}, f32[256,1280]{1,0:T(8,128)}) custom-call(s32[1,256]{1,0:T(1,128)S(1)} %bitcast.1, f32[16,24,256]{2,1,0:T(8,128)S(1)} %all-to-all-done.table_in, bf16[256,1280]{1,0:T(8,128)(2,1)S(1)} %copy-done, bf16[256,1280]{1,0:T(8,128)(2,1)S(1)} %collective-permute-done.sibling, bf16[256,1280]{1,0:T(8,128)(2,1)} %text.5, ...), custom_call_target="tpu_custom_call" | custom-call | flops 1000000 | bytes 100000 | tf_op jit(solution)/shard_map/image_products/pallas_call | solution.py:320
  89.5 0.2 collective-permute-start.11
  89.7 1.8 %collective-permute-done.13.refs_4_ = bf16[256,1280]{1,0:T(8,128)(2,1)} collective-permute-done((bf16[256,1280]{1,0:T(8,128)(2,1)}, bf16[256,1280]{1,0:T(8,128)(2,1)}, u32[]{:S(2)}, u32[]{:S(2)}) %collective-permute-start.13) | collective-permute-done | bytes 655392 | tf_op jit(solution)/shard_map/ppermute | solution.py:25
  91.5 6.9 %text_products.1 = (f32[256,1280]{1,0:T(8,128)}, f32[256,1280]{1,0:T(8,128)}) custom-call(s32[1,256]{1,0:T(1,128)S(1)} %bitcast.2, f32[16,24,256]{2,1,0:T(8,128)S(1)} %all-to-all-done.table_in, bf16[256,1280]{1,0:T(8,128)(2,1)S(1)} %copy-done.2, bf16[256,1280]{1,0:T(8,128)(2,1)S(1)} %collective-permute-done.12.sibling, bf16[256,1280]{1,0:T(8,128)(2,1)} %refs_0_.3, ...), custom_call_target="tpu_custom_call" | custom-call | flops 1000000 | bytes 100000 | tf_op jit(solution)/shard_map/text_products/pallas_call | solution.py:320
  98.4 0.7 collective-permute-start.14
  99.1 1.2 %add.11 = f32[256,1280]{1,0:T(8,128)} add(f32[256,1280]{1,0:T(8,128)S(1)} %copy-done.13, f32[256,1280]{1,0:T(8,128)S(1)} %collective-permute-done.11) | non-fusion elementwise | flops 327680 | bytes 3932160 | tf_op jit(solution)/shard_map/add | solution.py:398
  100.3 1.7 %collective-permute-done.14 = f32[256,1280]{1,0:T(8,128)S(1)} collective-permute-done((f32[256,1280]{1,0:T(8,128)}, f32[256,1280]{1,0:T(8,128)S(1)}, u32[]{:S(2)}, u32[]{:S(2)}) %collective-permute-start.14) | collective-permute-done | bytes 1310752 | tf_op jit(solution)/shard_map/ppermute | solution.py:25
  102.0 1.2 %add.12 = f32[256,1280]{1,0:T(8,128)} add(f32[256,1280]{1,0:T(8,128)S(1)} %copy-done.14, f32[256,1280]{1,0:T(8,128)S(1)} %collective-permute-done.14) | non-fusion elementwise | flops 327680 | bytes 3932160 | tf_op jit(solution)/shard_map/add | solution.py:398
  (39 shorter events, 0.2 us)
Async XLA Ops:
  0.6 25.6 %copy-start = (bf16[256,1280]{1,0:T(8,128)(2,1)S(1)}, bf16[256,1280]{1,0:T(8,128)(2,1)}, u32[]{:S(2)}) copy-start(bf16[256,1280]{1,0:T(8,128)(2,1)} %refs_0_.3) | copy-start | bytes 1966084
  0.6 19.4 %collective-permute-start.1 = (bf16[256,1280]{1,0:T(8,128)(2,1)}, bf16[256,1280]{1,0:T(8,128)(2,1)S(1)}, u32[]{:S(2)}, u32[]{:S(2)}) collective-permute-start(bf16[256,1280]{1,0:T(8,128)(2,1)} %text.5), channel_id=1, source_target_pairs={{4,0},{5,1},{6,2},{7,3},{8,4},{9,5},{10,6},{11,7},{12,8},{13,9},{1... | collective-permute-start | bytes 1966088 | tf_op jit(solution)/shard_map/ppermute | solution.py:25
  6.9 19.2 %collective-permute-start.2 = (bf16[256,1280]{1,0:T(8,128)(2,1)S(1)}, bf16[256,1280]{1,0:T(8,128)(2,1)S(1)}, u32[]{:S(2)}, u32[]{:S(2)}) collective-permute-start(bf16[256,1280]{1,0:T(8,128)(2,1)S(1)} %broadcast_select_fusion.2), channel_id=1, source_target_pairs={{0,2},{1,3},{2,0},{3,1},{4,6},{5,7},{6,4},{7,5},{8,10},{9,11},{10,... | collective-permute-start | bytes 1966088 | tf_op jit(solution)/shard_map/ppermute | solution.py:25
  20.1 28.0 %copy-start.11 = (bf16[256,1280]{1,0:T(8,128)(2,1)}, bf16[256,1280]{1,0:T(8,128)(2,1)S(1)}, u32[]{:S(2)}) copy-start(bf16[256,1280]{1,0:T(8,128)(2,1)S(1)} %collective-permute-done.1.t1.refs_1_) | copy-start | bytes 1966084
  20.1 19.2 %collective-permute-start.4 = (bf16[256,1280]{1,0:T(8,128)(2,1)S(1)}, bf16[256,1280]{1,0:T(8,128)(2,1)S(1)}, u32[]{:S(2)}, u32[]{:S(2)}) collective-permute-start(bf16[256,1280]{1,0:T(8,128)(2,1)S(1)} %collective-permute-done.1.t1.refs_1_), channel_id=1, source_target_pairs={{4,0},{5,1},{8,4},{9,5},{12,8},{13,9},{0,12},{1,13},{20,16},{21,17... | collective-permute-start | bytes 1966088 | tf_op jit(solution)/shard_map/ppermute | solution.py:25
  26.1 25.3 %copy-start.4 = (bf16[256,1280]{1,0:T(8,128)(2,1)}, bf16[256,1280]{1,0:T(8,128)(2,1)S(1)}, u32[]{:S(2)}) copy-start(bf16[256,1280]{1,0:T(8,128)(2,1)S(1)} %collective-permute-done.2.own_y.refs_5_.refs_7_) | copy-start | bytes 1966084
  26.2 15.7 %collective-permute-start.3 = (bf16[256,1280]{1,0:T(8,128)(2,1)S(1)}, bf16[256,1280]{1,0:T(8,128)(2,1)S(1)}, u32[]{:S(2)}, u32[]{:S(2)}) collective-permute-start(bf16[256,1280]{1,0:T(8,128)(2,1)S(1)} %collective-permute-done.1.t1.refs_1_), channel_id=1, source_target_pairs={{0,2},{1,3},{2,0},{3,1},{4,6},{5,7},{6,4},{7,5},{8,10},{9,11},{10,... | collective-permute-start | bytes 1966088 | tf_op jit(solution)/shard_map/ppermute | solution.py:25
  26.2 15.6 %collective-permute-start.6 = (bf16[256,1280]{1,0:T(8,128)(2,1)S(1)}, bf16[256,1280]{1,0:T(8,128)(2,1)S(1)}, u32[]{:S(2)}, u32[]{:S(2)}) collective-permute-start(bf16[256,1280]{1,0:T(8,128)(2,1)S(1)} %copy-done), channel_id=1, source_target_pairs={{14,2},{15,3},{2,6},{3,7},{6,10},{7,11},{10,14},{11,15},{30,18},{3... | collective-permute-start | bytes 1966088 | tf_op jit(solution)/shard_map/ppermute | solution.py:25
  27.0 21.1 %collective-permute-start = (bf16[256,1280]{1,0:T(8,128)(2,1)S(1)}, bf16[256,1280]{1,0:T(8,128)(2,1)S(1)}, u32[]{:S(2)}, u32[]{:S(2)}) collective-permute-start(bf16[256,1280]{1,0:T(8,128)(2,1)S(1)} %copy-done), channel_id=1, source_target_pairs={{0,1},{1,0},{2,3},{3,2},{4,5},{5,4},{6,7},{7,6},{8,9},{9,8},{10,11... | collective-permute-start | bytes 1966088 | tf_op jit(solution)/shard_map/ppermute | solution.py:25
  39.2 12.3 %copy-start.6 = (bf16[256,1280]{1,0:T(8,128)(2,1)}, bf16[256,1280]{1,0:T(8,128)(2,1)S(1)}, u32[]{:S(2)}) copy-start(bf16[256,1280]{1,0:T(8,128)(2,1)S(1)} %collective-permute-done.4.t2_lo.refs_3_) | copy-start | bytes 1966084
  39.2 19.1 %collective-permute-start.8 = (bf16[256,1280]{1,0:T(8,128)(2,1)S(1)}, bf16[256,1280]{1,0:T(8,128)(2,1)S(1)}, u32[]{:S(2)}, u32[]{:S(2)}) collective-permute-start(bf16[256,1280]{1,0:T(8,128)(2,1)S(1)} %copy-done), channel_id=1, source_target_pairs={{12,0},{13,1},{0,4},{1,5},{4,8},{5,9},{8,12},{9,13},{28,16},{29,17... | collective-permute-start | bytes 1966088 | tf_op jit(solution)/shard_map/ppermute | solution.py:25
  41.1 18.7 %collective-permute-start.5 = (bf16[256,1280]{1,0:T(8,128)(2,1)S(1)}, bf16[256,1280]{1,0:T(8,128)(2,1)S(1)}, u32[]{:S(2)}, u32[]{:S(2)}) collective-permute-start(bf16[256,1280]{1,0:T(8,128)(2,1)S(1)} %collective-permute-done.1.t1.refs_1_), channel_id=1, source_target_pairs={{6,2},{10,6},{14,10},{2,14},{22,18},{26,22},{30,26},{18,30}} | collective-permute-start | bytes 1966088 | tf_op jit(solution)/shard_map/ppermute | solution.py:25
  41.9 6.2 %copy-start.12 = (bf16[256,1280]{1,0:T(8,128)(2,1)}, bf16[256,1280]{1,0:T(8,128)(2,1)S(1)}, u32[]{:S(2)}) copy-start(bf16[256,1280]{1,0:T(8,128)(2,1)S(1)} %collective-permute-done.3.t1_y.refs_2_) | copy-start | bytes 1966084
  41.9 9.6 %copy-start.7 = (bf16[256,1280]{1,0:T(8,128)(2,1)}, bf16[256,1280]{1,0:T(8,128)(2,1)S(1)}, u32[]{:S(2)}) copy-start(bf16[256,1280]{1,0:T(8,128)(2,1)S(1)} %collective-permute-done.6.refs_2_) | copy-start | bytes 1966084
  42.0 17.9 %copy-start.1 = (bf16[256,1280]{1,0:T(8,128)(2,1)S(1)}, bf16[256,1280]{1,0:T(8,128)(2,1)}, u32[]{:S(2)}) copy-start(bf16[256,1280]{1,0:T(8,128)(2,1)} %text.5) | copy-start | bytes 1966084
  42.0 17.9 %collective-permute-start.7 = (bf16[256,1280]{1,0:T(8,128)(2,1)S(1)}, bf16[256,1280]{1,0:T(8,128)(2,1)S(1)}, u32[]{:S(2)}, u32[]{:S(2)}) collective-permute-start(bf16[256,1280]{1,0:T(8,128)(2,1)S(1)} %broadcast_select_fusion.1), channel_id=1, source_target_pairs={{0,2},{1,3},{2,0},{3,1},{4,6},{5,7},{6,4},{7,5},{8,10},{9,11},{10,... | collective-permute-start | bytes 1966088 | tf_op jit(solution)/shard_map/ppermute | solution.py:25
  47.3 18.1 %collective-permute-start.10 = (bf16[256,1280]{1,0:T(8,128)(2,1)S(1)}, bf16[256,1280]{1,0:T(8,128)(2,1)S(1)}, u32[]{:S(2)}, u32[]{:S(2)}) collective-permute-start(bf16[256,1280]{1,0:T(8,128)(2,1)S(1)} %collective-permute-done.6.refs_2_), channel_id=1, source_target_pairs={{14,2},{15,3},{2,6},{3,7},{6,10},{7,11},{10,14},{11,15},{30,18},{3... | collective-permute-start | bytes 1966088 | tf_op jit(solution)/shard_map/ppermute | solution.py:25
  58.3 7.1 %copy-start.8 = (bf16[256,1280]{1,0:T(8,128)(2,1)}, bf16[256,1280]{1,0:T(8,128)(2,1)S(1)}, u32[]{:S(2)}) copy-start(bf16[256,1280]{1,0:T(8,128)(2,1)S(1)} %collective-permute-done.8.refs_1_) | copy-start | bytes 1966084
  58.3 7.9 %collective-permute-start.9 = (bf16[256,1280]{1,0:T(8,128)(2,1)S(1)}, bf16[256,1280]{1,0:T(8,128)(2,1)}, u32[]{:S(2)}, u32[]{:S(2)}) collective-permute-start(bf16[256,1280]{1,0:T(8,128)(2,1)S(1)} %collective-permute-done.8.refs_1_), channel_id=1, source_target_pairs={{13,1},{1,5},{5,9},{9,13},{29,17},{17,21},{21,25},{25,29}} | collective-permute-start | bytes 1966088 | tf_op jit(solution)/shard_map/ppermute | solution.py:25
  59.9 29.8 %collective-permute-start.12 = (bf16[256,1280]{1,0:T(8,128)(2,1)S(1)}, bf16[256,1280]{1,0:T(8,128)(2,1)S(1)}, u32[]{:S(2)}, u32[]{:S(2)}) collective-permute-start(bf16[256,1280]{1,0:T(8,128)(2,1)S(1)} %copy-done.1), channel_id=1, source_target_pairs={{0,1},{1,0},{2,3},{3,2},{4,5},{5,4},{6,7},{7,6},{8,9},{9,8},{10,11... | collective-permute-start | bytes 1966088 | tf_op jit(solution)/shard_map/ppermute | solution.py:25
  59.9 0.8 copy-start.10
  59.9 1.1 %copy-start.5 = (bf16[256,1280]{1,0:T(8,128)(2,1)}, bf16[256,1280]{1,0:T(8,128)(2,1)S(1)}, u32[]{:S(2)}) copy-start(bf16[256,1280]{1,0:T(8,128)(2,1)S(1)} %collective-permute-done.7.t2_y.refs_6_.refs_3_) | copy-start | bytes 1966084
  65.4 17.2 %copy-start.3 = (s32[256]{0:T(256)S(1)}, s32[256]{0:T(256)}, u32[]{:S(2)}) copy-start(s32[256]{0:T(256)} %param.5) | copy-start | bytes 3076
  65.4 0.8 copy-start.9
  66.3 16.3 %all-to-all-start = ((f32[16,24,256]{2,1,0:T(8,128)}), f32[16,24,256]{2,1,0:T(8,128)S(1)}, u32[]{:S(2)}, u32[]{:S(2)}) async-start(f32[16,24,256]{2,1,0:T(8,128)} %far_scores.1), calls=%async_computation | async-start | bytes 786432 | tf_op jit(solution)/shard_map/all_to_all | solution.py:378
  72.4 19.1 %collective-permute-start.13 = (bf16[256,1280]{1,0:T(8,128)(2,1)}, bf16[256,1280]{1,0:T(8,128)(2,1)}, u32[]{:S(2)}, u32[]{:S(2)}) collective-permute-start(bf16[256,1280]{1,0:T(8,128)(2,1)} %broadcast_select_fusion), channel_id=1, source_target_pairs={{0,2},{1,3},{2,0},{3,1},{4,6},{5,7},{6,4},{7,5},{8,10},{9,11},{10,... | collective-permute-start | bytes 1966088 | tf_op jit(solution)/shard_map/ppermute | solution.py:25
  82.6 8.9 %copy-start.2 = (bf16[256,1280]{1,0:T(8,128)(2,1)S(1)}, bf16[256,1280]{1,0:T(8,128)(2,1)}, u32[]{:S(2)}) copy-start(bf16[256,1280]{1,0:T(8,128)(2,1)} %text.5) | copy-start | bytes 1966084
  89.5 9.6 %collective-permute-start.11 = (f32[256,1280]{1,0:T(8,128)}, f32[256,1280]{1,0:T(8,128)S(1)}, u32[]{:S(2)}, u32[]{:S(2)}) collective-permute-start(f32[256,1280]{1,0:T(8,128)} %get-tuple-element.26), channel_id=1, source_target_pairs={{0,1},{1,0},{2,3},{3,2},{4,5},{5,4},{6,7},{7,6},{8,9},{9,8},{10,11... | collective-permute-start | bytes 3932168 | tf_op jit(solution)/shard_map/ppermute | solution.py:25
  89.7 9.4 %copy-start.13 = (f32[256,1280]{1,0:T(8,128)S(1)}, f32[256,1280]{1,0:T(8,128)}, u32[]{:S(2)}) copy-start(f32[256,1280]{1,0:T(8,128)} %get-tuple-element.25) | copy-start | bytes 3932164
  98.4 3.6 %copy-start.14 = (f32[256,1280]{1,0:T(8,128)S(1)}, f32[256,1280]{1,0:T(8,128)}, u32[]{:S(2)}) copy-start(f32[256,1280]{1,0:T(8,128)} %get-tuple-element.28) | copy-start | bytes 3932164
  98.4 3.6 %collective-permute-start.14 = (f32[256,1280]{1,0:T(8,128)}, f32[256,1280]{1,0:T(8,128)S(1)}, u32[]{:S(2)}, u32[]{:S(2)}) collective-permute-start(f32[256,1280]{1,0:T(8,128)} %get-tuple-element.29), channel_id=1, source_target_pairs={{0,1},{1,0},{2,3},{3,2},{4,5},{5,4},{6,7},{7,6},{8,9},{9,8},{10,11... | collective-permute-start | bytes 3932168 | tf_op jit(solution)/shard_map/ppermute | solution.py:25

commit v6 on v5

--- a/solution.py
+++ b/solution.py
@@ -316,6 +316,8 @@
 
 
 def kernel_call(body, outs, scratch, copies, whole, blocks):
+    products = body in (image_products, text_products)
+    vmem_limit = vmem_bytes if products else vmem_bytes // 2
     spaces = [pltpu.VMEM] * len(whole) + [pl.ANY] * len(blocks)
     return pl.pallas_call(
         body,
@@ -323,7 +325,7 @@
         in_specs=[pl.BlockSpec(memory_space=space) for space in spaces],
         out_specs=[pl.BlockSpec(memory_space=space) for space, _ in outs],
         scratch_shapes=[*scratch, pltpu.SemaphoreType.DMA((copies,))],
-        compiler_params=pltpu.CompilerParams(vmem_limit_bytes=vmem_bytes),
+        compiler_params=pltpu.CompilerParams(vmem_limit_bytes=vmem_limit),
         cost_estimate=pl.CostEstimate(
             flops=1000000, bytes_accessed=100000, transcendentals=1000
         ),

time: 104 us -> 104 us (level)
  starting transfers between devices: 30.8 us -> 32.1 us
  local copies, waits for them, and re-layouts: 1.95 us -> 0.9 us
    all_to_all x1, starting transfers between devices: 4.08 us -> 5.77 us  [shards(): table = lax.all_to_all(after(message, i2_lo, i2_hi), 'dp', 0, 0, tiled=True)]
    unnamed x30 -> x32, local copies, waits for them, and re-layouts: 1.95 us -> 0.9 us
  transfers between devices with their start and end apart: 16 -> 16, of which waited for: 6 -> 6; matrix products, arithmetic and copies ran while one was open for 4% -> 4% of each run, Pallas kernels for 21% -> 20%
where the time goes in v6:
time: 104 us
  waiting for transfers between devices  42.9 us (41%)
  starting transfers between devices  32.1 us (31%)
  Pallas kernels  20.9 us (20%)
  other arithmetic  5.7 us (5%)
    ppermute x15, waiting for transfers between devices, send(): return lax.ppermute(block, 'dp', route)  34.7 us
    ppermute x15, starting transfers between devices, send(): return lax.ppermute(block, 'dp', route)  26.3 us
    pallas_call x4, Pallas kernels, kernel_call(): pl.pallas_call(body, out_shape=[out for _, out in outs], in_specs=[pl.Blo...  20.9 us
    all_to_all x1, waiting for transfers between devices, shards(): table = lax.all_to_all(after(message, i2_lo, i2_hi), 'dp', 0, 0, tiled=True)  8.25 us
    all_to_all x1, starting transfers between devices, shards(): table = lax.all_to_all(after(message, i2_lo, i2_hi), 'dp', 0, 0, tiled=True)  5.77 us
  transfers between devices with their start and end apart: 16, of which 6 were waited for; matrix products, arithmetic and copies ran while one was open for 4% of the time, Pallas kernels for 20%

profile of v6, /device:TPU:0, one launch (start us, length us, event | category | flops | bytes accessed | tf_op | source)
XLA Modules:
  0.0 103.5 jit_solution(11221100617311635855)
XLA Ops:
  0.6 5.1 %collective-permute-start.1 = (bf16[256,1280]{1,0:T(8,128)(2,1)}, bf16[256,1280]{1,0:T(8,128)(2,1)}, u32[]{:S(2)}, u32[]{:S(2)}) collective-permute-start(bf16[256,1280]{1,0:T(8,128)(2,1)} %text.5), channel_id=1, source_target_pairs={{4,0},{5,1},{6,2},{7,3},{8,4},{9,5},{10,6},{11,7},{12,8},{13,9},{1... | collective-permute-start | bytes 1966088 | tf_op jit(solution)/shard_map/ppermute | solution.py:25
  5.7 1.2 %broadcast_select_fusion.2 = bf16[256,1280]{1,0:T(8,128)(2,1)S(1)} fusion(bf16[256,1280]{1,0:T(8,128)(2,1)} %refs_0_.3, bf16[256,1280]{1,0:T(8,128)(2,1)} %text.5, pred[]{:T(512)S(6)} %lt.10), kind=kLoop, calls=%fused_computation.2 | loop fusion | flops 327680 | bytes 1966081 | tf_op jit(solution)/shard_map/jit(_where)/select_n | solution.py:356
  6.9 0.0 copy-start.1
  6.9 1.6 %collective-permute-start.2 = (bf16[256,1280]{1,0:T(8,128)(2,1)S(1)}, bf16[256,1280]{1,0:T(8,128)(2,1)S(1)}, u32[]{:S(2)}, u32[]{:S(2)}) collective-permute-start(bf16[256,1280]{1,0:T(8,128)(2,1)S(1)} %broadcast_select_fusion.2), channel_id=1, source_target_pairs={{0,2},{1,3},{2,0},{3,1},{4,6},{5,7},{6,4},{7,5},{8,10},{9,11},{10,... | collective-permute-start | bytes 1966088 | tf_op jit(solution)/shard_map/ppermute | solution.py:25
  8.5 11.5 %collective-permute-done.1.t1.refs_1_ = bf16[256,1280]{1,0:T(8,128)(2,1)} collective-permute-done((bf16[256,1280]{1,0:T(8,128)(2,1)}, bf16[256,1280]{1,0:T(8,128)(2,1)}, u32[]{:S(2)}, u32[]{:S(2)}) %collective-permute-start.1) | collective-permute-done | bytes 655392 | tf_op jit(solution)/shard_map/ppermute | solution.py:25
  20.1 6.2 %collective-permute-start.4 = (bf16[256,1280]{1,0:T(8,128)(2,1)}, bf16[256,1280]{1,0:T(8,128)(2,1)S(1)}, u32[]{:S(2)}, u32[]{:S(2)}) collective-permute-start(bf16[256,1280]{1,0:T(8,128)(2,1)} %collective-permute-done.1.t1.refs_1_), channel_id=1, source_target_pairs={{4,0},{5,1},{8,4},{9,5},{12,8},{13,9},{0,12},{1,13},{20,16},{21,17... | collective-permute-start | bytes 1966088 | tf_op jit(solution)/shard_map/ppermute | solution.py:25
  26.3 0.1 collective-permute-start.3
  26.3 0.7 collective-permute-start.6
  27.1 0.1 collective-permute-start
  27.1 12.5 %collective-permute-done.4.t2_lo.refs_3_ = bf16[256,1280]{1,0:T(8,128)(2,1)S(1)} collective-permute-done((bf16[256,1280]{1,0:T(8,128)(2,1)}, bf16[256,1280]{1,0:T(8,128)(2,1)S(1)}, u32[]{:S(2)}, u32[]{:S(2)}) %collective-permute-start.4) | collective-permute-done | bytes 655392 | tf_op jit(solution)/shard_map/ppermute | solution.py:25
  39.6 1.9 %collective-permute-start.8 = (bf16[256,1280]{1,0:T(8,128)(2,1)S(1)}, bf16[256,1280]{1,0:T(8,128)(2,1)S(1)}, u32[]{:S(2)}, u32[]{:S(2)}) collective-permute-start(bf16[256,1280]{1,0:T(8,128)(2,1)S(1)} %copy-done), channel_id=1, source_target_pairs={{12,0},{13,1},{0,4},{1,5},{4,8},{5,9},{8,12},{9,13},{28,16},{29,17... | collective-permute-start | bytes 1966088 | tf_op jit(solution)/shard_map/ppermute | solution.py:25
  41.6 0.7 collective-permute-start.5
  42.3 0.1 broadcast_select_fusion.1
  42.4 5.0 %collective-permute-start.7 = (bf16[256,1280]{1,0:T(8,128)(2,1)S(1)}, bf16[256,1280]{1,0:T(8,128)(2,1)S(1)}, u32[]{:S(2)}, u32[]{:S(2)}) collective-permute-start(bf16[256,1280]{1,0:T(8,128)(2,1)S(1)} %broadcast_select_fusion.1), channel_id=1, source_target_pairs={{0,2},{1,3},{2,0},{3,1},{4,6},{5,7},{6,4},{7,5},{8,10},{9,11},{10,... | collective-permute-start | bytes 1966088 | tf_op jit(solution)/shard_map/ppermute | solution.py:25
  47.4 0.7 collective-permute-start.10
  48.1 3.3 %near_scores.1 = (f32[256,128]{1,0:T(8,128)S(1)}, f32[24,256]{1,0:T(8,128)S(1)}) custom-call(bf16[256,1280]{1,0:T(8,128)(2,1)S(1)} %copy-done, bf16[256,1280]{1,0:T(8,128)(2,1)S(1)} %collective-permute-done.sibling, bf16[256,1280]{1,0:T(8,128)(2,1)S(1)} %copy-done.1, bf16[256,1280]{1,0:T(8,128)(2,1)} %collective-permute-done.1.t1.refs_1_, ...), custom_call_target="tpu_custom_call" | custom-call | flops 1000000 | bytes 100000 | tf_op jit(solution)/shard_map/near_scores/pallas_call | solution.py:322
  51.5 7.2 %collective-permute-done.8.refs_1_ = bf16[256,1280]{1,0:T(8,128)(2,1)S(1)} collective-permute-done((bf16[256,1280]{1,0:T(8,128)(2,1)S(1)}, bf16[256,1280]{1,0:T(8,128)(2,1)S(1)}, u32[]{:S(2)}, u32[]{:S(2)}) %collective-permute-start.8) | collective-permute-done | bytes 655392 | tf_op jit(solution)/shard_map/ppermute | solution.py:25
  58.7 1.5 %collective-permute-start.9 = (bf16[256,1280]{1,0:T(8,128)(2,1)S(1)}, bf16[256,1280]{1,0:T(8,128)(2,1)}, u32[]{:S(2)}, u32[]{:S(2)}) collective-permute-start(bf16[256,1280]{1,0:T(8,128)(2,1)S(1)} %collective-permute-done.8.refs_1_), channel_id=1, source_target_pairs={{13,1},{1,5},{5,9},{9,13},{29,17},{17,21},{21,25},{25,29}} | collective-permute-start | bytes 1966088 | tf_op jit(solution)/shard_map/ppermute | solution.py:25
  60.2 3.8 %far_scores.1 = f32[16,24,256]{2,1,0:T(8,128)} custom-call(f32[256,128]{1,0:T(8,128)S(1)} %get-tuple-element.17.near_rows, f32[24,256]{1,0:T(8,128)S(1)} %get-tuple-element.18.near_stat, bf16[256,1280]{1,0:T(8,128)(2,1)S(1)} %copy-done, bf16[256,1280]{1,0:T(8,128)(2,1)S(1)} %collective-permute-done.sibling, bf16[256,1280]{1,0:T(8,128)(2,1)S(1)} %copy-done.1, ...), custom_call_target="tpu_custom_call" | custom-call | flops 1000000 | bytes 100000 | tf_op jit(solution)/shard_map/far_scores/pallas_call | solution.py:322
  64.1 0.8 copy-done.13
  64.9 5.8 %all-to-all-start = ((f32[16,24,256]{2,1,0:T(8,128)}), f32[16,24,256]{2,1,0:T(8,128)S(1)}, u32[]{:S(2)}, u32[]{:S(2)}) async-start(f32[16,24,256]{2,1,0:T(8,128)} %far_scores.1), calls=%async_computation | async-start | bytes 786432 | tf_op jit(solution)/shard_map/all_to_all | solution.py:380
  70.7 2.1 %broadcast_select_fusion = bf16[256,1280]{1,0:T(8,128)(2,1)} fusion(bf16[256,1280]{1,0:T(8,128)(2,1)} %copy-done.12, bf16[256,1280]{1,0:T(8,128)(2,1)} %copy-done.13, pred[]{:T(512)S(6)} %lt.10), kind=kLoop, calls=%fused_computation | loop fusion | flops 327680 | bytes 1966081 | tf_op jit(solution)/shard_map/jit(_where)/select_n | solution.py:379
  72.7 1.9 %collective-permute-start.13 = (bf16[256,1280]{1,0:T(8,128)(2,1)}, bf16[256,1280]{1,0:T(8,128)(2,1)}, u32[]{:S(2)}, u32[]{:S(2)}) collective-permute-start(bf16[256,1280]{1,0:T(8,128)(2,1)} %broadcast_select_fusion), channel_id=1, source_target_pairs={{0,2},{1,3},{2,0},{3,1},{4,6},{5,7},{6,4},{7,5},{8,10},{9,11},{10,... | collective-permute-start | bytes 1966088 | tf_op jit(solution)/shard_map/ppermute | solution.py:25
  74.6 8.3 %all-to-all-done.table_in = f32[16,24,256]{2,1,0:T(8,128)S(1)} async-done(((f32[16,24,256]{2,1,0:T(8,128)}), f32[16,24,256]{2,1,0:T(8,128)S(1)}, u32[]{:S(2)}, u32[]{:S(2)}) %all-to-all-start) | async-done | bytes 393248 | tf_op jit(solution)/shard_map/all_to_all | solution.py:380
  82.9 6.9 %image_products.1 = (f32[256,1280]{1,0:T(8,128)}, f32[256,1280]{1,0:T(8,128)}) custom-call(s32[1,256]{1,0:T(1,128)S(1)} %bitcast.1, f32[16,24,256]{2,1,0:T(8,128)S(1)} %all-to-all-done.table_in, bf16[256,1280]{1,0:T(8,128)(2,1)S(1)} %copy-done, bf16[256,1280]{1,0:T(8,128)(2,1)S(1)} %copy-done.7, bf16[256,1280]{1,0:T(8,128)(2,1)} %text.5, ...), custom_call_target="tpu_custom_call" | custom-call | flops 1000000 | bytes 100000 | tf_op jit(solution)/shard_map/image_products/pallas_call | solution.py:322
  89.9 0.2 collective-permute-start.11
  90.0 1.8 %collective-permute-done.13.refs_4_ = bf16[256,1280]{1,0:T(8,128)(2,1)} collective-permute-done((bf16[256,1280]{1,0:T(8,128)(2,1)}, bf16[256,1280]{1,0:T(8,128)(2,1)}, u32[]{:S(2)}, u32[]{:S(2)}) %collective-permute-start.13) | collective-permute-done | bytes 655392 | tf_op jit(solution)/shard_map/ppermute | solution.py:25
  91.8 6.9 %text_products.1 = (f32[256,1280]{1,0:T(8,128)}, f32[256,1280]{1,0:T(8,128)}) custom-call(s32[1,256]{1,0:T(1,128)S(1)} %bitcast.2, f32[16,24,256]{2,1,0:T(8,128)S(1)} %all-to-all-done.table_in, bf16[256,1280]{1,0:T(8,128)(2,1)S(1)} %copy-done.2, bf16[256,1280]{1,0:T(8,128)(2,1)S(1)} %collective-permute-done.12.sibling, bf16[256,1280]{1,0:T(8,128)(2,1)} %refs_0_.3, ...), custom_call_target="tpu_custom_call" | custom-call | flops 1000000 | bytes 100000 | tf_op jit(solution)/shard_map/text_products/pallas_call | solution.py:322
  98.7 0.7 collective-permute-start.14
  99.4 1.2 %add.11 = f32[256,1280]{1,0:T(8,128)} add(f32[256,1280]{1,0:T(8,128)S(1)} %copy-done.14, f32[256,1280]{1,0:T(8,128)S(1)} %collective-permute-done.11) | non-fusion elementwise | flops 327680 | bytes 3932160 | tf_op jit(solution)/shard_map/add | solution.py:400
  100.6 1.7 %collective-permute-done.14 = f32[256,1280]{1,0:T(8,128)S(1)} collective-permute-done((f32[256,1280]{1,0:T(8,128)}, f32[256,1280]{1,0:T(8,128)S(1)}, u32[]{:S(2)}, u32[]{:S(2)}) %collective-permute-start.14) | collective-permute-done | bytes 1310752 | tf_op jit(solution)/shard_map/ppermute | solution.py:25
  102.3 1.2 %add.12 = f32[256,1280]{1,0:T(8,128)} add(f32[256,1280]{1,0:T(8,128)S(1)} %copy-done.15, f32[256,1280]{1,0:T(8,128)S(1)} %collective-permute-done.14) | non-fusion elementwise | flops 327680 | bytes 3932160 | tf_op jit(solution)/shard_map/add | solution.py:400
  (41 shorter events, 0.1 us)
Async XLA Ops:
  0.6 25.7 %copy-start = (bf16[256,1280]{1,0:T(8,128)(2,1)S(1)}, bf16[256,1280]{1,0:T(8,128)(2,1)}, u32[]{:S(2)}) copy-start(bf16[256,1280]{1,0:T(8,128)(2,1)} %refs_0_.3) | copy-start | bytes 1966084
  0.6 19.4 %collective-permute-start.1 = (bf16[256,1280]{1,0:T(8,128)(2,1)}, bf16[256,1280]{1,0:T(8,128)(2,1)}, u32[]{:S(2)}, u32[]{:S(2)}) collective-permute-start(bf16[256,1280]{1,0:T(8,128)(2,1)} %text.5), channel_id=1, source_target_pairs={{4,0},{5,1},{6,2},{7,3},{8,4},{9,5},{10,6},{11,7},{12,8},{13,9},{1... | collective-permute-start | bytes 1966088 | tf_op jit(solution)/shard_map/ppermute | solution.py:25
  6.9 41.2 %copy-start.1 = (bf16[256,1280]{1,0:T(8,128)(2,1)S(1)}, bf16[256,1280]{1,0:T(8,128)(2,1)}, u32[]{:S(2)}) copy-start(bf16[256,1280]{1,0:T(8,128)(2,1)} %text.5) | copy-start | bytes 1966084
  6.9 19.3 %collective-permute-start.2 = (bf16[256,1280]{1,0:T(8,128)(2,1)S(1)}, bf16[256,1280]{1,0:T(8,128)(2,1)S(1)}, u32[]{:S(2)}, u32[]{:S(2)}) collective-permute-start(bf16[256,1280]{1,0:T(8,128)(2,1)S(1)} %broadcast_select_fusion.2), channel_id=1, source_target_pairs={{0,2},{1,3},{2,0},{3,1},{4,6},{5,7},{6,4},{7,5},{8,10},{9,11},{10,... | collective-permute-start | bytes 1966088 | tf_op jit(solution)/shard_map/ppermute | solution.py:25
  20.1 19.6 %collective-permute-start.4 = (bf16[256,1280]{1,0:T(8,128)(2,1)}, bf16[256,1280]{1,0:T(8,128)(2,1)S(1)}, u32[]{:S(2)}, u32[]{:S(2)}) collective-permute-start(bf16[256,1280]{1,0:T(8,128)(2,1)} %collective-permute-done.1.t1.refs_1_), channel_id=1, source_target_pairs={{4,0},{5,1},{8,4},{9,5},{12,8},{13,9},{0,12},{1,13},{20,16},{21,17... | collective-permute-start | bytes 1966088 | tf_op jit(solution)/shard_map/ppermute | solution.py:25
  26.2 34.0 %copy-start.3 = (bf16[256,1280]{1,0:T(8,128)(2,1)}, bf16[256,1280]{1,0:T(8,128)(2,1)S(1)}, u32[]{:S(2)}) copy-start(bf16[256,1280]{1,0:T(8,128)(2,1)S(1)} %collective-permute-done.2.own_y.refs_5_.refs_7_) | copy-start | bytes 1966084
  26.3 16.0 %collective-permute-start.3 = (bf16[256,1280]{1,0:T(8,128)(2,1)}, bf16[256,1280]{1,0:T(8,128)(2,1)S(1)}, u32[]{:S(2)}, u32[]{:S(2)}) collective-permute-start(bf16[256,1280]{1,0:T(8,128)(2,1)} %collective-permute-done.1.t1.refs_1_), channel_id=1, source_target_pairs={{0,2},{1,3},{2,0},{3,1},{4,6},{5,7},{6,4},{7,5},{8,10},{9,11},{10,... | collective-permute-start | bytes 1966088 | tf_op jit(solution)/shard_map/ppermute | solution.py:25
  26.3 16.0 %collective-permute-start.6 = (bf16[256,1280]{1,0:T(8,128)(2,1)S(1)}, bf16[256,1280]{1,0:T(8,128)(2,1)S(1)}, u32[]{:S(2)}, u32[]{:S(2)}) collective-permute-start(bf16[256,1280]{1,0:T(8,128)(2,1)S(1)} %copy-done), channel_id=1, source_target_pairs={{14,2},{15,3},{2,6},{3,7},{6,10},{7,11},{10,14},{11,15},{30,18},{3... | collective-permute-start | bytes 1966088 | tf_op jit(solution)/shard_map/ppermute | solution.py:25
  27.1 21.1 %collective-permute-start = (bf16[256,1280]{1,0:T(8,128)(2,1)S(1)}, bf16[256,1280]{1,0:T(8,128)(2,1)S(1)}, u32[]{:S(2)}, u32[]{:S(2)}) collective-permute-start(bf16[256,1280]{1,0:T(8,128)(2,1)S(1)} %copy-done), channel_id=1, source_target_pairs={{0,1},{1,0},{2,3},{3,2},{4,5},{5,4},{6,7},{7,6},{8,9},{9,8},{10,11... | collective-permute-start | bytes 1966088 | tf_op jit(solution)/shard_map/ppermute | solution.py:25
  39.6 20.6 %copy-start.5 = (bf16[256,1280]{1,0:T(8,128)(2,1)}, bf16[256,1280]{1,0:T(8,128)(2,1)S(1)}, u32[]{:S(2)}) copy-start(bf16[256,1280]{1,0:T(8,128)(2,1)S(1)} %collective-permute-done.4.t2_lo.refs_3_) | copy-start | bytes 1966084
  39.6 19.0 %collective-permute-start.8 = (bf16[256,1280]{1,0:T(8,128)(2,1)S(1)}, bf16[256,1280]{1,0:T(8,128)(2,1)S(1)}, u32[]{:S(2)}, u32[]{:S(2)}) collective-permute-start(bf16[256,1280]{1,0:T(8,128)(2,1)S(1)} %copy-done), channel_id=1, source_target_pairs={{12,0},{13,1},{0,4},{1,5},{4,8},{5,9},{8,12},{9,13},{28,16},{29,17... | collective-permute-start | bytes 1966088 | tf_op jit(solution)/shard_map/ppermute | solution.py:25
  41.6 18.6 %collective-permute-start.5 = (bf16[256,1280]{1,0:T(8,128)(2,1)}, bf16[256,1280]{1,0:T(8,128)(2,1)S(1)}, u32[]{:S(2)}, u32[]{:S(2)}) collective-permute-start(bf16[256,1280]{1,0:T(8,128)(2,1)} %collective-permute-done.1.t1.refs_1_), channel_id=1, source_target_pairs={{6,2},{10,6},{14,10},{2,14},{22,18},{26,22},{30,26},{18,30}} | collective-permute-start | bytes 1966088 | tf_op jit(solution)/shard_map/ppermute | solution.py:25
  42.3 9.1 %copy-start.9 = (bf16[256,1280]{1,0:T(8,128)(2,1)}, bf16[256,1280]{1,0:T(8,128)(2,1)S(1)}, u32[]{:S(2)}) copy-start(bf16[256,1280]{1,0:T(8,128)(2,1)S(1)} %collective-permute-done.3.t1_y.refs_2_) | copy-start | bytes 1966084
  42.3 9.1 %copy-start.11 = (bf16[256,1280]{1,0:T(8,128)(2,1)}, bf16[256,1280]{1,0:T(8,128)(2,1)S(1)}, u32[]{:S(2)}) copy-start(bf16[256,1280]{1,0:T(8,128)(2,1)S(1)} %collective-permute-done.6.refs_2_) | copy-start | bytes 1966084
  42.4 17.8 %collective-permute-start.7 = (bf16[256,1280]{1,0:T(8,128)(2,1)S(1)}, bf16[256,1280]{1,0:T(8,128)(2,1)S(1)}, u32[]{:S(2)}, u32[]{:S(2)}) collective-permute-start(bf16[256,1280]{1,0:T(8,128)(2,1)S(1)} %broadcast_select_fusion.1), channel_id=1, source_target_pairs={{0,2},{1,3},{2,0},{3,1},{4,6},{5,7},{6,4},{7,5},{8,10},{9,11},{10,... | collective-permute-start | bytes 1966088 | tf_op jit(solution)/shard_map/ppermute | solution.py:25
  47.4 16.6 %collective-permute-start.10 = (bf16[256,1280]{1,0:T(8,128)(2,1)S(1)}, bf16[256,1280]{1,0:T(8,128)(2,1)S(1)}, u32[]{:S(2)}, u32[]{:S(2)}) collective-permute-start(bf16[256,1280]{1,0:T(8,128)(2,1)S(1)} %collective-permute-done.6.refs_2_), channel_id=1, source_target_pairs={{14,2},{15,3},{2,6},{3,7},{6,10},{7,11},{10,14},{11,15},{30,18},{3... | collective-permute-start | bytes 1966088 | tf_op jit(solution)/shard_map/ppermute | solution.py:25
  48.1 12.1 %copy-start.6 = (bf16[256,1280]{1,0:T(8,128)(2,1)}, bf16[256,1280]{1,0:T(8,128)(2,1)S(1)}, u32[]{:S(2)}) copy-start(bf16[256,1280]{1,0:T(8,128)(2,1)S(1)} %collective-permute-done.sibling) | copy-start | bytes 1966084
  58.7 5.3 %copy-start.12 = (bf16[256,1280]{1,0:T(8,128)(2,1)}, bf16[256,1280]{1,0:T(8,128)(2,1)S(1)}, u32[]{:S(2)}) copy-start(bf16[256,1280]{1,0:T(8,128)(2,1)S(1)} %collective-permute-done.8.refs_1_) | copy-start | bytes 1966084
  58.7 6.2 %collective-permute-start.9 = (bf16[256,1280]{1,0:T(8,128)(2,1)S(1)}, bf16[256,1280]{1,0:T(8,128)(2,1)}, u32[]{:S(2)}, u32[]{:S(2)}) collective-permute-start(bf16[256,1280]{1,0:T(8,128)(2,1)S(1)} %collective-permute-done.8.refs_1_), channel_id=1, source_target_pairs={{13,1},{1,5},{5,9},{9,13},{29,17},{17,21},{21,25},{25,29}} | collective-permute-start | bytes 1966088 | tf_op jit(solution)/shard_map/ppermute | solution.py:25
  60.2 29.8 %collective-permute-start.12 = (bf16[256,1280]{1,0:T(8,128)(2,1)S(1)}, bf16[256,1280]{1,0:T(8,128)(2,1)S(1)}, u32[]{:S(2)}, u32[]{:S(2)}) collective-permute-start(bf16[256,1280]{1,0:T(8,128)(2,1)S(1)} %copy-done.1), channel_id=1, source_target_pairs={{0,1},{1,0},{2,3},{3,2},{4,5},{5,4},{6,7},{7,6},{8,9},{9,8},{10,11... | collective-permute-start | bytes 1966088 | tf_op jit(solution)/shard_map/ppermute | solution.py:25
  60.2 3.8 %copy-start.8 = (bf16[256,1280]{1,0:T(8,128)(2,1)}, bf16[256,1280]{1,0:T(8,128)(2,1)S(1)}, u32[]{:S(2)}) copy-start(bf16[256,1280]{1,0:T(8,128)(2,1)S(1)} %collective-permute-done.5.t2_hi.refs_4_) | copy-start | bytes 1966084
  60.2 3.8 %copy-start.4 = (bf16[256,1280]{1,0:T(8,128)(2,1)}, bf16[256,1280]{1,0:T(8,128)(2,1)S(1)}, u32[]{:S(2)}) copy-start(bf16[256,1280]{1,0:T(8,128)(2,1)S(1)} %collective-permute-done.7.t2_y.refs_6_.refs_3_) | copy-start | bytes 1966084
  64.0 18.9 %copy-start.7 = (bf16[256,1280]{1,0:T(8,128)(2,1)S(1)}, bf16[256,1280]{1,0:T(8,128)(2,1)}, u32[]{:S(2)}) copy-start(bf16[256,1280]{1,0:T(8,128)(2,1)} %copy-done.6) | copy-start | bytes 1966084
  64.0 18.9 %copy-start.10 = (s32[256]{0:T(256)S(1)}, s32[256]{0:T(256)}, u32[]{:S(2)}) copy-start(s32[256]{0:T(256)} %param.5) | copy-start | bytes 3076
  64.0 0.8 copy-start.13
  64.9 18.0 %all-to-all-start = ((f32[16,24,256]{2,1,0:T(8,128)}), f32[16,24,256]{2,1,0:T(8,128)S(1)}, u32[]{:S(2)}, u32[]{:S(2)}) async-start(f32[16,24,256]{2,1,0:T(8,128)} %far_scores.1), calls=%async_computation | async-start | bytes 786432 | tf_op jit(solution)/shard_map/all_to_all | solution.py:380
  72.7 19.1 %collective-permute-start.13 = (bf16[256,1280]{1,0:T(8,128)(2,1)}, bf16[256,1280]{1,0:T(8,128)(2,1)}, u32[]{:S(2)}, u32[]{:S(2)}) collective-permute-start(bf16[256,1280]{1,0:T(8,128)(2,1)} %broadcast_select_fusion), channel_id=1, source_target_pairs={{0,2},{1,3},{2,0},{3,1},{4,6},{5,7},{6,4},{7,5},{8,10},{9,11},{10,... | collective-permute-start | bytes 1966088 | tf_op jit(solution)/shard_map/ppermute | solution.py:25
  82.9 8.9 %copy-start.2 = (bf16[256,1280]{1,0:T(8,128)(2,1)S(1)}, bf16[256,1280]{1,0:T(8,128)(2,1)}, u32[]{:S(2)}) copy-start(bf16[256,1280]{1,0:T(8,128)(2,1)} %text.5) | copy-start | bytes 1966084
  89.9 9.5 %collective-permute-start.11 = (f32[256,1280]{1,0:T(8,128)}, f32[256,1280]{1,0:T(8,128)S(1)}, u32[]{:S(2)}, u32[]{:S(2)}) collective-permute-start(f32[256,1280]{1,0:T(8,128)} %get-tuple-element.26), channel_id=1, source_target_pairs={{0,1},{1,0},{2,3},{3,2},{4,5},{5,4},{6,7},{7,6},{8,9},{9,8},{10,11... | collective-permute-start | bytes 3932168 | tf_op jit(solution)/shard_map/ppermute | solution.py:25
  90.0 9.4 %copy-start.14 = (f32[256,1280]{1,0:T(8,128)S(1)}, f32[256,1280]{1,0:T(8,128)}, u32[]{:S(2)}) copy-start(f32[256,1280]{1,0:T(8,128)} %get-tuple-element.25) | copy-start | bytes 3932164
  98.7 3.6 %copy-start.15 = (f32[256,1280]{1,0:T(8,128)S(1)}, f32[256,1280]{1,0:T(8,128)}, u32[]{:S(2)}) copy-start(f32[256,1280]{1,0:T(8,128)} %get-tuple-element.28) | copy-start | bytes 3932164
  98.7 3.5 %collective-permute-start.14 = (f32[256,1280]{1,0:T(8,128)}, f32[256,1280]{1,0:T(8,128)S(1)}, u32[]{:S(2)}, u32[]{:S(2)}) collective-permute-start(f32[256,1280]{1,0:T(8,128)} %get-tuple-element.29), channel_id=1, source_target_pairs={{0,1},{1,0},{2,3},{3,2},{4,5},{5,4},{6,7},{7,6},{8,9},{9,8},{10,11... | collective-permute-start | bytes 3932168 | tf_op jit(solution)/shard_map/ppermute | solution.py:25
